TPU v7x, 32 devices: a whole 2x2x4 slice. The times are simulated.
32 devices in a mesh: rep: 8 (over y, x, core), fsdp: 4 (over z).
Axes of the slice: x: 2, y: 2, z: 4, core: 2. Of those that a mesh axis runs over, the one named last changes fastest.
Arguments:
- weights: bfloat16 [8, 4096, 2048], P('rep', None, 'fsdp'), may hold values from -6 to 6
- momentum: float32 [8, 4096, 2048], P('rep', None, 'fsdp'), may hold values from -6 to 6
- states: bfloat16 [2, 8, 512, 4096], P(None, 'rep', 'fsdp')
- plan: int32 [2], replicated, may hold values from 1 to 4, as said below
Outputs:
- changes: bfloat16 [2, 8, 4096, 2048], P(None, 'rep', None, 'fsdp')
Inputs may be any that keep to these rules, and one draw needn't show every extreme that they name: `plan`: every entry is a power of two, one entry is 4 and the other entries are smaller.
All inputs are finite; a program needn't handle non-finite values.
Results may differ from a plain program's by a relative error of at most 0.008.
Values may be sent and summed in bfloat16 or wider, within the bound.
A program may use at most 128 MiB of HBM per device.

v0:
```python
from functools import partial
import math

import jax
import jax.numpy as jnp
from jax import lax
from jax.sharding import PartitionSpec as P

step_size = 0.1
moment_keep = 0.9


def as_sent(array):
    return jax.tree.map(lambda a: a.astype(jnp.bfloat16) if a.dtype == jnp.float32 else a, array)


def swapped(value, axis, distance):
    mask = 2**distance
    pairs = [(source, source ^ mask) for source in range(lax.axis_size(axis))]
    return lax.ppermute(value, axis, pairs)


def normalize(row_block):
    values = row_block.astype(jnp.float32)
    return (values * lax.rsqrt(jnp.mean(values * values, axis=-1, keepdims=True) + 1e-06)).astype(
        jnp.bfloat16
    )


def swap_both(bit_level, operands):
    return swapped((as_sent(operands[0]), as_sent(operands[1])), "rep", bit_level)


def following_rows(column_float):
    width = column_float.shape[1]
    return jnp.concatenate([column_float[1:], jnp.zeros((1, width), jnp.float32)], 0)


def local(weights, momentum, states, plan):
    weight_now = weights[0]
    moment_now = momentum[0]
    width_out = weight_now.shape[1]
    model_width = weight_now.shape[0]
    scale_in = 1.0 / math.sqrt(model_width)
    levels = lax.axis_size("rep").bit_length() - 1
    total_cols = width_out * lax.axis_size("fsdp")
    changes = []
    for step_index in range(states.shape[0]):
        own_rows = states[step_index, 0]
        distance = plan[step_index]
        bit_index = jnp.zeros((), jnp.int32)
        for bit_level in range(1, levels):
            bit_index = bit_index + (distance >= 1 << bit_level).astype(jnp.int32)
        partner_weight, partner_moment = lax.switch(
            bit_index,
            [partial(swap_both, bit_level) for bit_level in range(levels)],
            (weight_now, moment_now),
        )
        normed = normalize(own_rows)
        window = own_rows[:, :total_cols]
        columns = lax.all_to_all(window, "fsdp", split_axis=1, concat_axis=0, tiled=True)
        seq_len = columns.shape[0]
        column_float = columns.astype(jnp.float32)
        following = following_rows(column_float)
        row_piece = lax.all_gather(normed, "fsdp", axis=0, tiled=True)
        count_rows = row_piece.shape[0]
        position = lax.iota(jnp.int32, count_rows)
        predicted = (
            jnp.dot(row_piece, weight_now, preferred_element_type=jnp.float32) * scale_in
            + column_float
        )
        residual = jnp.where((position < seq_len - 1)[:, None], predicted - following, 0.0).astype(
            jnp.bfloat16
        )
        summed = jnp.zeros((model_width, width_out), jnp.float32) + lax.dot_general(
            row_piece, residual, (((0,), (0,)), ((), ())), preferred_element_type=jnp.float32
        )
        gradient = summed * scale_in
        square_sum = lax.psum(jnp.sum(gradient * gradient), "fsdp")
        update = gradient * lax.rsqrt(square_sum / (model_width * total_cols) + 1e-06)
        mean_weight = 0.5 * (weight_now.astype(jnp.float32) + partner_weight.astype(jnp.float32))
        mean_moment = 0.5 * (moment_now + partner_moment)
        moment_now = moment_keep * mean_moment + update
        new_weight = (mean_weight - step_size * moment_now).astype(jnp.bfloat16)
        changes.append(
            (new_weight.astype(jnp.float32) - weight_now.astype(jnp.float32)).astype(jnp.bfloat16)
        )
        weight_now = new_weight
    return jnp.stack(changes)[:, None]


def solution(mesh):
    placed = (P("rep", None, "fsdp"), P("rep", None, "fsdp"), P(None, "rep", "fsdp", None), P())
    return jax.shard_map(
        local, mesh=mesh, in_specs=placed, out_specs=P(None, "rep", None, "fsdp"), check_vma=False
    )
```

profile of v0, /device:TPU:0, one launch (start us, length us, event | category | flops | bytes accessed | tf_op | source)
XLA Modules:
  0.0 516.6 jit_solution(17992081209900479502)
XLA Ops:
  6.5 1.7 fusion.30
  8.2 0.7 copy.12
  9.5 1.2 fusion.16
  10.7 0.7 copy.13
  12.0 1.3 fusion.18
  13.3 0.9 slice.32
  14.2 6.3 %all-to-all-start = ((bf16[128,4,512]{0,2,1:T(8,128)(2,1)}), bf16[128,4,512]{0,2,1:T(8,128)(2,1)S(1)}, u32[]{:S(2)}, u32[]{:S(2)}) async-start(bf16[128,4,512]{0,2,1:T(8,128)(2,1)} %bitcast.4), calls=%async_computation | async-start | bytes 1048576 | tf_op jit(solution)/shard_map/all_to_all | solution.py:61
  20.5 0.8 slice.34
  21.3 30.6 %all-to-all-done = bf16[128,4,512]{0,2,1:T(8,128)(2,1)S(1)} async-done(((bf16[128,4,512]{0,2,1:T(8,128)(2,1)}), bf16[128,4,512]{0,2,1:T(8,128)(2,1)S(1)}, u32[]{:S(2)}, u32[]{:S(2)}) %all-to-all-start) | async-done | bytes 524320 | tf_op jit(solution)/shard_map/all_to_all | solution.py:61
  51.9 4.1 all-to-all-start.1
  56.0 0.6 fusion.31
  59.3 183.7 %conditional.8 = (bf16[4096,512]{1,0:T(8,128)(2,1)}, bf16[4096,512]{1,0:T(8,128)(2,1)}) conditional(s32[]{:T(128)} %bitcast.1, (bf16[4096,512]{1,0:T(8,128)(2,1)}, f32[4096,512]{1,0:T(8,128)}) %tuple.110, (bf16[4096,512]{1,0:T(8,128)(2,1)}, f32[4096,512]{1,0:T(8,128)}) %tuple.111, (bf16[4096,512]{1,0:T(8,128)(2,1)}, ...), branch_computations={%region_0.0_spmd, %region_1.0_spmd, %region_2.0_spmd} | conditional | flops 2097152 | bytes 62914684
  59.3 4.1 convert_element_type.106
  63.4 1.6 collective-permute-start.3
  65.5 91.6 %collective-permute-done.3 = bf16[4096,512]{1,0:T(8,128)(2,1)} collective-permute-done((bf16[4096,512]{1,0:T(8,128)(2,1)S(1)}, bf16[4096,512]{1,0:T(8,128)(2,1)}, u32[]{:S(2)}, u32[]{:S(2)}) %collective-permute-start.3) | collective-permute-done | bytes 4194336 | tf_op jit(solution)/shard_map/cond/branch_1_fun/ppermute | solution.py:20
  157.1 85.9 %collective-permute-done.2 = bf16[4096,512]{1,0:T(8,128)(2,1)} collective-permute-done((bf16[4096,512]{1,0:T(8,128)(2,1)S(1)}, bf16[4096,512]{1,0:T(8,128)(2,1)}, u32[]{:S(2)}, u32[]{:S(2)}) %collective-permute-start.2) | collective-permute-done | bytes 4194336 | tf_op jit(solution)/shard_map/cond/branch_1_fun/ppermute | solution.py:20
  243.4 1.2 slice.33
  244.6 1.1 convert_bitcast_fusion
  246.2 6.2 %fusion.25 = bf16[512,512]{1,0:T(8,128)(2,1)S(1)} fusion(f32[512,512]{1,0:T(8,128)S(1)} %bitcast.51, bf16[512,4096]{0,1:T(8,128)(2,1)} %all-gather.3.cloned.1.call-done, f32[511,512]{1,0:T(8,128)} %slice.33, pred[512]{0:T(512)(128)(4,1)S(1)} %iota_compare_fusion, bf16[1,4096,512]{2,1,0:T(8,128)(2,1)} %param.10), kind=kOutput, calls=%fused_computation.40 | convolution fusion | flops 2148794368 | bytes 11008512 | tf_op jit(solution)/shard_map/dot_general | solution.py:69
  252.5 6.4 %multiply_reduce_fusion.1 = (f32[]{:T(128)}, f32[4096,512]{1,0:T(8,128)}) fusion(bf16[512,4096]{0,1:T(8,128)(2,1)S(1)} %copy-done.9, bf16[512,512]{1,0:T(8,128)(2,1)S(1)} %fusion.25), kind=kOutput, calls=%fused_computation.21 | convolution fusion | flops 2153775104 | bytes 13107204 | tf_op jit(solution)/shard_map/dot_general | solution.py:75
  258.9 12.7 %psum.14 = f32[]{:T(128)} all-reduce(f32[]{:T(128)} %get-tuple-element.92), channel_id=1, replica_groups=mesh['rep'=8,'fsdp'=4] {'fsdp'}, use_global_device_ids=true, to_apply=%region_5.6 | all-reduce | flops 1 | bytes 8 | tf_op jit(solution)/shard_map/psum | solution.py:79
  272.2 17.0 %fusion.13 = (bf16[1,4096,512]{2,1,0:T(8,128)(2,1)}, bf16[4096,512]{1,0:T(8,128)(2,1)}, f32[4096,512]{1,0:T(8,128)}) fusion(bf16[1,4096,512]{2,1,0:T(8,128)(2,1)} %param.10, bf16[4096,512]{1,0:T(8,128)(2,1)} %get-tuple-element.79, f32[4096,512]{1,0:T(8,128)} %get-tuple-element.93, f32[]{:T(128)S(6)} %mul.87, bf16[4096,512]{1,0:T(8,128)(2,1)} %get-tuple-element.80, ...), kind=kLoop, calls=%fused_computation.22 | loop fusion | flops 31457280 | bytes 46137348 | tf_op jit(solution)/shard_map/stack | solution.py:89
  289.2 6.0 %fusion.26 = bf16[512,512]{1,0:T(8,128)(2,1)S(1)} fusion(f32[512,512]{1,0:T(8,128)S(1)} %bitcast.49, bf16[512,4096]{0,1:T(8,128)(2,1)} %all-gather.5.cloned.1.call-done, bf16[4096,512]{1,0:T(8,128)(2,1)} %get-tuple-element.86, f32[511,512]{1,0:T(8,128)S(1)} %slice.35, pred[512]{0:T(512)(128)(4,1)S(1)} %iota_compare_fusion), kind=kOutput, calls=%fused_computation.41 | convolution fusion | flops 2148794368 | bytes 11008512 | tf_op jit(solution)/shard_map/dot_general | solution.py:69
  295.2 6.2 %multiply_reduce_fusion = (f32[]{:T(128)}, f32[4096,512]{1,0:T(8,128)}) fusion(bf16[512,4096]{0,1:T(8,128)(2,1)S(1)} %copy-done.8, bf16[512,512]{1,0:T(8,128)(2,1)S(1)} %fusion.26), kind=kOutput, calls=%fused_computation.20 | convolution fusion | flops 2153775104 | bytes 13107204 | tf_op jit(solution)/shard_map/dot_general | solution.py:75
  301.4 9.1 %psum.15 = f32[]{:T(128)} all-reduce(f32[]{:T(128)} %get-tuple-element.94), channel_id=1, replica_groups=mesh['rep'=8,'fsdp'=4] {'fsdp'}, use_global_device_ids=true, to_apply=%region_11.12 | all-reduce | flops 1 | bytes 8 | tf_op jit(solution)/shard_map/psum | solution.py:79
  311.2 178.7 %conditional.9 = (bf16[4096,512]{1,0:T(8,128)(2,1)}, bf16[4096,512]{1,0:T(8,128)(2,1)}) conditional(s32[]{:T(128)} %bitcast.8, (bf16[4096,512]{1,0:T(8,128)(2,1)}, f32[4096,512]{1,0:T(8,128)}) %tuple.70, (bf16[4096,512]{1,0:T(8,128)(2,1)}, f32[4096,512]{1,0:T(8,128)}) %tuple.70, (bf16[4096,512]{1,0:T(8,128)(2,1)}, ...), branch_computations={%region_6.7_spmd, %region_7.8_spmd, %region_8.9_spmd} | conditional | flops 2097152 | bytes 62914684
  311.3 4.1 convert_element_type.110
  315.4 1.6 collective-permute-start.11
  317.5 91.6 %collective-permute-done.11 = bf16[4096,512]{1,0:T(8,128)(2,1)} collective-permute-done((bf16[4096,512]{1,0:T(8,128)(2,1)S(1)}, bf16[4096,512]{1,0:T(8,128)(2,1)}, u32[]{:S(2)}, u32[]{:S(2)}) %collective-permute-start.11) | collective-permute-done | bytes 4194336 | tf_op jit(solution)/shard_map/cond/branch_2_fun/ppermute | solution.py:20
  409.1 80.9 %collective-permute-done.10 = bf16[4096,512]{1,0:T(8,128)(2,1)} collective-permute-done((bf16[4096,512]{1,0:T(8,128)(2,1)S(1)}, bf16[4096,512]{1,0:T(8,128)(2,1)}, u32[]{:S(2)}, u32[]{:S(2)}) %collective-permute-start.10) | collective-permute-done | bytes 4194336 | tf_op jit(solution)/shard_map/cond/branch_2_fun/ppermute | solution.py:20
  490.0 13.5 %fusion.14 = bf16[1,4096,512]{2,1,0:T(8,128)(2,1)} fusion(f32[4096,512]{1,0:T(8,128)} %get-tuple-element.95, f32[]{:T(128)S(6)} %mul.99, f32[4096,512]{1,0:T(8,128)} %get-tuple-element.87, bf16[4096,512]{1,0:T(8,128)(2,1)} %get-tuple-element.84, bf16[4096,512]{1,0:T(8,128)(2,1)} %get-tuple-element.83, bf16[4096,512]{1,0:T(8,128)(2,1)} %get-tuple-element.86), kind=kLoop, calls=%fused_computation.23 | loop fusion | flops 31457280 | bytes 33554436 | tf_op jit(solution)/shard_map/stack | solution.py:89
  503.5 6.3 %maximum_bitcast_fusion = bf16[2,1,4096,512]{3,2,1,0:T(8,128)(2,1)} fusion(bf16[1,4096,512]{2,1,0:T(8,128)(2,1)} %fusion.14, bf16[1,4096,512]{2,1,0:T(8,128)(2,1)S(1)} %copy-done.3), kind=kLoop, calls=%fused_computation.12 | loop fusion | flops 4194304 | bytes 16777216 | tf_op jit(solution)/shard_map/broadcast_in_dim | solution.py:89
  (30 shorter events, 3.2 us)
Async XLA Ops:
  6.5 239.7 %all-gather.3.cloned.1.call-start = ((), (), s32[]{:S(2)}) async-start(), calls=%async_computation.2 | async-start | bytes 5242880 | tf_op jit(solution)/shard_map/all_gather | solution.py:65
  10.7 278.6 %all-gather.5.cloned.1.call-start = ((), (), s32[]{:S(2)}) async-start(), calls=%async_computation.3 | async-start | bytes 5242880 | tf_op jit(solution)/shard_map/all_gather | solution.py:65
  11.4 44.6 %copy-start.7 = (s32[2]{0:T(128)S(1)}, s32[2]{0:T(128)}, u32[]{:S(2)}) copy-start(s32[2]{0:T(128)} %param.13) | copy-start | bytes 28
  14.2 37.7 %all-to-all-start = ((bf16[128,4,512]{0,2,1:T(8,128)(2,1)}), bf16[128,4,512]{0,2,1:T(8,128)(2,1)S(1)}, u32[]{:S(2)}, u32[]{:S(2)}) async-start(bf16[128,4,512]{0,2,1:T(8,128)(2,1)} %bitcast.4), calls=%async_computation | async-start | bytes 1048576 | tf_op jit(solution)/shard_map/all_to_all | solution.py:61
  51.9 192.7 %all-to-all-start.1 = ((bf16[128,4,512]{0,2,1:T(8,128)(2,1)}), bf16[128,4,512]{0,2,1:T(8,128)(2,1)}, u32[]{:S(2)}, u32[]{:S(2)}) async-start(bf16[128,4,512]{0,2,1:T(8,128)(2,1)} %bitcast.10), calls=%async_computation.1 | async-start | bytes 1048576 | tf_op jit(solution)/shard_map/all_to_all | solution.py:61
  59.3 5.7 %copy-start.5 = (bf16[4096,512]{1,0:T(8,128)(2,1)S(1)}, bf16[4096,512]{1,0:T(8,128)(2,1)}, u32[]{:S(2)}) copy-start(bf16[4096,512]{1,0:T(8,128)(2,1)} %get-tuple-element.55) | copy-start | bytes 12582916
  63.4 93.7 %collective-permute-start.3 = (bf16[4096,512]{1,0:T(8,128)(2,1)S(1)}, bf16[4096,512]{1,0:T(8,128)(2,1)}, u32[]{:S(2)}, u32[]{:S(2)}) collective-permute-start(bf16[4096,512]{1,0:T(8,128)(2,1)S(1)} %convert_element_type.106), channel_id=1, source_target_pairs={{0,8},{4,12},{8,0},{12,4},{16,24},{20,28},{24,16},{28,20},{1,9},{5... | collective-permute-start | bytes 12582920 | tf_op jit(solution)/shard_map/cond/branch_1_fun/ppermute | solution.py:20
  65.0 178.0 %collective-permute-start.2 = (bf16[4096,512]{1,0:T(8,128)(2,1)S(1)}, bf16[4096,512]{1,0:T(8,128)(2,1)}, u32[]{:S(2)}, u32[]{:S(2)}) collective-permute-start(bf16[4096,512]{1,0:T(8,128)(2,1)S(1)} %copy-done.5), channel_id=1, source_target_pairs={{0,8},{4,12},{8,0},{12,4},{16,24},{20,28},{24,16},{28,20},{1,9},{5... | collective-permute-start | bytes 12582920 | tf_op jit(solution)/shard_map/cond/branch_1_fun/ppermute | solution.py:20
  246.2 6.2 %copy-start.9 = (bf16[512,4096]{0,1:T(8,128)(2,1)S(1)}, bf16[512,4096]{0,1:T(8,128)(2,1)}, u32[]{:S(2)}) copy-start(bf16[512,4096]{0,1:T(8,128)(2,1)} %all-gather.3.cloned.1.call-done) | copy-start | bytes 12582916
  289.2 6.0 %copy-start.8 = (bf16[512,4096]{0,1:T(8,128)(2,1)S(1)}, bf16[512,4096]{0,1:T(8,128)(2,1)}, u32[]{:S(2)}) copy-start(bf16[512,4096]{0,1:T(8,128)(2,1)} %all-gather.5.cloned.1.call-done) | copy-start | bytes 12582916
  311.3 5.7 %copy-start.2 = (bf16[4096,512]{1,0:T(8,128)(2,1)S(1)}, bf16[4096,512]{1,0:T(8,128)(2,1)}, u32[]{:S(2)}) copy-start(bf16[4096,512]{1,0:T(8,128)(2,1)} %get-tuple-element.63) | copy-start | bytes 12582916
  315.4 93.7 %collective-permute-start.11 = (bf16[4096,512]{1,0:T(8,128)(2,1)S(1)}, bf16[4096,512]{1,0:T(8,128)(2,1)}, u32[]{:S(2)}, u32[]{:S(2)}) collective-permute-start(bf16[4096,512]{1,0:T(8,128)(2,1)S(1)} %convert_element_type.110), channel_id=1, source_target_pairs={{0,16},{4,20},{8,24},{12,28},{16,0},{20,4},{24,8},{28,12},{1,17},{... | collective-permute-start | bytes 12582920 | tf_op jit(solution)/shard_map/cond/branch_2_fun/ppermute | solution.py:20
  317.0 173.0 %collective-permute-start.10 = (bf16[4096,512]{1,0:T(8,128)(2,1)S(1)}, bf16[4096,512]{1,0:T(8,128)(2,1)}, u32[]{:S(2)}, u32[]{:S(2)}) collective-permute-start(bf16[4096,512]{1,0:T(8,128)(2,1)S(1)} %copy-done.2), channel_id=1, source_target_pairs={{0,16},{4,20},{8,24},{12,28},{16,0},{20,4},{24,8},{28,12},{1,17},{... | collective-permute-start | bytes 12582920 | tf_op jit(solution)/shard_map/cond/branch_2_fun/ppermute | solution.py:20
  490.0 13.5 %copy-start.3 = (bf16[1,4096,512]{2,1,0:T(8,128)(2,1)S(1)}, bf16[1,4096,512]{2,1,0:T(8,128)(2,1)}, u32[]{:S(2)}) copy-start(bf16[1,4096,512]{2,1,0:T(8,128)(2,1)} %get-tuple-element.85) | copy-start | bytes 12582916
Sparse Core Ops, SparseCore 0:
  10.8 103.7 all-gather.2
  116.1 80.8 all-gather.4
where the time goes:
time: 517 us
  waiting for transfers between devices  381 us (74%)
  other arithmetic  49.8 us (10%)
  matrix products  24.8 us (5%)
  blocking collectives  21.7 us (4%)
  between operations  17.6 us (3%)
  starting transfers between devices  14.7 us (3%)
  local copies, waits for them, and re-layouts  7.38 us (1%)
    ppermute x4, waiting for transfers between devices, swapped(): return lax.ppermute(value, axis, pairs)  350 us
    all_to_all x2, waiting for transfers between devices, local(): lax.all_to_all(window, 'fsdp', split_axis=1, concat_axis=0, tiled=True)  30.6 us
    another operation x2, other arithmetic, local(): return jnp.stack(changes)[:, None]  30.5 us
    psum x2, blocking collectives, local(): square_sum = lax.psum(jnp.sum(gradient * gradient), 'fsdp')  21.7 us
    dot_general x2, matrix products, local(): lax.dot_general(row_piece, residual, (((0,), (0,)), ((), ())), preferred_...  12.6 us
    dot_general x2, matrix products, local(): jnp.dot(row_piece, weight_now, preferred_element_type=jnp.float32)  12.2 us
    all_to_all x2, starting transfers between devices, local(): lax.all_to_all(window, 'fsdp', split_axis=1, concat_axis=0, tiled=True)  10.4 us
  transfers between devices with their start and end apart: 8, of which 5 were waited for; matrix products, arithmetic and copies ran while one was open for 8% of the time, Pallas kernels for 0%

commit v1 on v0

v1 whole, which is shorter than its diff:
```python
from functools import partial
import math

import jax
import jax.numpy as jnp
from jax import lax
from jax.sharding import PartitionSpec as P

step_size = 0.1
moment_keep = 0.9
pair_keep = 0.5 * moment_keep
f32 = jnp.float32
bf16 = jnp.bfloat16


def swapped(value, bit):
    mask = 2**bit
    pairs = [(source, source ^ mask) for source in range(lax.axis_size("rep"))]
    return lax.ppermute(value, "rep", pairs)


def normalize(row_block):
    values = row_block.astype(f32)
    return (values * lax.rsqrt(jnp.mean(values * values, axis=-1, keepdims=True) + 1e-06)).astype(bf16)


def fsdp_sum(value):
    size = lax.axis_size("fsdp")
    tile = jnp.full((8, 128), value, f32)
    total = tile
    for shift in range(1, size):
        total = total + lax.ppermute(tile, "fsdp", [(s, (s + shift) % size) for s in range(size)])
    return total[0, 0]


def gradient_of(rows, weight):
    depth, width = weight.shape
    scale_in = 1.0 / math.sqrt(depth)
    normed = normalize(rows)
    first = lax.axis_index("fsdp") * width
    column = lax.dynamic_slice_in_dim(rows, first, width, 1).astype(f32)
    following = jnp.concatenate([column[1:], jnp.zeros((1, width), f32)], 0)
    predicted = jnp.dot(normed, weight, preferred_element_type=f32) * scale_in + column
    inside = lax.iota(jnp.int32, rows.shape[0]) < rows.shape[0] - 1
    residual = jnp.where(inside[:, None], predicted - following, 0.0).astype(bf16)
    gradient = scale_in * lax.dot_general(
        normed, residual, (((0,), (0,)), ((), ())), preferred_element_type=f32
    )
    count = depth * width * lax.axis_size("fsdp")
    return gradient, lax.rsqrt(fsdp_sum(jnp.sum(gradient * gradient)) / count + 1e-06)


def both_steps(bits, weight, moment, states):
    bit0, bit1 = bits
    side = (lax.axis_index("rep") >> bit1) & 1
    half = weight.shape[0] // 2

    def part(value, which):
        return lax.dynamic_slice_in_dim(value, which * half, half, 0)

    mine, other = side, 1 - side
    rows0 = lax.all_gather(states[0, 0], "fsdp", axis=0, tiled=True)
    combined = 0.5 * weight.astype(f32) - step_size * pair_keep * moment
    partner_combined = swapped(combined.astype(bf16), bit0)
    partner_half = swapped(part(moment, other).astype(bf16), bit1)
    pair_half = part(moment, mine) + partner_half.astype(f32)
    all_half = pair_half + swapped(pair_half.astype(bf16), bit0).astype(f32)
    rows1 = lax.all_gather(states[1, 0], "fsdp", axis=0, tiled=True)

    gradient0, factor0 = gradient_of(rows0, weight)
    update0 = gradient0 * factor0
    weight1 = (combined + partner_combined.astype(f32) - step_size * update0).astype(bf16)
    change0 = (weight1.astype(f32) - weight.astype(f32)).astype(bf16)

    base = 0.5 * weight1.astype(f32) - step_size * pair_keep * update0
    base_other = part(base, other)
    base_mine = part(base, mine) - step_size * pair_keep * pair_keep * all_half
    got_mine = swapped(base_other.astype(bf16), bit1)
    got_other = swapped(base_mine.astype(bf16), bit1)

    gradient1, factor1 = gradient_of(rows1, weight1)
    change1 = jnp.zeros_like(change0)
    for which, own, got in ((mine, base_mine, got_mine), (other, base_other, got_other)):
        new = (own + got.astype(f32) - step_size * (part(gradient1, which) * factor1)).astype(bf16)
        change = (new.astype(f32) - part(weight1, which).astype(f32)).astype(bf16)
        change1 = lax.dynamic_update_slice_in_dim(change1, change, which * half, 0)
    return jnp.stack([change0, change1])[:, None]


def local(weights, momentum, states, plan):
    levels = lax.axis_size("rep").bit_length() - 1
    top = levels - 1
    cases = [(top, low) for low in range(top)] + [(low, top) for low in range(top)]
    top_last = (plan[1] >= (1 << top)).astype(jnp.int32)
    smaller = jnp.minimum(plan[0], plan[1])
    index = top_last * top
    for bit in range(1, top):
        index = index + (smaller >= 1 << bit).astype(jnp.int32)
    return lax.switch(
        index, [partial(both_steps, bits) for bits in cases], weights[0], momentum[0], states
    )


def solution(mesh):
    placed = (P("rep", None, "fsdp"), P("rep", None, "fsdp"), P(None, "rep", "fsdp", None), P())
    return jax.shard_map(
        local, mesh=mesh, in_specs=placed, out_specs=P(None, "rep", None, "fsdp"), check_vma=False
    )
```

time: 517 us -> 352 us (0.68)
  waiting for transfers between devices: 381 us -> 173 us
  loops' own time: 0.09 us -> 28.1 us
  blocking collectives: 21.7 us -> 0 us
  other arithmetic: 49.8 us -> 69.7 us
  local copies, waits for them, and re-layouts: 7.38 us -> 17.5 us
    ppermute x4 -> x11, waiting for transfers between devices: 350 us -> 90.6 us  [the longest x5 87.2 us: swapped(): return lax.ppermute(value, 'rep', pairs)]
    all_gather x2, waiting for transfers between devices: 0.02 us -> 82 us  [the longest x1 58.6 us: both_steps(): rows1 = lax.all_gather(states[1, 0], 'fsdp', axis=0, tiled=True)]
    all_to_all x2 -> x0, waiting for transfers between devices: 30.6 us -> none  [local(): lax.all_to_all(window, 'fsdp', split_axis=1, concat_axis=0, tiled=True)]
    another operation x0 -> x1, loops' own time: none -> 28.1 us  [local(): lax.switch(index, [partial(both_steps, bits) for bits in cases], weights[...]
    psum x2 -> x0, blocking collectives: 21.7 us -> none  [local(): square_sum = lax.psum(jnp.sum(gradient * gradient), 'fsdp')]
    another operation x2 -> x1, other arithmetic: 30.5 us -> 10.8 us  [both_steps(): return jnp.stack([change0, change1])[:, None]]
    dynamic_update_slice x0 -> x2, other arithmetic: none -> 14.5 us  [both_steps(): change1 = lax.dynamic_update_slice_in_dim(change1, change, which * half, 0)]
    all_to_all x2 -> x0, starting transfers between devices: 10.4 us -> none  [local(): lax.all_to_all(window, 'fsdp', split_axis=1, concat_axis=0, tiled=True)]
  transfers between devices with their start and end apart: 8 -> 13, of which waited for: 5 -> 8; matrix products, arithmetic and copies ran while one was open for 8% -> 29% of each run, Pallas kernels for 0% -> 0%
where the time goes in v1:
time: 352 us; the launch traced here: 347 us
  waiting for transfers between devices  173 us (49%)
  other arithmetic  69.7 us (20%)
  matrix products  28.8 us (8%)
  loops' own time  28.1 us (8%)
  local copies, waits for them, and re-layouts  17.5 us (5%)
  between operations  15.7 us (4%)
  starting transfers between devices  14 us (4%)
    ppermute x5, waiting for transfers between devices, swapped(): return lax.ppermute(value, 'rep', pairs)  87.2 us
    all_gather x1, waiting for transfers between devices, both_steps(): rows1 = lax.all_gather(states[1, 0], 'fsdp', axis=0, tiled=True)  58.6 us
    dot_general x2, matrix products, gradient_of(): lax.dot_general(normed, residual, (((0,), (0,)), ((), ())), preferred_ele...  28.8 us
    another operation x1, loops' own time, local(): lax.switch(index, [partial(both_steps, bits) for bits in cases], weights[...  28.1 us
    all_gather x1, waiting for transfers between devices, both_steps(): rows0 = lax.all_gather(states[0, 0], 'fsdp', axis=0, tiled=True)  23.4 us
    dynamic_update_slice x2, other arithmetic, both_steps(): change1 = lax.dynamic_update_slice_in_dim(change1, change, which * half, 0)  14.5 us
    another operation x1, other arithmetic, both_steps(): return jnp.stack([change0, change1])[:, None]  10.8 us
    sub x1, other arithmetic, both_steps(): base = 0.5 * weight1.astype(f32) - step_size * pair_keep * update0  9.69 us
  transfers between devices with their start and end apart: 13, of which 8 were waited for; matrix products, arithmetic and copies ran while one was open for 29% of the time, Pallas kernels for 0%

profile of v1, /device:TPU:0, one launch (start us, length us, event | category | flops | bytes accessed | tf_op | source)
XLA Modules:
  0.0 347.2 jit_solution(17480473662015655531)
XLA Ops:
  6.5 1.3 fusion.268
  9.6 330.3 %conditional.1 = (bf16[2,1,4096,512]{3,2,0,1:T(8,128)(2,1)}) conditional(s32[]{:T(128)} %bitcast.56, (bf16[4096,512]{1,0:T(8,128)(2,1)}, f32[4096,512]{1,0:T(8,128)}, bf16[2,1,128,4096]{3,2,1,0:T(8,128)(2,1)}) %tuple.63, (bf16[4096,512]{1,0:T(8,128)(2,1)}, f32[4096,512]{1,0:T(8,128)}, ...), branch_computations={%region_0.5_spmd, %region_5.10_spmd, %region_10.15_spmd, %region_1... | conditional | flops 8734120960 | bytes 467820192 | solution.py:99
  35.9 3.1 fusion.263
  39.7 3.9 %dynamic-slice_convert_fusion.12 = bf16[2048,512]{1,0:T(8,128)(2,1)} fusion(f32[4096,512]{1,0:T(8,128)} %get-tuple-element.44, s32[]{:T(128)S(6)} %select_n.83), kind=kLoop, calls=%fused_computation.216 | loop fusion | bytes 4194308 | tf_op jit(solution)/shard_map/cond/branch_3_fun/convert_element_type | solution.py:65
  43.7 3.0 collective-permute-start.37
  46.7 7.5 %fusion.193 = bf16[4096,512]{1,0:T(8,128)(2,1)} fusion(f32[4096,512]{1,0:T(8,128)} %get-tuple-element.44, bf16[4096,512]{1,0:T(8,128)(2,1)S(1)} %copy-done.6), kind=kLoop, calls=%fused_computation.208 | loop fusion | flops 10485760 | bytes 16777216 | tf_op jit(solution)/shard_map/cond/branch_3_fun/convert_element_type | solution.py:64
  54.2 1.3 collective-permute-start.33
  55.5 37.0 %collective-permute-done.37 = bf16[2048,512]{1,0:T(8,128)(2,1)S(1)} collective-permute-done((bf16[2048,512]{1,0:T(8,128)(2,1)}, bf16[2048,512]{1,0:T(8,128)(2,1)S(1)}, u32[]{:S(2)}, u32[]{:S(2)}) %collective-permute-start.37) | collective-permute-done | bytes 2097184 | tf_op jit(solution)/shard_map/cond/branch_3_fun/ppermute | solution.py:19
  92.5 5.0 %fusion.195 = bf16[2048,512]{1,0:T(8,128)(2,1)} fusion(bf16[2048,512]{1,0:T(8,128)(2,1)S(1)} %collective-permute-done.37, f32[4096,512]{1,0:T(8,128)} %get-tuple-element.44, s32[]{:T(128)S(6)} %select_n.82), kind=kLoop, calls=%fused_computation.218 | loop fusion | flops 3145728 | bytes 8388612 | tf_op jit(solution)/shard_map/cond/branch_3_fun/convert_element_type | solution.py:67
  97.5 1.7 collective-permute-start.38
  99.2 23.4 %all-gather.29.cloned.1.call-done = bf16[1,1,512,4096]{3,2,1,0:T(8,128)(2,1)} async-done(((bf16[1,1,128,4096]{3,2,1,0:T(8,128)(2,1)}), bf16[1,1,512,4096]{3,2,1,0:T(8,128)(2,1)}) %all-gather.29.cloned.1.call-update) | async-done | bytes 4194320 | tf_op jit(solution)/shard_map/cond/branch_3_fun/all_gather | solution.py:62
  123.8 3.1 fusion.189
  127.0 14.7 %multiply_reduce_fusion.7 = (f32[]{:T(128)}, f32[4096,512]{1,0:T(8,128)}) fusion(bf16[4096,512]{1,0:T(8,128)(2,1)} %get-tuple-element.43, bf16[1,1,512,4096]{3,2,1,0:T(8,128)(2,1)} %all-gather.29.cloned.1.call-done, f32[512]{0:T(512)S(1)} %add_rsqrt_fusion.7, f32[511,512]{1,0:T(8,128)S(1)} %slice_bitcast_fusion.7, ...), kind=kOutput, calls=%fused_computation.206 | convolution fusion | flops 4315414528 | bytes 22549000 | tf_op jit(solution)/shard_map/cond/branch_3_fun/dot_general | solution.py:46
  143.0 2.1 collective-permute-start.34
  145.1 58.6 %all-gather.31.cloned.1.call-done = bf16[1,1,512,4096]{3,2,1,0:T(8,128)(2,1)} async-done(((bf16[1,1,128,4096]{3,2,1,0:T(8,128)(2,1)}), bf16[1,1,512,4096]{3,2,1,0:T(8,128)(2,1)}) %all-gather.31.cloned.1.call-update) | async-done | bytes 4194320 | tf_op jit(solution)/shard_map/cond/branch_3_fun/all_gather | solution.py:68
  203.8 1.3 dynamic-slice_convert_fusion.14
  205.2 3.2 fusion.191
  210.4 10.8 %fusion.194 = (bf16[1,4096,512]{2,1,0:T(8,128)(2,1)}, bf16[4096,512]{1,0:T(8,128)(2,1)S(1)}) fusion(bf16[4096,512]{1,0:T(8,128)(2,1)S(1)} %copy-done.7, f32[4096,512]{1,0:T(8,128)} %get-tuple-element.76, f32[]{:T(128)} %bitcast.46, bf16[4096,512]{1,0:T(8,128)(2,1)} %collective-permute-done.33, f32[4096,512]{1,0:T(8,128)} %get-tuple-element.44), kind=kLoop, calls=%fused_computation.209 | loop fusion | flops 27262976 | bytes 33554436 | tf_op jit(solution)/shard_map/cond/branch_3_fun/stack | solution.py:87
  221.3 9.7 %fusion.188 = f32[4096,512]{1,0:T(8,128)} fusion(bf16[4096,512]{1,0:T(8,128)(2,1)S(1)} %get-tuple-element.54, f32[4096,512]{1,0:T(8,128)} %get-tuple-element.76, f32[]{:T(128)} %bitcast.46), kind=kLoop, calls=%fused_computation.198 | loop fusion | flops 10485760 | bytes 20971524 | tf_op jit(solution)/shard_map/cond/branch_3_fun/sub | solution.py:75
  231.0 3.9 %dynamic-slice_convert_fusion.13 = bf16[2048,512]{1,0:T(8,128)(2,1)} fusion(f32[4096,512]{1,0:T(8,128)} %fusion.188, s32[]{:T(128)S(6)} %select_n.83), kind=kLoop, calls=%fused_computation.217 | loop fusion | bytes 4194308 | tf_op jit(solution)/shard_map/cond/branch_3_fun/convert_element_type | solution.py:78
  234.9 1.5 collective-permute-start.39
  236.4 5.7 %fusion.247 = bf16[2048,512]{1,0:T(8,128)(2,1)} fusion(bf16[2048,512]{1,0:T(8,128)(2,1)} %collective-permute-done.38, bf16[2048,512]{1,0:T(8,128)(2,1)S(1)} %copy-done.26, f32[4096,512]{1,0:T(8,128)S(1)} %bitcast.319, s32[]{:T(128)S(6)} %select_n.82, f32[4096,512]{1,0:T(8,128)} %fusion.188), kind=kLoop, calls=%fused_computation.251 | loop fusion | flops 7340032 | bytes 14680068 | tf_op jit(solution)/shard_map/cond/branch_3_fun/convert_element_type | solution.py:79
  242.6 14.1 %multiply_reduce_fusion.6 = (f32[]{:T(128)}, f32[4096,512]{1,0:T(8,128)}) fusion(bf16[4096,512]{1,0:T(8,128)(2,1)} %copy-done.14, bf16[1,1,512,4096]{3,2,1,0:T(8,128)(2,1)} %all-gather.31.cloned.1.call-done, f32[512]{0:T(512)S(1)} %add_rsqrt_fusion.6, f32[511,512]{1,0:T(8,128)S(1)} %slice_bitcast_fusion.6, pred[512]{0:T(512)(128)(4,1)S(1)} %iota_compare_fusion.3, ...), kind=kOutput, calls=%fused_computation.204 | convolution fusion | flops 4315414528 | bytes 22549000 | tf_op jit(solution)/shard_map/cond/branch_3_fun/dot_general | solution.py:46
  258.7 1.9 collective-permute-start.40
  261.4 1.5 collective-permute-done.41
  262.9 1.2 collective-permute-done.40
  266.1 17.6 %collective-permute-done.39 = bf16[2048,512]{1,0:T(8,128)(2,1)} collective-permute-done((bf16[2048,512]{1,0:T(8,128)(2,1)}, bf16[2048,512]{1,0:T(8,128)(2,1)}, u32[]{:S(2)}, u32[]{:S(2)}) %collective-permute-start.39) | collective-permute-done | bytes 2097184 | tf_op jit(solution)/shard_map/cond/branch_3_fun/ppermute | solution.py:19
  283.7 2.4 stack.48
  286.1 8.8 %fusion.197 = bf16[1,4096,512]{2,1,0:T(8,128)(2,1)} fusion(bf16[1,4096,512]{2,1,0:T(8,128)(2,1)} %stack.48, s32[]{:T(128)S(6)} %select_n.82, f32[4096,512]{1,0:T(8,128)} %get-tuple-element.78, bf16[2048,512]{1,0:T(8,128)(2,1)} %collective-permute-done.39, bf16[4096,512]{1,0:T(8,128)(2,1)S(1)} %copy-done.15, f32[]{:T(128)} %bitcast.52, ...), kind=kLoop, calls=%fused_computation.220 | loop fusion | flops 16777216 | bytes 23069188 | tf_op jit(solution)/shard_map/cond/branch_3_fun/dynamic_update_slice | solution.py:86
  294.9 32.6 %collective-permute-done.43 = bf16[2048,512]{1,0:T(8,128)(2,1)} collective-permute-done((bf16[2048,512]{1,0:T(8,128)(2,1)}, bf16[2048,512]{1,0:T(8,128)(2,1)}, u32[]{:S(2)}, u32[]{:S(2)}) %collective-permute-start.43) | collective-permute-done | bytes 2097184 | tf_op jit(solution)/shard_map/cond/branch_3_fun/ppermute | solution.py:19
  327.5 5.7 %fusion.199 = bf16[1,4096,512]{2,1,0:T(8,128)(2,1)} fusion(bf16[1,4096,512]{2,1,0:T(8,128)(2,1)} %fusion.197, s32[]{:T(128)S(6)} %select_n.83, f32[4096,512]{1,0:T(8,128)} %get-tuple-element.78, bf16[2048,512]{1,0:T(8,128)(2,1)} %collective-permute-done.43, f32[4096,512]{1,0:T(8,128)S(1)} %bitcast.331, bf16[4096,512]{1,0:T(8,128)(2,1)S(1)} %copy-done.15, ...), kind=kLoop, calls=%fused_computation.222 | loop fusion | flops 10485760 | bytes 14680580 | tf_op jit(solution)/shard_map/cond/branch_3_fun/dynamic_update_slice | solution.py:86
  333.3 6.3 %maximum_bitcast_fusion.3 = bf16[2,1,4096,512]{3,2,0,1:T(8,128)(2,1)} fusion(bf16[1,4096,512]{2,1,0:T(8,128)(2,1)} %fusion.199, bf16[1,4096,512]{2,1,0:T(8,128)(2,1)S(1)} %copy-done.31), kind=kLoop, calls=%fused_computation.203 | loop fusion | flops 4194304 | bytes 16777216 | tf_op jit(solution)/shard_map/cond/branch_3_fun/broadcast_in_dim | solution.py:87
  (53 shorter events, 9.3 us)
Async XLA Ops:
  35.8 86.7 %all-gather.29.cloned.1.call-start = ((), (), s32[]{:S(2)}) async-start(), calls=%async_computation.6 | async-start | bytes 5242880 | tf_op jit(solution)/shard_map/cond/branch_3_fun/all_gather | solution.py:62
  39.0 164.8 %all-gather.31.cloned.1.call-start = ((), (), s32[]{:S(2)}) async-start(), calls=%async_computation.7 | async-start | bytes 5242880 | tf_op jit(solution)/shard_map/cond/branch_3_fun/all_gather | solution.py:68
  39.7 6.9 %copy-start.6 = (bf16[4096,512]{1,0:T(8,128)(2,1)S(1)}, bf16[4096,512]{1,0:T(8,128)(2,1)}, u32[]{:S(2)}) copy-start(bf16[4096,512]{1,0:T(8,128)(2,1)} %get-tuple-element.43) | copy-start | bytes 12582916 | tf_op jit(solution)/shard_map/cond
  43.7 48.8 %collective-permute-start.37 = (bf16[2048,512]{1,0:T(8,128)(2,1)}, bf16[2048,512]{1,0:T(8,128)(2,1)S(1)}, u32[]{:S(2)}, u32[]{:S(2)}) collective-permute-start(bf16[2048,512]{1,0:T(8,128)(2,1)} %dynamic-slice_convert_fusion.12), channel_id=1, source_target_pairs={{0,16},{4,20},{8,24},{12,28},{16,0},{20,4},{24,8},{28,12},{1,17},{... | collective-permute-start | bytes 6291464 | tf_op jit(solution)/shard_map/cond/branch_3_fun/ppermute | solution.py:19
  54.2 156.2 %collective-permute-start.33 = (bf16[4096,512]{1,0:T(8,128)(2,1)}, bf16[4096,512]{1,0:T(8,128)(2,1)}, u32[]{:S(2)}, u32[]{:S(2)}) collective-permute-start(bf16[4096,512]{1,0:T(8,128)(2,1)} %fusion.193), channel_id=1, source_target_pairs={{0,8},{4,12},{8,0},{12,4},{16,24},{20,28},{24,16},{28,20},{1,9},{5... | collective-permute-start | bytes 12582920 | tf_op jit(solution)/shard_map/cond/branch_3_fun/ppermute | solution.py:19
  92.5 5.0 %copy-start.25 = (bf16[2048,512]{1,0:T(8,128)(2,1)}, bf16[2048,512]{1,0:T(8,128)(2,1)S(1)}, u32[]{:S(2)}) copy-start(bf16[2048,512]{1,0:T(8,128)(2,1)S(1)} %collective-permute-done.37) | copy-start | bytes 6291460 | tf_op jit(solution)/shard_map/cond
  97.5 138.9 %collective-permute-start.38 = (bf16[2048,512]{1,0:T(8,128)(2,1)}, bf16[2048,512]{1,0:T(8,128)(2,1)}, u32[]{:S(2)}, u32[]{:S(2)}) collective-permute-start(bf16[2048,512]{1,0:T(8,128)(2,1)} %fusion.195), channel_id=1, source_target_pairs={{0,8},{4,12},{8,0},{12,4},{16,24},{20,28},{24,16},{28,20},{1,9},{5... | collective-permute-start | bytes 6291464 | tf_op jit(solution)/shard_map/cond/branch_3_fun/ppermute | solution.py:19
  142.4 66.1 %collective-permute-start.36 = (f32[8,128]{1,0:T(8,128)S(1)}, f32[8,128]{1,0:T(8,128)S(1)}, u32[]{:S(2)}, u32[]{:S(2)}) collective-permute-start(f32[8,128]{1,0:T(8,128)S(1)} %broadcast_in_dim.108), channel_id=1, source_target_pairs={{0,3},{1,0},{2,1},{3,2},{4,7},{5,4},{6,5},{7,6},{8,11},{9,8},{10,9... | collective-permute-start | bytes 12296 | tf_op jit(solution)/shard_map/cond/branch_3_fun/ppermute | solution.py:32
  142.5 66.0 %collective-permute-start.35 = (f32[8,128]{1,0:T(8,128)S(1)}, f32[8,128]{1,0:T(8,128)S(1)}, u32[]{:S(2)}, u32[]{:S(2)}) collective-permute-start(f32[8,128]{1,0:T(8,128)S(1)} %broadcast_in_dim.108), channel_id=1, source_target_pairs={{0,2},{1,3},{2,0},{3,1},{4,6},{5,7},{6,4},{7,5},{8,10},{9,11},{10,... | collective-permute-start | bytes 12296 | tf_op jit(solution)/shard_map/cond/branch_3_fun/ppermute | solution.py:32
  143.0 65.5 %collective-permute-start.34 = (f32[8,128]{1,0:T(8,128)S(1)}, f32[8,128]{1,0:T(8,128)S(1)}, u32[]{:S(2)}, u32[]{:S(2)}) collective-permute-start(f32[8,128]{1,0:T(8,128)S(1)} %broadcast_in_dim.108), channel_id=1, source_target_pairs={{0,1},{1,2},{2,3},{3,0},{4,5},{5,6},{6,7},{7,4},{8,9},{9,10},{10,1... | collective-permute-start | bytes 12296 | tf_op jit(solution)/shard_map/cond/branch_3_fun/ppermute | solution.py:32
  203.8 6.6 %copy-start.7 = (bf16[4096,512]{1,0:T(8,128)(2,1)S(1)}, bf16[4096,512]{1,0:T(8,128)(2,1)}, u32[]{:S(2)}) copy-start(bf16[4096,512]{1,0:T(8,128)(2,1)} %get-tuple-element.43) | copy-start | bytes 12582916 | tf_op jit(solution)/shard_map/cond
  205.2 31.2 %slice-start.6 = ((s8[8388608]{0:T(1024)(128)(4,1)}), s8[4194304]{0:T(1024)(128)(4,1)S(1)}, s32[]{:S(2)}) async-start(s8[8388608]{0:T(1024)(128)(4,1)} %bitcast.318), calls=%async_computation.14 | async-start | bytes 8388608 | tf_op jit(solution)/shard_map/cond
  210.4 26.0 %slice-start.7 = ((s8[8388608]{0:T(1024)(128)(4,1)}), s8[4194304]{0:T(1024)(128)(4,1)S(1)}, s32[]{:S(2)}) async-start(s8[8388608]{0:T(1024)(128)(4,1)} %bitcast.318), calls=%async_computation.15 | async-start | bytes 8388608 | tf_op jit(solution)/shard_map/cond
  221.3 9.7 %copy-start.14 = (bf16[4096,512]{1,0:T(8,128)(2,1)}, bf16[4096,512]{1,0:T(8,128)(2,1)S(1)}, u32[]{:S(2)}) copy-start(bf16[4096,512]{1,0:T(8,128)(2,1)S(1)} %get-tuple-element.54) | copy-start | bytes 12582916 | tf_op jit(solution)/shard_map/cond
  231.0 5.4 %copy-start.26 = (bf16[2048,512]{1,0:T(8,128)(2,1)S(1)}, bf16[2048,512]{1,0:T(8,128)(2,1)}, u32[]{:S(2)}) copy-start(bf16[2048,512]{1,0:T(8,128)(2,1)} %copy-done.25) | copy-start | bytes 6291460 | tf_op jit(solution)/shard_map/cond
  234.9 48.8 %collective-permute-start.39 = (bf16[2048,512]{1,0:T(8,128)(2,1)}, bf16[2048,512]{1,0:T(8,128)(2,1)}, u32[]{:S(2)}, u32[]{:S(2)}) collective-permute-start(bf16[2048,512]{1,0:T(8,128)(2,1)} %dynamic-slice_convert_fusion.13), channel_id=1, source_target_pairs={{0,16},{4,20},{8,24},{12,28},{16,0},{20,4},{24,8},{28,12},{1,17},{... | collective-permute-start | bytes 6291464 | tf_op jit(solution)/shard_map/cond/branch_3_fun/ppermute | solution.py:19
  242.1 85.4 %collective-permute-start.43 = (bf16[2048,512]{1,0:T(8,128)(2,1)}, bf16[2048,512]{1,0:T(8,128)(2,1)}, u32[]{:S(2)}, u32[]{:S(2)}) collective-permute-start(bf16[2048,512]{1,0:T(8,128)(2,1)} %fusion.247), channel_id=1, source_target_pairs={{0,16},{4,20},{8,24},{12,28},{16,0},{20,4},{24,8},{28,12},{1,17},{... | collective-permute-start | bytes 6291464 | tf_op jit(solution)/shard_map/cond/branch_3_fun/ppermute | solution.py:19
  242.6 43.5 %copy-start.27 = (bf16[2048,512]{1,0:T(8,128)(2,1)S(1)}, bf16[2048,512]{1,0:T(8,128)(2,1)}, u32[]{:S(2)}) copy-start(bf16[2048,512]{1,0:T(8,128)(2,1)} %copy-done.25) | copy-start | bytes 6291460 | tf_op jit(solution)/shard_map/cond
  256.7 29.4 %copy-start.15 = (bf16[4096,512]{1,0:T(8,128)(2,1)S(1)}, bf16[4096,512]{1,0:T(8,128)(2,1)}, u32[]{:S(2)}) copy-start(bf16[4096,512]{1,0:T(8,128)(2,1)} %copy-done.14) | copy-start | bytes 12582916 | tf_op jit(solution)/shard_map/cond
  257.5 3.9 %collective-permute-start.42 = (f32[8,128]{1,0:T(8,128)S(1)}, f32[8,128]{1,0:T(8,128)S(1)}, u32[]{:S(2)}, u32[]{:S(2)}) collective-permute-start(f32[8,128]{1,0:T(8,128)S(1)} %broadcast_in_dim.110), channel_id=1, source_target_pairs={{0,3},{1,0},{2,1},{3,2},{4,7},{5,4},{6,5},{7,6},{8,11},{9,8},{10,9... | collective-permute-start | bytes 12296 | tf_op jit(solution)/shard_map/cond/branch_3_fun/ppermute | solution.py:32
  258.4 4.5 %collective-permute-start.41 = (f32[8,128]{1,0:T(8,128)S(1)}, f32[8,128]{1,0:T(8,128)S(1)}, u32[]{:S(2)}, u32[]{:S(2)}) collective-permute-start(f32[8,128]{1,0:T(8,128)S(1)} %broadcast_in_dim.110), channel_id=1, source_target_pairs={{0,2},{1,3},{2,0},{3,1},{4,6},{5,7},{6,4},{7,5},{8,10},{9,11},{10,... | collective-permute-start | bytes 12296 | tf_op jit(solution)/shard_map/cond/branch_3_fun/ppermute | solution.py:32
  258.7 5.4 %collective-permute-start.40 = (f32[8,128]{1,0:T(8,128)S(1)}, f32[8,128]{1,0:T(8,128)S(1)}, u32[]{:S(2)}, u32[]{:S(2)}) collective-permute-start(f32[8,128]{1,0:T(8,128)S(1)} %broadcast_in_dim.110), channel_id=1, source_target_pairs={{0,1},{1,2},{2,3},{3,0},{4,5},{5,6},{6,7},{7,4},{8,9},{9,10},{10,1... | collective-permute-start | bytes 12296 | tf_op jit(solution)/shard_map/cond/branch_3_fun/ppermute | solution.py:32
  283.7 43.8 %slice-start.14 = ((s8[8388608]{0:T(1024)(128)(4,1)}), s8[4194304]{0:T(1024)(128)(4,1)S(1)}, s32[]{:S(2)}) async-start(s8[8388608]{0:T(1024)(128)(4,1)} %bitcast.330), calls=%async_computation.22 | async-start | bytes 8388608 | tf_op jit(solution)/shard_map/cond
  286.1 41.4 %slice-start.15 = ((s8[8388608]{0:T(1024)(128)(4,1)}), s8[4194304]{0:T(1024)(128)(4,1)S(1)}, s32[]{:S(2)}) async-start(s8[8388608]{0:T(1024)(128)(4,1)} %bitcast.330), calls=%async_computation.23 | async-start | bytes 8388608 | tf_op jit(solution)/shard_map/cond
  294.9 38.3 %copy-start.31 = (bf16[1,4096,512]{2,1,0:T(8,128)(2,1)S(1)}, bf16[1,4096,512]{2,1,0:T(8,128)(2,1)}, u32[]{:S(2)}) copy-start(bf16[1,4096,512]{2,1,0:T(8,128)(2,1)} %get-tuple-element.53) | copy-start | bytes 12582916 | tf_op jit(solution)/shard_map/cond
Sparse Core Ops, SparseCore 0:
  39.1 83.4 all-gather.28
  124.1 79.5 all-gather.30

commit v2 on v1

--- a/solution.py
+++ b/solution.py
@@ -1,4 +1,3 @@
-from functools import partial
 import math
 
 import jax
@@ -50,55 +49,58 @@
     return gradient, lax.rsqrt(fsdp_sum(jnp.sum(gradient * gradient)) / count + 1e-06)
 
 
-def both_steps(bits, weight, moment, states):
-    bit0, bit1 = bits
-    side = (lax.axis_index("rep") >> bit1) & 1
+def local(weights, momentum, states, plan):
+    weight, moment = weights[0], momentum[0]
+    top = lax.axis_size("rep").bit_length() - 2
+    top_last = plan[1] > plan[0]
+    smaller = jnp.minimum(plan[0], plan[1])
     half = weight.shape[0] // 2
+
+    def exchanged(first, second):
+        to_top = jnp.where(top_last, second, first).astype(bf16)
+        to_low = jnp.where(top_last, first, second).astype(bf16)
+        from_top = swapped(to_top, top)
+        from_low = swapped(to_low, 0)
+        for bit in range(1, top):
+            from_low = jnp.where(smaller == 1 << bit, swapped(to_low, bit), from_low)
+        return jnp.where(top_last, from_low, from_top), jnp.where(top_last, from_top, from_low)
 
     def part(value, which):
         return lax.dynamic_slice_in_dim(value, which * half, half, 0)
 
-    mine, other = side, 1 - side
+    mine = ((lax.axis_index("rep") & plan[1]) > 0).astype(jnp.int32)
+    other = 1 - mine
     rows0 = lax.all_gather(states[0, 0], "fsdp", axis=0, tiled=True)
+    rows1 = lax.all_gather(states[1, 0], "fsdp", axis=0, tiled=True)
+
     combined = 0.5 * weight.astype(f32) - step_size * pair_keep * moment
-    partner_combined = swapped(combined.astype(bf16), bit0)
-    partner_half = swapped(part(moment, other).astype(bf16), bit1)
-    pair_half = part(moment, mine) + partner_half.astype(f32)
-    all_half = pair_half + swapped(pair_half.astype(bf16), bit0).astype(f32)
-    rows1 = lax.all_gather(states[1, 0], "fsdp", axis=0, tiled=True)
+    got_low_rows, got_moment = exchanged(combined[:half], part(moment, other))
+    got_high_rows, _ = exchanged(combined[half:], combined[half:])
+    pair_half = part(moment, mine) + got_moment.astype(f32)
 
     gradient0, factor0 = gradient_of(rows0, weight)
     update0 = gradient0 * factor0
-    weight1 = (combined + partner_combined.astype(f32) - step_size * update0).astype(bf16)
+    partner_combined = jnp.concatenate([got_low_rows, got_high_rows], 0).astype(f32)
+    weight1 = (combined + partner_combined - step_size * update0).astype(bf16)
     change0 = (weight1.astype(f32) - weight.astype(f32)).astype(bf16)
 
     base = 0.5 * weight1.astype(f32) - step_size * pair_keep * update0
     base_other = part(base, other)
+    got_pair, got_mine = exchanged(pair_half, base_other)
+    all_half = pair_half + got_pair.astype(f32)
     base_mine = part(base, mine) - step_size * pair_keep * pair_keep * all_half
-    got_mine = swapped(base_other.astype(bf16), bit1)
-    got_other = swapped(base_mine.astype(bf16), bit1)
+    sent_mine = base_mine.astype(bf16)
+    _, got_other = exchanged(sent_mine, sent_mine)
 
+    rows1, _ = lax.optimization_barrier((rows1, sent_mine))
     gradient1, factor1 = gradient_of(rows1, weight1)
-    change1 = jnp.zeros_like(change0)
+    changes = jnp.zeros((2, 1) + weight.shape, bf16)
+    changes = lax.dynamic_update_slice(changes, change0[None, None], (0, 0, 0, 0))
     for which, own, got in ((mine, base_mine, got_mine), (other, base_other, got_other)):
         new = (own + got.astype(f32) - step_size * (part(gradient1, which) * factor1)).astype(bf16)
         change = (new.astype(f32) - part(weight1, which).astype(f32)).astype(bf16)
-        change1 = lax.dynamic_update_slice_in_dim(change1, change, which * half, 0)
-    return jnp.stack([change0, change1])[:, None]
-
-
-def local(weights, momentum, states, plan):
-    levels = lax.axis_size("rep").bit_length() - 1
-    top = levels - 1
-    cases = [(top, low) for low in range(top)] + [(low, top) for low in range(top)]
-    top_last = (plan[1] >= (1 << top)).astype(jnp.int32)
-    smaller = jnp.minimum(plan[0], plan[1])
-    index = top_last * top
-    for bit in range(1, top):
-        index = index + (smaller >= 1 << bit).astype(jnp.int32)
-    return lax.switch(
-        index, [partial(both_steps, bits) for bits in cases], weights[0], momentum[0], states
-    )
+        changes = lax.dynamic_update_slice(changes, change[None, None], (1, 0, which * half, 0))
+    return changes
 
 
 def solution(mesh):

time: 352 us -> 288 us (0.82); the launches traced: 347 us -> 287 us
  waiting for transfers between devices: 173 us -> 135 us
  loops' own time: 28.1 us -> 0 us
  starting transfers between devices: 14 us -> 22.3 us
  local copies, waits for them, and re-layouts: 17.5 us -> 13.6 us
    all_gather x2, waiting for transfers between devices: 82 us -> 10.8 us  [the longest x1 10.8 us: local(): rows0 = lax.all_gather(states[0, 0], 'fsdp', axis=0, tiled=True)]
    ppermute x5 -> x12, waiting for transfers between devices: 87.2 us -> 124 us  [swapped(): return lax.ppermute(value, 'rep', pairs)]
    another operation x1 -> x0, loops' own time: 28.1 us -> none  [local(): lax.switch(index, [partial(both_steps, bits) for bits in cases], weights[...]
    another operation x1 -> x0, other arithmetic: 10.8 us -> none  [both_steps(): return jnp.stack([change0, change1])[:, None]]
    dot_general x2, matrix products: 28.8 us -> 20.5 us  [gradient_of(): lax.dot_general(normed, residual, (((0,), (0,)), ((), ())), preferred_ele...]
    convert_element_type x2 -> x0, local copies, waits for them, and re-layouts: 7.86 us -> none  [the longest x1 3.94 us: both_steps(): partner_half = swapped(part(moment, other).astype(bf16), bit1)]
    dynamic_update_slice x0 -> x1, local copies, waits for them, and re-layouts: none -> 6.65 us  [local(): lax.dynamic_update_slice(changes, change0[None, None], (0, 0, 0, 0))]
    sub x1 -> x2, other arithmetic: 9.69 us -> 15.1 us  [the longest x1 9.14 us: local(): base = 0.5 * weight1.astype(f32) - step_size * pair_keep * update0]
  transfers between devices with their start and end apart: 13 -> 20, of which waited for: 8 -> 7; matrix products, arithmetic and copies ran while one was open for 29% -> 29% of each run, Pallas kernels for 0% -> 0%
where the time goes in v2:
time: 288 us; the launch traced here: 287 us
  waiting for transfers between devices  135 us (47%)
  other arithmetic  72.9 us (25%)
  matrix products  25.6 us (9%)
  starting transfers between devices  22.3 us (8%)
  between operations  18 us (6%)
  local copies, waits for them, and re-layouts  13.6 us (5%)
    ppermute x12, waiting for transfers between devices, swapped(): return lax.ppermute(value, 'rep', pairs)  124 us
    dot_general x2, matrix products, gradient_of(): lax.dot_general(normed, residual, (((0,), (0,)), ((), ())), preferred_ele...  20.5 us
    convert_element_type x2, other arithmetic, exchanged(): to_low = jnp.where(top_last, first, second).astype(bf16)  19 us
    dynamic_update_slice x2, other arithmetic, local(): lax.dynamic_update_slice(changes, change[None, None], (1, 0, which * half...  13.5 us
    ppermute x12, starting transfers between devices, swapped(): return lax.ppermute(value, 'rep', pairs)  13 us
    all_gather x1, waiting for transfers between devices, local(): rows0 = lax.all_gather(states[0, 0], 'fsdp', axis=0, tiled=True)  10.8 us
    ppermute x6, starting transfers between devices, fsdp_sum(): lax.ppermute(tile, 'fsdp', [(s, (s + shift) % size) for s in range(size)])  9.27 us
    sub x1, other arithmetic, local(): base = 0.5 * weight1.astype(f32) - step_size * pair_keep * update0  9.14 us
  transfers between devices with their start and end apart: 20, of which 7 were waited for; matrix products, arithmetic and copies ran while one was open for 29% of the time, Pallas kernels for 0%

profile of v2, /device:TPU:0, one launch (start us, length us, event | category | flops | bytes accessed | tf_op | source)
XLA Modules:
  0.0 287.2 jit_solution(16555831279696874426)
XLA Ops:
  6.5 3.1 %fusion.68 = (bf16[1,1,128,4096]{3,2,1,0:T(8,128)(2,1)}, bf16[1,1,128,4096]{3,2,1,0:T(8,128)(2,1)}) fusion(bf16[2,1,128,4096]{3,2,1,0:T(8,128)(2,1)} %param.6), kind=kLoop, calls=%fused_computation.66 | loop fusion | bytes 4194304 | tf_op jit(solution)/shard_map/slice | solution.py:74
  12.0 6.0 %fusion = f32[4096,512]{1,0:T(8,128)S(1)} fusion(f32[1,4096,512]{2,1,0:T(8,128)} %param.5, bf16[1,4096,512]{2,1,0:T(8,128)(2,1)} %param.4), kind=kLoop, calls=%fused_computation.7 | loop fusion | flops 8388608 | bytes 20971520 | tf_op jit(solution)/shard_map/sub | solution.py:76
  18.0 9.6 %fusion.8 = (bf16[2048,512]{1,0:T(8,128)(2,1)}, bf16[2048,512]{1,0:T(8,128)(2,1)}, bf16[2048,512]{1,0:T(8,128)(2,1)}) fusion(f32[4096,512]{1,0:T(8,128)S(1)} %fusion, f32[1,4096,512]{2,1,0:T(8,128)} %param.5, s32[]{:T(128)S(6)} %select_n.97, pred[]{:T(512)S(6)} %gt.6), kind=kLoop, calls=%fused_computation.23 | loop fusion | flops 2097152 | bytes 12582917 | tf_op jit(solution)/shard_map/convert_element_type | solution.py:61
  27.6 2.9 %collective-permute-start = (bf16[2048,512]{1,0:T(8,128)(2,1)}, bf16[2048,512]{1,0:T(8,128)(2,1)S(1)}, u32[]{:S(2)}, u32[]{:S(2)}) collective-permute-start(bf16[2048,512]{1,0:T(8,128)(2,1)} %get-tuple-element.11), channel_id=1, source_target_pairs={{0,8},{4,12},{8,0},{12,4},{16,24},{20,28},{24,16},{28,20},{1,9},{5... | collective-permute-start | bytes 6291464 | tf_op jit(solution)/shard_map/ppermute | solution.py:18
  30.5 1.5 collective-permute-start.2
  33.8 43.4 %collective-permute-done = bf16[2048,512]{1,0:T(8,128)(2,1)S(1)} collective-permute-done((bf16[2048,512]{1,0:T(8,128)(2,1)}, bf16[2048,512]{1,0:T(8,128)(2,1)S(1)}, u32[]{:S(2)}, u32[]{:S(2)}) %collective-permute-start) | collective-permute-done | bytes 2097184 | tf_op jit(solution)/shard_map/ppermute | solution.py:18
  77.1 2.1 collective-permute-start.5
  79.2 3.2 %broadcast_select_fusion.2 = bf16[2048,512]{1,0:T(8,128)(2,1)} fusion(bf16[2048,512]{1,0:T(8,128)(2,1)} %collective-permute-done.2, pred[]{:T(512)S(6)} %gt.6, bf16[2048,512]{1,0:T(8,128)(2,1)S(1)} %collective-permute-done, bf16[2048,512]{1,0:T(8,128)(2,1)} %collective-permute-done.1, pred[]{:T(512)S(6)} %eq.2), kind=kLoop, calls=%fused_computation.41 | loop fusion | flops 2097152 | bytes 8388610 | tf_op jit(solution)/shard_map/jit(_where)/select_n | solution.py:66
  82.4 10.8 %all-gather.5.cloned.1.call-done = bf16[1,1,512,4096]{3,2,1,0:T(8,128)(2,1)} async-done(((bf16[1,1,128,4096]{3,2,1,0:T(8,128)(2,1)}), bf16[1,1,512,4096]{3,2,1,0:T(8,128)(2,1)}) %all-gather.5.cloned.1.call-update) | async-done | bytes 4194320 | tf_op jit(solution)/shard_map/all_gather | solution.py:73
  93.3 3.2 %fusion.5 = f32[512]{0:T(512)S(1)} fusion(bf16[1,1,512,4096]{3,2,1,0:T(8,128)(2,1)} %all-gather.5.cloned.1.call-done), kind=kLoop, calls=%fused_computation.12 | loop fusion | flops 6290944 | bytes 4196352 | tf_op jit(solution)/shard_map/reduce_sum | solution.py:23
  97.8 5.1 %fusion.54 = bf16[512,512]{1,0:T(8,128)(2,1)S(1)} fusion(bf16[1,4096,512]{2,1,0:T(8,128)(2,1)S(1)} %copy-done.4, bf16[1,1,512,4096]{3,2,1,0:T(8,128)(2,1)} %all-gather.5.cloned.1.call-done, f32[512]{0:T(512)S(1)} %add_rsqrt_fusion.1, f32[511,512]{1,0:T(8,128)S(1)} %slice_bitcast_fusion, pred[512]{0:T(512)(128)(4,1)S(1)} %iota_compare_fusion, s32[]{:T(128)S(6)} %select_n.104), kind=kOutput, calls=%fused_computation.52 | convolution fusion | flops 2155347968 | bytes 10486276 | tf_op jit(solution)/shard_map/dot_general | solution.py:42
  102.9 6.7 %multiply_reduce_fusion.1 = (f32[]{:T(128)}, f32[4096,512]{1,0:T(8,128)}) fusion(bf16[512,512]{1,0:T(8,128)(2,1)S(1)} %fusion.54, bf16[1,1,512,4096]{3,2,1,0:T(8,128)(2,1)S(1)} %copy-done.9, f32[512]{0:T(512)S(1)} %add_rsqrt_fusion.1), kind=kOutput, calls=%fused_computation.16 | convolution fusion | flops 2160066560 | bytes 13109252 | tf_op jit(solution)/shard_map/dot_general | solution.py:45
  111.3 10.0 %collective-permute-done.3 = bf16[2048,512]{1,0:T(8,128)(2,1)} collective-permute-done((bf16[2048,512]{1,0:T(8,128)(2,1)}, bf16[2048,512]{1,0:T(8,128)(2,1)}, u32[]{:S(2)}, u32[]{:S(2)}) %collective-permute-start.3) | collective-permute-done | bytes 2097184 | tf_op jit(solution)/shard_map/ppermute | solution.py:18
  121.4 3.8 %collective-permute-start.8 = (f32[8,128]{1,0:T(8,128)S(1)}, f32[8,128]{1,0:T(8,128)S(1)}, u32[]{:S(2)}, u32[]{:S(2)}) collective-permute-start(f32[8,128]{1,0:T(8,128)S(1)} %broadcast_in_dim.40), channel_id=1, source_target_pairs={{0,3},{1,0},{2,1},{3,2},{4,7},{5,4},{6,5},{7,6},{8,11},{9,8},{10,9... | collective-permute-start | bytes 12296 | tf_op jit(solution)/shard_map/ppermute | solution.py:31
  125.2 1.9 select_select_fusion
  129.0 9.1 %fusion.2 = (f32[4096,512]{1,0:T(8,128)S(1)}, bf16[4096,512]{1,0:T(8,128)(2,1)}) fusion(f32[4096,512]{1,0:T(8,128)} %get-tuple-element.19, f32[]{:T(128)} %bitcast.9, f32[4096,512]{1,0:T(8,128)} %copy-done.3, bf16[2048,512]{1,0:T(8,128)(2,1)S(1)} %select_select_fusion, bf16[2048,512]{1,0:T(8,128)(2,1)S(1)} %copy-done.8), kind=kLoop, calls=%fused_computation.9 | loop fusion | flops 27262976 | bytes 33554436 | tf_op jit(solution)/shard_map/sub | solution.py:87
  138.2 9.4 %select_convert_fusion.1 = (bf16[2048,512]{1,0:T(8,128)(2,1)}, f32[2048,512]{1,0:T(8,128)S(1)}) fusion(f32[4096,512]{1,0:T(8,128)S(1)} %get-tuple-element.9, s32[]{:T(128)S(6)} %select_n.97, pred[]{:T(512)S(6)} %gt.6, bf16[2048,512]{1,0:T(8,128)(2,1)} %collective-permute-done.2, bf16[2048,512]{1,0:T(8,128)(2,1)} %copy-done.5, ...), kind=kLoop, calls=%fused_computation.33 | loop fusion | flops 5242880 | bytes 18874378 | tf_op jit(solution)/shard_map/convert_element_type | solution.py:61
  148.3 1.6 collective-permute-start.11
  150.7 1.5 collective-permute-start.9
  152.1 42.5 %collective-permute-done.11 = bf16[2048,512]{1,0:T(8,128)(2,1)S(1)} collective-permute-done((bf16[2048,512]{1,0:T(8,128)(2,1)S(1)}, bf16[2048,512]{1,0:T(8,128)(2,1)S(1)}, u32[]{:S(2)}, u32[]{:S(2)}) %collective-permute-start.11) | collective-permute-done | bytes 2097184 | tf_op jit(solution)/shard_map/ppermute | solution.py:18
  194.7 4.1 %collective-permute-done.9 = bf16[2048,512]{1,0:T(8,128)(2,1)} collective-permute-done((bf16[2048,512]{1,0:T(8,128)(2,1)S(1)}, bf16[2048,512]{1,0:T(8,128)(2,1)}, u32[]{:S(2)}, u32[]{:S(2)}) %collective-permute-start.9) | collective-permute-done | bytes 2097184 | tf_op jit(solution)/shard_map/ppermute | solution.py:18
  198.8 2.9 %fusion.62 = bf16[2048,512]{1,0:T(8,128)(2,1)} fusion(f32[2048,512]{1,0:T(8,128)S(1)} %get-tuple-element.8, bf16[2048,512]{1,0:T(8,128)(2,1)S(1)} %collective-permute-done.11, pred[]{:T(512)S(6)} %gt.6, f32[4096,512]{1,0:T(8,128)S(1)} %get-tuple-element.9, s32[]{:T(128)S(6)} %mul.130, bf16[2048,512]{1,0:T(8,128)(2,1)} %collective-permute-done.9, ...), kind=kLoop, calls=%fused_computation.55 | loop fusion | flops 7340032 | bytes 16777222 | tf_op jit(solution)/shard_map/convert_element_type | solution.py:92
  202.9 3.1 %fusion.3 = f32[512]{0:T(512)S(1)} fusion(bf16[512,4096]{1,0:T(8,128)(2,1)} %bitcast.69), kind=kLoop, calls=%fused_computation.10 | loop fusion | flops 6290944 | bytes 4196352 | tf_op jit(solution)/shard_map/reduce_sum | solution.py:23
  206.1 13.7 %multiply_reduce_fusion = (f32[]{:T(128)}, f32[4096,512]{1,0:T(8,128)}) fusion(bf16[4096,512]{1,0:T(8,128)(2,1)} %get-tuple-element.10, bf16[512,4096]{1,0:T(8,128)(2,1)} %bitcast.70, f32[512]{0:T(512)S(1)} %add_rsqrt_fusion, f32[511,512]{1,0:T(8,128)S(1)} %slice.49, pred[512]{0:T(512)(128)(4,1)S(1)} %iota_compare_fusion, s32[]{:T(128)S(6)} %select_n.104), kind=kOutput, calls=%fused_computation.14 | convolution fusion | flops 4315414528 | bytes 22549000 | tf_op jit(solution)/shard_map/dot_general | solution.py:45
  220.5 4.3 %collective-permute-start.13 = (f32[8,128]{1,0:T(8,128)S(1)}, f32[8,128]{1,0:T(8,128)S(1)}, u32[]{:S(2)}, u32[]{:S(2)}) collective-permute-start(f32[8,128]{1,0:T(8,128)S(1)} %broadcast_in_dim.42), channel_id=1, source_target_pairs={{0,2},{1,3},{2,0},{3,1},{4,6},{5,7},{6,4},{7,5},{8,10},{9,11},{10,... | collective-permute-start | bytes 12296 | tf_op jit(solution)/shard_map/ppermute | solution.py:31
  224.8 1.4 collective-permute-start.15
  226.2 1.5 collective-permute-start.16
  227.7 6.8 %fusion.7 = bf16[1,1,4096,512]{3,2,1,0:T(8,128)(2,1)} fusion(bf16[4096,512]{1,0:T(8,128)(2,1)} %get-tuple-element.10, bf16[1,4096,512]{2,1,0:T(8,128)(2,1)} %param.4), kind=kLoop, calls=%fused_computation.18 | loop fusion | flops 8388608 | bytes 12582912 | tf_op jit(solution)/shard_map/broadcast_in_dim | solution.py:98
  234.5 6.7 %dynamic_update_slice.9 = bf16[2,1,4096,512]{3,2,1,0:T(8,128)(2,1)} pad(bf16[1,1,4096,512]{3,2,1,0:T(8,128)(2,1)} %fusion.7, bf16[]{:T(256)} %constant.60.clone.1), padding=0_1x0_0x0_0x0_0 | pad | bytes 12582914 | tf_op jit(solution)/shard_map/dynamic_update_slice | solution.py:98
  243.1 6.2 %fusion.13 = bf16[2,1,4096,512]{3,2,1,0:T(8,128)(2,1)} fusion(bf16[2,1,4096,512]{3,2,1,0:T(8,128)(2,1)} %dynamic_update_slice.9, s32[]{:T(128)S(6)} %mul.130, f32[4096,512]{1,0:T(8,128)} %get-tuple-element.21, bf16[4096,512]{1,0:T(8,128)(2,1)} %get-tuple-element.10, f32[]{:T(128)} %bitcast.13, bf16[2048,512]{1,0:T(8,128)(2,1)} %copy-done.6, pred[]{:T(512)S(6)} %gt.6, ...), kind=kLoop, calls=%fused_computation.35 | loop fusion | flops 17825792 | bytes 23069190 | tf_op jit(solution)/shard_map/dynamic_update_slice | solution.py:102
  249.3 22.6 %collective-permute-done.15 = bf16[2048,512]{1,0:T(8,128)(2,1)} collective-permute-done((bf16[2048,512]{1,0:T(8,128)(2,1)}, bf16[2048,512]{1,0:T(8,128)(2,1)}, u32[]{:S(2)}, u32[]{:S(2)}) %collective-permute-start.15) | collective-permute-done | bytes 2097184 | tf_op jit(solution)/shard_map/ppermute | solution.py:18
  273.1 7.3 %fusion.15 = bf16[2,1,4096,512]{3,2,1,0:T(8,128)(2,1)} fusion(bf16[2,1,4096,512]{3,2,1,0:T(8,128)(2,1)} %fusion.13, s32[]{:T(128)S(6)} %select_n.97, f32[4096,512]{1,0:T(8,128)} %get-tuple-element.21, f32[4096,512]{1,0:T(8,128)S(1)} %bitcast.67, bf16[4096,512]{1,0:T(8,128)(2,1)} %get-tuple-element.10, bf16[2048,512]{1,0:T(8,128)(2,1)} %collective-permute-done.15, ...), kind=kLoop, calls=%fused_computation.37 | loop fusion | flops 12582912 | bytes 18874886 | tf_op jit(solution)/shard_map/dynamic_update_slice | solution.py:102
  (71 shorter events, 11.1 us)
Async XLA Ops:
  6.5 86.7 %all-gather.5.cloned.1.call-start = ((), (), s32[]{:S(2)}) async-start(), calls=%async_computation | async-start | bytes 5242880 | tf_op jit(solution)/shard_map/all_gather | solution.py:73
  9.6 192.1 %all-gather.7.cloned.1.call-start = ((), (), s32[]{:S(2)}) async-start(), calls=%async_computation.1 | async-start | bytes 5242880 | tf_op jit(solution)/shard_map/all_gather | solution.py:74
  18.0 9.6 %copy-start.3 = (f32[4096,512]{1,0:T(8,128)}, f32[4096,512]{1,0:T(8,128)S(1)}, u32[]{:S(2)}) copy-start(f32[4096,512]{1,0:T(8,128)S(1)} %fusion) | copy-start | bytes 25165828
  27.6 49.6 %collective-permute-start = (bf16[2048,512]{1,0:T(8,128)(2,1)}, bf16[2048,512]{1,0:T(8,128)(2,1)S(1)}, u32[]{:S(2)}, u32[]{:S(2)}) collective-permute-start(bf16[2048,512]{1,0:T(8,128)(2,1)} %get-tuple-element.11), channel_id=1, source_target_pairs={{0,8},{4,12},{8,0},{12,4},{16,24},{20,28},{24,16},{28,20},{1,9},{5... | collective-permute-start | bytes 6291464 | tf_op jit(solution)/shard_map/ppermute | solution.py:18
  30.5 48.8 %collective-permute-start.1 = (bf16[2048,512]{1,0:T(8,128)(2,1)}, bf16[2048,512]{1,0:T(8,128)(2,1)}, u32[]{:S(2)}, u32[]{:S(2)}) collective-permute-start(bf16[2048,512]{1,0:T(8,128)(2,1)} %get-tuple-element.11), channel_id=1, source_target_pairs={{0,4},{4,0},{8,12},{12,8},{16,20},{20,16},{24,28},{28,24},{1,5},{5... | collective-permute-start | bytes 6291464 | tf_op jit(solution)/shard_map/ppermute | solution.py:18
  30.5 48.8 %collective-permute-start.2 = (bf16[2048,512]{1,0:T(8,128)(2,1)}, bf16[2048,512]{1,0:T(8,128)(2,1)}, u32[]{:S(2)}, u32[]{:S(2)}) collective-permute-start(bf16[2048,512]{1,0:T(8,128)(2,1)} %get-tuple-element.12), channel_id=1, source_target_pairs={{0,16},{4,20},{8,24},{12,28},{16,0},{20,4},{24,8},{28,12},{1,17},{... | collective-permute-start | bytes 6291464 | tf_op jit(solution)/shard_map/ppermute | solution.py:18
  32.0 89.4 %collective-permute-start.3 = (bf16[2048,512]{1,0:T(8,128)(2,1)}, bf16[2048,512]{1,0:T(8,128)(2,1)}, u32[]{:S(2)}, u32[]{:S(2)}) collective-permute-start(bf16[2048,512]{1,0:T(8,128)(2,1)} %get-tuple-element.13), channel_id=1, source_target_pairs={{0,8},{4,12},{8,0},{12,4},{16,24},{20,28},{24,16},{28,20},{1,9},{5... | collective-permute-start | bytes 6291464 | tf_op jit(solution)/shard_map/ppermute | solution.py:18
  32.5 92.7 %collective-permute-start.4 = (bf16[2048,512]{1,0:T(8,128)(2,1)}, bf16[2048,512]{1,0:T(8,128)(2,1)}, u32[]{:S(2)}, u32[]{:S(2)}) collective-permute-start(bf16[2048,512]{1,0:T(8,128)(2,1)} %get-tuple-element.13), channel_id=1, source_target_pairs={{0,4},{4,0},{8,12},{12,8},{16,20},{20,16},{24,28},{28,24},{1,5},{5... | collective-permute-start | bytes 6291464 | tf_op jit(solution)/shard_map/ppermute | solution.py:18
  77.1 5.3 %copy-start.5 = (bf16[2048,512]{1,0:T(8,128)(2,1)}, bf16[2048,512]{1,0:T(8,128)(2,1)S(1)}, u32[]{:S(2)}) copy-start(bf16[2048,512]{1,0:T(8,128)(2,1)S(1)} %collective-permute-done) | copy-start | bytes 6291460
  77.1 48.1 %collective-permute-start.5 = (bf16[2048,512]{1,0:T(8,128)(2,1)}, bf16[2048,512]{1,0:T(8,128)(2,1)}, u32[]{:S(2)}, u32[]{:S(2)}) collective-permute-start(bf16[2048,512]{1,0:T(8,128)(2,1)} %get-tuple-element.13), channel_id=1, source_target_pairs={{0,16},{4,20},{8,24},{12,28},{16,0},{20,4},{24,8},{28,12},{1,17},{... | collective-permute-start | bytes 6291464 | tf_op jit(solution)/shard_map/ppermute | solution.py:18
  93.2 4.5 %copy-start.4 = (bf16[1,4096,512]{2,1,0:T(8,128)(2,1)S(1)}, bf16[1,4096,512]{2,1,0:T(8,128)(2,1)}, u32[]{:S(2)}) copy-start(bf16[1,4096,512]{2,1,0:T(8,128)(2,1)} %param.4) | copy-start | bytes 12582916
  97.8 5.1 %copy-start.9 = (bf16[1,1,512,4096]{3,2,1,0:T(8,128)(2,1)S(1)}, bf16[1,1,512,4096]{3,2,1,0:T(8,128)(2,1)}, u32[]{:S(2)}) copy-start(bf16[1,1,512,4096]{3,2,1,0:T(8,128)(2,1)} %all-gather.5.cloned.1.call-done) | copy-start | bytes 12582916
  110.3 18.7 %copy-start.8 = (bf16[2048,512]{1,0:T(8,128)(2,1)S(1)}, bf16[2048,512]{1,0:T(8,128)(2,1)}, u32[]{:S(2)}) copy-start(bf16[2048,512]{1,0:T(8,128)(2,1)} %broadcast_select_fusion.2) | copy-start | bytes 6291460
  110.3 16.8 %collective-permute-start.6 = (f32[8,128]{1,0:T(8,128)S(1)}, f32[8,128]{1,0:T(8,128)S(1)}, u32[]{:S(2)}, u32[]{:S(2)}) collective-permute-start(f32[8,128]{1,0:T(8,128)S(1)} %broadcast_in_dim.40), channel_id=1, source_target_pairs={{0,1},{1,2},{2,3},{3,0},{4,5},{5,6},{6,7},{7,4},{8,9},{9,10},{10,1... | collective-permute-start | bytes 12296 | tf_op jit(solution)/shard_map/ppermute | solution.py:31
  110.4 16.8 %collective-permute-start.7 = (f32[8,128]{1,0:T(8,128)S(1)}, f32[8,128]{1,0:T(8,128)S(1)}, u32[]{:S(2)}, u32[]{:S(2)}) collective-permute-start(f32[8,128]{1,0:T(8,128)S(1)} %broadcast_in_dim.40), channel_id=1, source_target_pairs={{0,2},{1,3},{2,0},{3,1},{4,6},{5,7},{6,4},{7,5},{8,10},{9,11},{10,... | collective-permute-start | bytes 12296 | tf_op jit(solution)/shard_map/ppermute | solution.py:31
  121.4 5.8 %collective-permute-start.8 = (f32[8,128]{1,0:T(8,128)S(1)}, f32[8,128]{1,0:T(8,128)S(1)}, u32[]{:S(2)}, u32[]{:S(2)}) collective-permute-start(f32[8,128]{1,0:T(8,128)S(1)} %broadcast_in_dim.40), channel_id=1, source_target_pairs={{0,3},{1,0},{2,1},{3,2},{4,7},{5,4},{6,5},{7,6},{8,11},{9,8},{10,9... | collective-permute-start | bytes 12296 | tf_op jit(solution)/shard_map/ppermute | solution.py:31
  138.2 60.6 %copy-start = (f32[4096,512]{1,0:T(8,128)}, f32[4096,512]{1,0:T(8,128)S(1)}, u32[]{:S(2)}) copy-start(f32[4096,512]{1,0:T(8,128)S(1)} %get-tuple-element.9) | copy-start | bytes 25165828
  147.5 51.3 %copy-start.1 = (f32[2048,512]{1,0:T(8,128)}, f32[2048,512]{1,0:T(8,128)S(1)}, u32[]{:S(2)}) copy-start(f32[2048,512]{1,0:T(8,128)S(1)} %get-tuple-element.8) | copy-start | bytes 12582916
  148.3 46.4 %collective-permute-start.11 = (bf16[2048,512]{1,0:T(8,128)(2,1)S(1)}, bf16[2048,512]{1,0:T(8,128)(2,1)S(1)}, u32[]{:S(2)}, u32[]{:S(2)}) collective-permute-start(bf16[2048,512]{1,0:T(8,128)(2,1)S(1)} %select_convert_fusion), channel_id=1, source_target_pairs={{0,16},{4,20},{8,24},{12,28},{16,0},{20,4},{24,8},{28,12},{1,17},{... | collective-permute-start | bytes 6291464 | tf_op jit(solution)/shard_map/ppermute | solution.py:18
  150.7 44.0 %collective-permute-start.10 = (bf16[2048,512]{1,0:T(8,128)(2,1)S(1)}, bf16[2048,512]{1,0:T(8,128)(2,1)S(1)}, u32[]{:S(2)}, u32[]{:S(2)}) collective-permute-start(bf16[2048,512]{1,0:T(8,128)(2,1)S(1)} %copy-done.10), channel_id=1, source_target_pairs={{0,4},{4,0},{8,12},{12,8},{16,20},{20,16},{24,28},{28,24},{1,5},{5... | collective-permute-start | bytes 6291464 | tf_op jit(solution)/shard_map/ppermute | solution.py:18
  150.7 48.1 %collective-permute-start.9 = (bf16[2048,512]{1,0:T(8,128)(2,1)S(1)}, bf16[2048,512]{1,0:T(8,128)(2,1)}, u32[]{:S(2)}, u32[]{:S(2)}) collective-permute-start(bf16[2048,512]{1,0:T(8,128)(2,1)S(1)} %copy-done.10), channel_id=1, source_target_pairs={{0,8},{4,12},{8,0},{12,4},{16,24},{20,28},{24,16},{28,20},{1,9},{5... | collective-permute-start | bytes 6291464 | tf_op jit(solution)/shard_map/ppermute | solution.py:18
  194.7 4.1 %copy-start.6 = (bf16[2048,512]{1,0:T(8,128)(2,1)}, bf16[2048,512]{1,0:T(8,128)(2,1)S(1)}, u32[]{:S(2)}) copy-start(bf16[2048,512]{1,0:T(8,128)(2,1)S(1)} %collective-permute-done.11) | copy-start | bytes 6291460
  194.7 4.1 %copy-start.7 = (bf16[2048,512]{1,0:T(8,128)(2,1)}, bf16[2048,512]{1,0:T(8,128)(2,1)S(1)}, u32[]{:S(2)}) copy-start(bf16[2048,512]{1,0:T(8,128)(2,1)S(1)} %collective-permute-done.10) | copy-start | bytes 6291460
  220.4 7.3 %collective-permute-start.12 = (f32[8,128]{1,0:T(8,128)S(1)}, f32[8,128]{1,0:T(8,128)S(1)}, u32[]{:S(2)}, u32[]{:S(2)}) collective-permute-start(f32[8,128]{1,0:T(8,128)S(1)} %broadcast_in_dim.42), channel_id=1, source_target_pairs={{0,1},{1,2},{2,3},{3,0},{4,5},{5,6},{6,7},{7,4},{8,9},{9,10},{10,1... | collective-permute-start | bytes 12296 | tf_op jit(solution)/shard_map/ppermute | solution.py:31
  220.5 20.7 %collective-permute-start.13 = (f32[8,128]{1,0:T(8,128)S(1)}, f32[8,128]{1,0:T(8,128)S(1)}, u32[]{:S(2)}, u32[]{:S(2)}) collective-permute-start(f32[8,128]{1,0:T(8,128)S(1)} %broadcast_in_dim.42), channel_id=1, source_target_pairs={{0,2},{1,3},{2,0},{3,1},{4,6},{5,7},{6,4},{7,5},{8,10},{9,11},{10,... | collective-permute-start | bytes 12296 | tf_op jit(solution)/shard_map/ppermute | solution.py:31
  224.8 16.4 %collective-permute-start.14 = (f32[8,128]{1,0:T(8,128)S(1)}, f32[8,128]{1,0:T(8,128)S(1)}, u32[]{:S(2)}, u32[]{:S(2)}) collective-permute-start(f32[8,128]{1,0:T(8,128)S(1)} %broadcast_in_dim.42), channel_id=1, source_target_pairs={{0,3},{1,0},{2,1},{3,2},{4,7},{5,4},{6,5},{7,6},{8,11},{9,8},{10,9... | collective-permute-start | bytes 12296 | tf_op jit(solution)/shard_map/ppermute | solution.py:31
  224.8 47.1 %collective-permute-start.15 = (bf16[2048,512]{1,0:T(8,128)(2,1)}, bf16[2048,512]{1,0:T(8,128)(2,1)}, u32[]{:S(2)}, u32[]{:S(2)}) collective-permute-start(bf16[2048,512]{1,0:T(8,128)(2,1)} %fusion.62), channel_id=1, source_target_pairs={{0,16},{4,20},{8,24},{12,28},{16,0},{20,4},{24,8},{28,12},{1,17},{... | collective-permute-start | bytes 6291464 | tf_op jit(solution)/shard_map/ppermute | solution.py:18
  226.2 46.8 %collective-permute-start.16 = (bf16[2048,512]{1,0:T(8,128)(2,1)}, bf16[2048,512]{1,0:T(8,128)(2,1)}, u32[]{:S(2)}, u32[]{:S(2)}) collective-permute-start(bf16[2048,512]{1,0:T(8,128)(2,1)} %fusion.62), channel_id=1, source_target_pairs={{0,8},{4,12},{8,0},{12,4},{16,24},{20,28},{24,16},{28,20},{1,9},{5... | collective-permute-start | bytes 6291464 | tf_op jit(solution)/shard_map/ppermute | solution.py:18
  227.7 45.3 %collective-permute-start.17 = (bf16[2048,512]{1,0:T(8,128)(2,1)}, bf16[2048,512]{1,0:T(8,128)(2,1)}, u32[]{:S(2)}, u32[]{:S(2)}) collective-permute-start(bf16[2048,512]{1,0:T(8,128)(2,1)} %fusion.62), channel_id=1, source_target_pairs={{0,4},{4,0},{8,12},{12,8},{16,20},{20,16},{24,28},{28,24},{1,5},{5... | collective-permute-start | bytes 6291464 | tf_op jit(solution)/shard_map/ppermute | solution.py:18
  227.7 15.3 %slice-start = ((s8[8388608]{0:T(1024)(128)(4,1)}), s8[4194304]{0:T(1024)(128)(4,1)S(1)}, s32[]{:S(2)}) async-start(s8[8388608]{0:T(1024)(128)(4,1)} %bitcast.66), calls=%async_computation.2 | async-start | bytes 8388608
  234.5 8.5 %slice-start.1 = ((s8[8388608]{0:T(1024)(128)(4,1)}), s8[4194304]{0:T(1024)(128)(4,1)S(1)}, s32[]{:S(2)}) async-start(s8[8388608]{0:T(1024)(128)(4,1)} %bitcast.66), calls=%async_computation.3 | async-start | bytes 8388608
  234.5 8.5 %copy-start.2 = (f32[2048,512]{1,0:T(8,128)S(1)}, f32[2048,512]{1,0:T(8,128)}, u32[]{:S(2)}) copy-start(f32[2048,512]{1,0:T(8,128)} %copy-done.1) | copy-start | bytes 12582916
  (2 other events, 6.3 us)
Sparse Core Ops, SparseCore 0:
  9.8 83.4 all-gather.4
  94.8 79.5 all-gather.6

commit v3 on v2

--- a/solution.py
+++ b/solution.py
@@ -63,42 +63,72 @@
         from_low = swapped(to_low, 0)
         for bit in range(1, top):
             from_low = jnp.where(smaller == 1 << bit, swapped(to_low, bit), from_low)
-        return jnp.where(top_last, from_low, from_top), jnp.where(top_last, from_top, from_low)
+        return (
+            jnp.where(top_last, from_low, from_top),
+            jnp.where(top_last, from_top, from_low),
+            (to_top, to_low),
+        )
 
     def part(value, which):
         return lax.dynamic_slice_in_dim(value, which * half, half, 0)
+
+    def after(value, earlier):
+        return lax.optimization_barrier((value, earlier))[0]
+
+    def combined(weight, moment, which):
+        return 0.5 * part(weight, which).astype(f32) - step_size * pair_keep * part(moment, which)
 
     mine = ((lax.axis_index("rep") & plan[1]) > 0).astype(jnp.int32)
     other = 1 - mine
     rows0 = lax.all_gather(states[0, 0], "fsdp", axis=0, tiled=True)
     rows1 = lax.all_gather(states[1, 0], "fsdp", axis=0, tiled=True)
 
-    combined = 0.5 * weight.astype(f32) - step_size * pair_keep * moment
-    got_low_rows, got_moment = exchanged(combined[:half], part(moment, other))
-    got_high_rows, _ = exchanged(combined[half:], combined[half:])
-    pair_half = part(moment, mine) + got_moment.astype(f32)
+    got_other, got_moment, sent1 = exchanged(
+        combined(weight, moment, other), part(moment, other)
+    )
+    weight_b, moment_b = after((weight, moment), sent1)
+    combined_mine = combined(weight_b, moment_b, mine)
+    got_mine, _, sent2 = exchanged(combined_mine, combined_mine)
+    weight_c, moment_c = after((weight, moment), sent2)
 
     gradient0, factor0 = gradient_of(rows0, weight)
-    update0 = gradient0 * factor0
-    partner_combined = jnp.concatenate([got_low_rows, got_high_rows], 0).astype(f32)
-    weight1 = (combined + partner_combined - step_size * update0).astype(bf16)
+
+    def step0(weight, moment, gradient, got, which):
+        update = part(gradient, which) * factor0
+        new = combined(weight, moment, which) + got.astype(f32) - step_size * update
+        return new.astype(bf16), step_size * pair_keep * update
+
+    weight1_other, pull_other = step0(weight_c, moment_c, gradient0, got_other, other)
+    pair_half = part(moment_c, mine) + got_moment.astype(f32)
+    got_pair, got1_mine, sent3 = exchanged(
+        pair_half, 0.5 * weight1_other.astype(f32) - pull_other
+    )
+    got_mine, gradient0_d = after((got_mine, gradient0), sent3)
+    weight1_mine, pull_mine = step0(weight_c, moment_c, gradient0_d, got_mine, mine)
+    weight1 = jnp.zeros_like(weight)
+    weight1 = lax.dynamic_update_slice_in_dim(weight1, weight1_other, other * half, 0)
+    weight1 = lax.dynamic_update_slice_in_dim(weight1, weight1_mine, mine * half, 0)
     change0 = (weight1.astype(f32) - weight.astype(f32)).astype(bf16)
 
-    base = 0.5 * weight1.astype(f32) - step_size * pair_keep * update0
-    base_other = part(base, other)
-    got_pair, got_mine = exchanged(pair_half, base_other)
+    gradient1, factor1 = gradient_of(after(rows1, sent3), weight1)
+    got_pair, gradient1 = lax.optimization_barrier((got_pair, gradient1))
     all_half = pair_half + got_pair.astype(f32)
-    base_mine = part(base, mine) - step_size * pair_keep * pair_keep * all_half
-    sent_mine = base_mine.astype(bf16)
-    _, got_other = exchanged(sent_mine, sent_mine)
+    base_other = 0.5 * weight1_other.astype(f32) - step_size * pair_keep * factor0 * part(gradient0, other)
+    base_mine = (
+        0.5 * weight1_mine.astype(f32)
+        - step_size * pair_keep * factor0 * part(gradient0_d, mine)
+        - step_size * pair_keep * pair_keep * all_half
+    )
+    _, got1_other, sent4 = exchanged(base_mine, base_mine)
 
-    rows1, _ = lax.optimization_barrier((rows1, sent_mine))
-    gradient1, factor1 = gradient_of(rows1, weight1)
     changes = jnp.zeros((2, 1) + weight.shape, bf16)
     changes = lax.dynamic_update_slice(changes, change0[None, None], (0, 0, 0, 0))
-    for which, own, got in ((mine, base_mine, got_mine), (other, base_other, got_other)):
+    for which, now, own, got in (
+        (mine, weight1_mine, base_mine, got1_mine),
+        (other, weight1_other, base_other, got1_other),
+    ):
         new = (own + got.astype(f32) - step_size * (part(gradient1, which) * factor1)).astype(bf16)
-        change = (new.astype(f32) - part(weight1, which).astype(f32)).astype(bf16)
+        change = (new.astype(f32) - now.astype(f32)).astype(bf16)
         changes = lax.dynamic_update_slice(changes, change[None, None], (1, 0, which * half, 0))
     return changes
 

time: 288 us -> 273 us (0.948)
  waiting for transfers between devices: 135 us -> 124 us
  other arithmetic: 72.9 us -> 66.9 us
  matrix products: 25.6 us -> 29.1 us
  starting transfers between devices: 22.3 us -> 19.4 us
    ppermute x12, waiting for transfers between devices: 124 us -> 30.5 us  [swapped(): return lax.ppermute(value, 'rep', pairs)]
    all_gather x1, waiting for transfers between devices: 10.8 us -> 65.7 us  [local(): rows0 = lax.all_gather(states[0, 0], 'fsdp', axis=0, tiled=True)]
    all_gather x1, waiting for transfers between devices: 0.01 us -> 26.7 us  [local(): rows1 = lax.all_gather(states[1, 0], 'fsdp', axis=0, tiled=True)]
    sub x2 -> x0, other arithmetic: 15.1 us -> none  [the longest x1 9.14 us: local(): base = 0.5 * weight1.astype(f32) - step_size * pair_keep * update0]
    convert_element_type x1 -> x3, other arithmetic: 0.75 us -> 12.7 us  [exchanged(): to_top = jnp.where(top_last, second, first).astype(bf16)]
    dot_general x2, matrix products: 20.5 us -> 29.1 us  [gradient_of(): lax.dot_general(normed, residual, (((0,), (0,)), ((), ())), preferred_ele...]
    dynamic_update_slice x0 -> x1, other arithmetic: none -> 6.84 us  [local(): lax.dynamic_update_slice_in_dim(weight1, weight1_mine, mine * half, 0)]
    dot_general x1 -> x0, matrix products: 5.08 us -> none  [gradient_of(): jnp.dot(normed, weight, preferred_element_type=f32) * scale_in + column]
  transfers between devices with their start and end apart: 20 -> 20, of which waited for: 7 -> 6; matrix products, arithmetic and copies ran while one was open for 29% -> 37% of each run, Pallas kernels for 0% -> 0%
where the time goes in v3:
time: 273 us; the launch traced here: 272 us
  waiting for transfers between devices  124 us (45%)
  other arithmetic  66.9 us (25%)
  matrix products  29.1 us (11%)
  starting transfers between devices  19.4 us (7%)
  between operations  18.3 us (7%)
  local copies, waits for them, and re-layouts  14.9 us (5%)
    all_gather x1, waiting for transfers between devices, local(): rows0 = lax.all_gather(states[0, 0], 'fsdp', axis=0, tiled=True)  65.7 us
    ppermute x12, waiting for transfers between devices, swapped(): return lax.ppermute(value, 'rep', pairs)  30.5 us
    dot_general x2, matrix products, gradient_of(): lax.dot_general(normed, residual, (((0,), (0,)), ((), ())), preferred_ele...  29.1 us
    all_gather x1, waiting for transfers between devices, local(): rows1 = lax.all_gather(states[1, 0], 'fsdp', axis=0, tiled=True)  26.7 us
    convert_element_type x2, other arithmetic, exchanged(): to_low = jnp.where(top_last, first, second).astype(bf16)  13.9 us
    convert_element_type x3, other arithmetic, exchanged(): to_top = jnp.where(top_last, second, first).astype(bf16)  12.7 us
    dynamic_update_slice x2, other arithmetic, local(): lax.dynamic_update_slice(changes, change[None, None], (1, 0, which * half...  11.7 us
    ppermute x12, starting transfers between devices, swapped(): return lax.ppermute(value, 'rep', pairs)  11.4 us
  transfers between devices with their start and end apart: 20, of which 6 were waited for; matrix products, arithmetic and copies ran while one was open for 37% of the time, Pallas kernels for 0%

profile of v3, /device:TPU:0, one launch (start us, length us, event | category | flops | bytes accessed | tf_op | source)
XLA Modules:
  0.0 272.4 jit_solution(9267592641521803087)
XLA Ops:
  6.5 3.1 %fusion.67 = (bf16[1,1,128,4096]{3,2,1,0:T(8,128)(2,1)}, bf16[1,1,128,4096]{3,2,1,0:T(8,128)(2,1)}) fusion(bf16[2,1,128,4096]{3,2,1,0:T(8,128)(2,1)} %param.6), kind=kLoop, calls=%fused_computation.78 | loop fusion | bytes 4194304 | tf_op jit(solution)/shard_map/slice | solution.py:84
  12.4 6.0 %fusion.15 = (bf16[2048,512]{1,0:T(8,128)(2,1)}, bf16[2048,512]{1,0:T(8,128)(2,1)}) fusion(f32[1,4096,512]{2,1,0:T(8,128)} %param.5, s32[]{:T(128)S(6)} %select_n.106, pred[]{:T(512)S(6)} %gt.6, bf16[1,4096,512]{2,1,0:T(8,128)(2,1)} %param.4), kind=kLoop, calls=%fused_computation.32 | loop fusion | flops 8388608 | bytes 10485765 | tf_op jit(solution)/shard_map/convert_element_type | solution.py:61
  18.5 3.9 %subtract_convert_fusion.4 = bf16[2048,512]{1,0:T(8,128)(2,1)} fusion(f32[4096,512]{1,0:T(8,128)S(1)} %bitcast.80, s32[]{:T(128)S(6)} %mul.161, bf16[4096,512]{1,0:T(8,128)(2,1)} %bitcast.81), kind=kLoop, calls=%fused_computation.39 | loop fusion | flops 5242880 | bytes 8388612 | tf_op jit(solution)/shard_map/convert_element_type | solution.py:60
  22.4 3.0 %collective-permute-start.8 = (bf16[2048,512]{1,0:T(8,128)(2,1)}, bf16[2048,512]{1,0:T(8,128)(2,1)S(1)}, u32[]{:S(2)}, u32[]{:S(2)}) collective-permute-start(bf16[2048,512]{1,0:T(8,128)(2,1)} %subtract_convert_fusion.4), channel_id=1, source_target_pairs={{0,16},{4,20},{8,24},{12,28},{16,0},{20,4},{24,8},{28,12},{1,17},{... | collective-permute-start | bytes 6291464 | tf_op jit(solution)/shard_map/ppermute | solution.py:18
  25.5 2.0 collective-permute-start
  27.6 65.7 %all-gather.5.cloned.1.call-done = bf16[1,1,512,4096]{3,2,1,0:T(8,128)(2,1)} async-done(((bf16[1,1,128,4096]{3,2,1,0:T(8,128)(2,1)}), bf16[1,1,512,4096]{3,2,1,0:T(8,128)(2,1)}) %all-gather.5.cloned.1.call-update) | async-done | bytes 4194320 | tf_op jit(solution)/shard_map/all_gather | solution.py:83
  94.6 3.1 %fusion.2 = f32[512]{0:T(512)S(1)} fusion(bf16[1,1,512,4096]{3,2,1,0:T(8,128)(2,1)} %all-gather.5.cloned.1.call-done), kind=kLoop, calls=%fused_computation.6 | loop fusion | flops 6290944 | bytes 4196352 | tf_op jit(solution)/shard_map/reduce_sum | solution.py:23
  97.8 14.6 %multiply_reduce_fusion.1 = (f32[]{:T(128)}, f32[4096,512]{1,0:T(8,128)}) fusion(bf16[1,1,512,4096]{3,2,1,0:T(8,128)(2,1)} %all-gather.5.cloned.1.call-done, f32[512]{0:T(512)S(1)} %add_rsqrt_fusion.1, f32[511,512]{1,0:T(8,128)S(1)} %slice_bitcast_fusion, pred[512]{0:T(512)(128)(4,1)S(1)} %iota_compare_fusion, s32[]{:T(128)S(6)} %select_n.112, ...), kind=kOutput, calls=%fused_computation.10 | convolution fusion | flops 4315414528 | bytes 22549000 | tf_op jit(solution)/shard_map/dot_general | solution.py:45
  112.4 5.5 %collective-permute-done.6 = bf16[2048,512]{1,0:T(8,128)(2,1)} collective-permute-done((bf16[2048,512]{1,0:T(8,128)(2,1)}, bf16[2048,512]{1,0:T(8,128)(2,1)}, u32[]{:S(2)}, u32[]{:S(2)}) %collective-permute-start.6) | collective-permute-done | bytes 2097184 | tf_op jit(solution)/shard_map/ppermute | solution.py:18
  118.6 3.8 %collective-permute-start.5 = (f32[8,128]{1,0:T(8,128)S(1)}, f32[8,128]{1,0:T(8,128)S(1)}, u32[]{:S(2)}, u32[]{:S(2)}) collective-permute-start(f32[8,128]{1,0:T(8,128)S(1)} %broadcast_in_dim.44), channel_id=1, source_target_pairs={{0,3},{1,0},{2,1},{3,2},{4,7},{5,4},{6,5},{7,6},{8,11},{9,8},{10,9... | collective-permute-start | bytes 12296 | tf_op jit(solution)/shard_map/ppermute | solution.py:31
  124.9 3.8 %select_select_fusion = bf16[2048,512]{1,0:T(8,128)(2,1)} fusion(bf16[2048,512]{1,0:T(8,128)(2,1)S(1)} %collective-permute-done.8, bf16[2048,512]{1,0:T(8,128)(2,1)} %collective-permute-done.6, bf16[2048,512]{1,0:T(8,128)(2,1)} %collective-permute-done.7, pred[]{:T(512)S(6)} %eq.2, pred[]{:T(512)S(6)} %gt.6), kind=kLoop, calls=%fused_computation.44 | loop fusion | flops 2097152 | bytes 8388610 | tf_op jit(solution)/shard_map/jit(_where)/select_n | solution.py:67
  131.6 7.9 %select_convert_fusion = (bf16[2048,512]{1,0:T(8,128)(2,1)}, f32[2048,512]{1,0:T(8,128)S(1)}, bf16[2048,512]{1,0:T(8,128)(2,1)S(1)}) fusion(pred[]{:T(512)S(6)} %gt.6, f32[]{:T(128)} %bitcast.10, f32[4096,512]{1,0:T(8,128)S(1)} %copy-done, s32[]{:T(128)S(6)} %select_n.106, bf16[2048,512]{1,0:T(8,128)(2,1)} %collective-permute-done.2, ...), kind=kLoop, calls=%fused_computation.35 | loop fusion | flops 20971520 | bytes 29360142 | tf_op jit(solution)/shard_map/convert_element_type | solution.py:61
  139.5 1.6 collective-permute-start.9
  141.3 2.9 %select_convert_fusion.1 = (bf16[2048,512]{1,0:T(8,128)(2,1)}, bf16[4096,512]{1,0:T(8,128)(2,1)S(1)}) fusion(f32[2048,512]{1,0:T(8,128)S(1)} %get-tuple-element.26, pred[]{:T(512)S(6)} %gt.6, f32[]{:T(128)} %bitcast.10, f32[4096,512]{1,0:T(8,128)S(1)} %copy-done, s32[]{:T(128)S(6)} %select_n.106, bf16[2048,512]{1,0:T(8,128)(2,1)S(1)} %get-tuple-element.27, ...), kind=kLoop, calls=%fused_computation.36 | loop fusion | flops 6291456 | bytes 14680073 | tf_op jit(solution)/shard_map/convert_element_type | solution.py:60
  144.2 2.0 copy-done.10
  146.2 1.6 collective-permute-start.11
  147.8 26.7 %all-gather.7.cloned.1.call-done = bf16[1,1,512,4096]{3,2,1,0:T(8,128)(2,1)} async-done(((bf16[1,1,128,4096]{3,2,1,0:T(8,128)(2,1)}), bf16[1,1,512,4096]{3,2,1,0:T(8,128)(2,1)}) %all-gather.7.cloned.1.call-update) | async-done | bytes 4194320 | tf_op jit(solution)/shard_map/all_gather | solution.py:84
  174.5 3.2 %fusion = f32[512]{0:T(512)S(1)} fusion(bf16[512,4096]{1,0:T(8,128)(2,1)} %bitcast.84), kind=kLoop, calls=%fused_computation.4 | loop fusion | flops 6290944 | bytes 4196352 | tf_op jit(solution)/shard_map/reduce_sum | solution.py:23
  177.7 1.2 dynamic-slice_convert_fusion.1
  179.0 6.8 %constant_dynamic-update-slice_fusion = (bf16[4096,512]{1,0:T(8,128)(2,1)}, bf16[2048,512]{1,0:T(8,128)(2,1)S(1)}) fusion(bf16[4096,512]{1,0:T(8,128)(2,1)} %copy-done.10, s32[]{:T(128)S(6)} %mul.161, f32[]{:T(128)} %bitcast.10, f32[4096,512]{1,0:T(8,128)} %get-tuple-element.19, bf16[2048,512]{1,0:T(8,128)(2,1)} %select_select_fusion, ...), kind=kLoop, calls=%fused_computation.65 | loop fusion | flops 10485760 | bytes 16777732 | tf_op jit(solution)/shard_map/dynamic_update_slice | solution.py:110
  185.9 14.5 %multiply_reduce_fusion = (f32[]{:T(128)}, f32[4096,512]{1,0:T(8,128)}) fusion(bf16[4096,512]{1,0:T(8,128)(2,1)} %get-tuple-element.23, bf16[512,4096]{1,0:T(8,128)(2,1)} %bitcast.86, f32[512]{0:T(512)S(1)} %add_rsqrt_fusion, f32[511,512]{1,0:T(8,128)S(1)} %slice.37, pred[512]{0:T(512)(128)(4,1)S(1)} %iota_compare_fusion, s32[]{:T(128)S(6)} %select_n.112), kind=kOutput, calls=%fused_computation.8 | convolution fusion | flops 4315414528 | bytes 22549000 | tf_op jit(solution)/shard_map/dot_general | solution.py:45
  202.0 1.9 collective-permute-start.12
  203.9 2.5 broadcast_select_fusion.2
  206.5 5.9 %fusion.66 = bf16[2048,512]{1,0:T(8,128)(2,1)} fusion(f32[2048,512]{1,0:T(8,128)S(1)} %copy-done.2, bf16[2048,512]{1,0:T(8,128)(2,1)S(1)} %broadcast_select_fusion.2, f32[4096,512]{1,0:T(8,128)} %get-tuple-element.19, s32[]{:T(128)S(6)} %mul.161, f32[]{:T(128)S(6)} %mul.183, bf16[2048,512]{1,0:T(8,128)(2,1)S(1)} %get-tuple-element.24), kind=kLoop, calls=%fused_computation.77 | loop fusion | flops 9437184 | bytes 14680072 | tf_op jit(solution)/shard_map/convert_element_type | solution.py:60
  212.4 1.4 collective-permute-start.15
  213.8 1.5 collective-permute-start.16
  215.3 5.6 %fusion.13 = bf16[1,1,4096,512]{3,2,1,0:T(8,128)(2,1)} fusion(bf16[4096,512]{1,0:T(8,128)(2,1)} %get-tuple-element.23, bf16[1,4096,512]{2,1,0:T(8,128)(2,1)S(1)} %copy-done.5), kind=kLoop, calls=%fused_computation.26 | loop fusion | flops 8388608 | bytes 12582912 | tf_op jit(solution)/shard_map/broadcast_in_dim | solution.py:125
  220.9 6.3 %dynamic_update_slice.17 = bf16[2,1,4096,512]{3,2,1,0:T(8,128)(2,1)} pad(bf16[1,1,4096,512]{3,2,1,0:T(8,128)(2,1)} %fusion.13, bf16[]{:T(256)} %constant.21.clone.1), padding=0_1x0_0x0_0x0_0 | pad | bytes 12582914 | tf_op jit(solution)/shard_map/dynamic_update_slice | solution.py:125
  228.9 6.5 %fusion.17 = bf16[2,1,4096,512]{3,2,1,0:T(8,128)(2,1)} fusion(bf16[2,1,4096,512]{3,2,1,0:T(8,128)(2,1)} %dynamic_update_slice.17, s32[]{:T(128)S(6)} %mul.161, bf16[2048,512]{1,0:T(8,128)(2,1)} %copy-done.6, f32[4096,512]{1,0:T(8,128)} %get-tuple-element.22, f32[]{:T(128)} %bitcast.13, bf16[2048,512]{1,0:T(8,128)(2,1)} %collective-permute-done.11, ...), kind=kLoop, calls=%fused_computation.42 | loop fusion | flops 19922944 | bytes 25166346 | tf_op jit(solution)/shard_map/dynamic_update_slice | solution.py:132
  235.5 23.8 %collective-permute-done.15 = bf16[2048,512]{1,0:T(8,128)(2,1)} collective-permute-done((bf16[2048,512]{1,0:T(8,128)(2,1)}, bf16[2048,512]{1,0:T(8,128)(2,1)}, u32[]{:S(2)}, u32[]{:S(2)}) %collective-permute-start.15) | collective-permute-done | bytes 2097184 | tf_op jit(solution)/shard_map/ppermute | solution.py:18
  259.3 1.2 collective-permute-done.16
  260.5 5.1 %bitcast_dynamic-update-slice_fusion = bf16[2,1,4096,512]{3,2,1,0:T(8,128)(2,1)} fusion(bf16[2,1,4096,512]{3,2,1,0:T(8,128)(2,1)} %fusion.17, s32[]{:T(128)S(6)} %select_n.106, f32[4096,512]{1,0:T(8,128)} %get-tuple-element.22, bf16[2048,512]{1,0:T(8,128)(2,1)} %collective-permute-done.15, f32[4096,512]{1,0:T(8,128)S(1)} %bitcast.77, ...), kind=kLoop, calls=%fused_computation.43 | loop fusion | flops 15728640 | bytes 18874890 | tf_op jit(solution)/shard_map/dynamic_update_slice | solution.py:132
  (71 shorter events, 9.3 us)
Async XLA Ops:
  6.5 86.8 %all-gather.5.cloned.1.call-start = ((), (), s32[]{:S(2)}) async-start(), calls=%async_computation | async-start | bytes 5242880 | tf_op jit(solution)/shard_map/all_gather | solution.py:83
  9.7 164.8 %all-gather.7.cloned.1.call-start = ((), (), s32[]{:S(2)}) async-start(), calls=%async_computation.1 | async-start | bytes 5242880 | tf_op jit(solution)/shard_map/all_gather | solution.py:84
  12.4 6.0 %copy-start.3 = (f32[1,4096,512]{2,1,0:T(8,128)S(1)}, f32[1,4096,512]{2,1,0:T(8,128)}, u32[]{:S(2)}) copy-start(f32[1,4096,512]{2,1,0:T(8,128)} %param.5) | copy-start | bytes 25165828
  22.4 75.3 %collective-permute-start.8 = (bf16[2048,512]{1,0:T(8,128)(2,1)}, bf16[2048,512]{1,0:T(8,128)(2,1)S(1)}, u32[]{:S(2)}, u32[]{:S(2)}) collective-permute-start(bf16[2048,512]{1,0:T(8,128)(2,1)} %subtract_convert_fusion.4), channel_id=1, source_target_pairs={{0,16},{4,20},{8,24},{12,28},{16,0},{20,4},{24,8},{28,12},{1,17},{... | collective-permute-start | bytes 6291464 | tf_op jit(solution)/shard_map/ppermute | solution.py:18
  25.4 106.1 %collective-permute-start.2 = (bf16[2048,512]{1,0:T(8,128)(2,1)}, bf16[2048,512]{1,0:T(8,128)(2,1)}, u32[]{:S(2)}, u32[]{:S(2)}) collective-permute-start(bf16[2048,512]{1,0:T(8,128)(2,1)} %get-tuple-element.29), channel_id=1, source_target_pairs={{0,16},{4,20},{8,24},{12,28},{16,0},{20,4},{24,8},{28,12},{1,17},{... | collective-permute-start | bytes 6291464 | tf_op jit(solution)/shard_map/ppermute | solution.py:18
  25.5 106.0 %collective-permute-start = (bf16[2048,512]{1,0:T(8,128)(2,1)}, bf16[2048,512]{1,0:T(8,128)(2,1)}, u32[]{:S(2)}, u32[]{:S(2)}) collective-permute-start(bf16[2048,512]{1,0:T(8,128)(2,1)} %get-tuple-element.28), channel_id=1, source_target_pairs={{0,8},{4,12},{8,0},{12,4},{16,24},{20,28},{24,16},{28,20},{1,9},{5... | collective-permute-start | bytes 6291464 | tf_op jit(solution)/shard_map/ppermute | solution.py:18
  27.5 90.4 %collective-permute-start.6 = (bf16[2048,512]{1,0:T(8,128)(2,1)}, bf16[2048,512]{1,0:T(8,128)(2,1)}, u32[]{:S(2)}, u32[]{:S(2)}) collective-permute-start(bf16[2048,512]{1,0:T(8,128)(2,1)} %subtract_convert_fusion.4), channel_id=1, source_target_pairs={{0,8},{4,12},{8,0},{12,4},{16,24},{20,28},{24,16},{28,20},{1,9},{5... | collective-permute-start | bytes 6291464 | tf_op jit(solution)/shard_map/ppermute | solution.py:18
  27.6 96.1 %collective-permute-start.7 = (bf16[2048,512]{1,0:T(8,128)(2,1)}, bf16[2048,512]{1,0:T(8,128)(2,1)}, u32[]{:S(2)}, u32[]{:S(2)}) collective-permute-start(bf16[2048,512]{1,0:T(8,128)(2,1)} %subtract_convert_fusion.4), channel_id=1, source_target_pairs={{0,4},{4,0},{8,12},{12,8},{16,20},{20,16},{24,28},{28,24},{1,5},{5... | collective-permute-start | bytes 6291464 | tf_op jit(solution)/shard_map/ppermute | solution.py:18
  97.7 33.8 %collective-permute-start.1 = (bf16[2048,512]{1,0:T(8,128)(2,1)}, bf16[2048,512]{1,0:T(8,128)(2,1)}, u32[]{:S(2)}, u32[]{:S(2)}) collective-permute-start(bf16[2048,512]{1,0:T(8,128)(2,1)} %get-tuple-element.28), channel_id=1, source_target_pairs={{0,4},{4,0},{8,12},{12,8},{16,20},{20,16},{24,28},{28,24},{1,5},{5... | collective-permute-start | bytes 6291464 | tf_op jit(solution)/shard_map/ppermute | solution.py:18
  118.6 5.2 %collective-permute-start.5 = (f32[8,128]{1,0:T(8,128)S(1)}, f32[8,128]{1,0:T(8,128)S(1)}, u32[]{:S(2)}, u32[]{:S(2)}) collective-permute-start(f32[8,128]{1,0:T(8,128)S(1)} %broadcast_in_dim.44), channel_id=1, source_target_pairs={{0,3},{1,0},{2,1},{3,2},{4,7},{5,4},{6,5},{7,6},{8,11},{9,8},{10,9... | collective-permute-start | bytes 12296 | tf_op jit(solution)/shard_map/ppermute | solution.py:31
  123.7 7.9 %copy-start = (f32[4096,512]{1,0:T(8,128)S(1)}, f32[4096,512]{1,0:T(8,128)}, u32[]{:S(2)}) copy-start(f32[4096,512]{1,0:T(8,128)} %get-tuple-element.19) | copy-start | bytes 25165828
  123.7 5.1 %collective-permute-start.4 = (f32[8,128]{1,0:T(8,128)S(1)}, f32[8,128]{1,0:T(8,128)S(1)}, u32[]{:S(2)}, u32[]{:S(2)}) collective-permute-start(f32[8,128]{1,0:T(8,128)S(1)} %broadcast_in_dim.44), channel_id=1, source_target_pairs={{0,2},{1,3},{2,0},{3,1},{4,6},{5,7},{6,4},{7,5},{8,10},{9,11},{10,... | collective-permute-start | bytes 12296 | tf_op jit(solution)/shard_map/ppermute | solution.py:31
  123.8 5.9 %collective-permute-start.3 = (f32[8,128]{1,0:T(8,128)S(1)}, f32[8,128]{1,0:T(8,128)S(1)}, u32[]{:S(2)}, u32[]{:S(2)}) collective-permute-start(f32[8,128]{1,0:T(8,128)S(1)} %broadcast_in_dim.44), channel_id=1, source_target_pairs={{0,1},{1,2},{2,3},{3,0},{4,5},{5,6},{6,7},{7,4},{8,9},{9,10},{10,1... | collective-permute-start | bytes 12296 | tf_op jit(solution)/shard_map/ppermute | solution.py:31
  139.5 4.7 %copy-start.1 = (f32[2048,512]{1,0:T(8,128)}, f32[2048,512]{1,0:T(8,128)S(1)}, u32[]{:S(2)}) copy-start(f32[2048,512]{1,0:T(8,128)S(1)} %get-tuple-element.26) | copy-start | bytes 12582916
  139.5 4.8 %copy-start.8 = (bf16[2048,512]{1,0:T(8,128)(2,1)}, bf16[2048,512]{1,0:T(8,128)(2,1)S(1)}, u32[]{:S(2)}) copy-start(bf16[2048,512]{1,0:T(8,128)(2,1)S(1)} %get-tuple-element.27) | copy-start | bytes 6291460
  139.5 64.5 %collective-permute-start.9 = (bf16[2048,512]{1,0:T(8,128)(2,1)}, bf16[2048,512]{1,0:T(8,128)(2,1)}, u32[]{:S(2)}, u32[]{:S(2)}) collective-permute-start(bf16[2048,512]{1,0:T(8,128)(2,1)} %get-tuple-element.25), channel_id=1, source_target_pairs={{0,8},{4,12},{8,0},{12,4},{16,24},{20,28},{24,16},{28,20},{1,9},{5... | collective-permute-start | bytes 6291464 | tf_op jit(solution)/shard_map/ppermute | solution.py:18
  141.1 62.9 %collective-permute-start.10 = (bf16[2048,512]{1,0:T(8,128)(2,1)}, bf16[2048,512]{1,0:T(8,128)(2,1)}, u32[]{:S(2)}, u32[]{:S(2)}) collective-permute-start(bf16[2048,512]{1,0:T(8,128)(2,1)} %get-tuple-element.25), channel_id=1, source_target_pairs={{0,4},{4,0},{8,12},{12,8},{16,20},{20,16},{24,28},{28,24},{1,5},{5... | collective-permute-start | bytes 6291464 | tf_op jit(solution)/shard_map/ppermute | solution.py:18
  146.2 55.8 %collective-permute-start.11 = (bf16[2048,512]{1,0:T(8,128)(2,1)}, bf16[2048,512]{1,0:T(8,128)(2,1)}, u32[]{:S(2)}, u32[]{:S(2)}) collective-permute-start(bf16[2048,512]{1,0:T(8,128)(2,1)} %get-tuple-element.32), channel_id=1, source_target_pairs={{0,16},{4,20},{8,24},{12,28},{16,0},{20,4},{24,8},{28,12},{1,17},{... | collective-permute-start | bytes 6291464 | tf_op jit(solution)/shard_map/ppermute | solution.py:18
  174.5 4.5 %copy-start.4 = (bf16[1,4096,512]{2,1,0:T(8,128)(2,1)S(1)}, bf16[1,4096,512]{2,1,0:T(8,128)(2,1)}, u32[]{:S(2)}) copy-start(bf16[1,4096,512]{2,1,0:T(8,128)(2,1)} %param.4) | copy-start | bytes 12582916
  185.9 20.6 %copy-start.6 = (bf16[2048,512]{1,0:T(8,128)(2,1)}, bf16[2048,512]{1,0:T(8,128)(2,1)S(1)}, u32[]{:S(2)}) copy-start(bf16[2048,512]{1,0:T(8,128)(2,1)S(1)} %get-tuple-element.24) | copy-start | bytes 6291460
  200.9 14.4 %collective-permute-start.14 = (f32[8,128]{1,0:T(8,128)S(1)}, f32[8,128]{1,0:T(8,128)S(1)}, u32[]{:S(2)}, u32[]{:S(2)}) collective-permute-start(f32[8,128]{1,0:T(8,128)S(1)} %broadcast_in_dim.46), channel_id=1, source_target_pairs={{0,3},{1,0},{2,1},{3,2},{4,7},{5,4},{6,5},{7,6},{8,11},{9,8},{10,9... | collective-permute-start | bytes 12296 | tf_op jit(solution)/shard_map/ppermute | solution.py:31
  201.6 25.6 %collective-permute-start.13 = (f32[8,128]{1,0:T(8,128)S(1)}, f32[8,128]{1,0:T(8,128)S(1)}, u32[]{:S(2)}, u32[]{:S(2)}) collective-permute-start(f32[8,128]{1,0:T(8,128)S(1)} %broadcast_in_dim.46), channel_id=1, source_target_pairs={{0,2},{1,3},{2,0},{3,1},{4,6},{5,7},{6,4},{7,5},{8,10},{9,11},{10,... | collective-permute-start | bytes 12296 | tf_op jit(solution)/shard_map/ppermute | solution.py:31
  202.0 4.5 %copy-start.2 = (f32[2048,512]{1,0:T(8,128)S(1)}, f32[2048,512]{1,0:T(8,128)}, u32[]{:S(2)}) copy-start(f32[2048,512]{1,0:T(8,128)} %copy-done.1) | copy-start | bytes 12582916
  202.0 25.2 %collective-permute-start.12 = (f32[8,128]{1,0:T(8,128)S(1)}, f32[8,128]{1,0:T(8,128)S(1)}, u32[]{:S(2)}, u32[]{:S(2)}) collective-permute-start(f32[8,128]{1,0:T(8,128)S(1)} %broadcast_in_dim.46), channel_id=1, source_target_pairs={{0,1},{1,2},{2,3},{3,0},{4,5},{5,6},{6,7},{7,4},{8,9},{9,10},{10,1... | collective-permute-start | bytes 12296 | tf_op jit(solution)/shard_map/ppermute | solution.py:31
  206.4 6.0 %copy-start.7 = (bf16[2048,512]{1,0:T(8,128)(2,1)}, bf16[2048,512]{1,0:T(8,128)(2,1)S(1)}, u32[]{:S(2)}) copy-start(bf16[2048,512]{1,0:T(8,128)(2,1)S(1)} %broadcast_select_fusion.2) | copy-start | bytes 6291460
  206.5 8.8 %copy-start.5 = (bf16[1,4096,512]{2,1,0:T(8,128)(2,1)S(1)}, bf16[1,4096,512]{2,1,0:T(8,128)(2,1)}, u32[]{:S(2)}) copy-start(bf16[1,4096,512]{2,1,0:T(8,128)(2,1)} %param.4) | copy-start | bytes 12582916
  212.4 46.9 %collective-permute-start.15 = (bf16[2048,512]{1,0:T(8,128)(2,1)}, bf16[2048,512]{1,0:T(8,128)(2,1)}, u32[]{:S(2)}, u32[]{:S(2)}) collective-permute-start(bf16[2048,512]{1,0:T(8,128)(2,1)} %fusion.66), channel_id=1, source_target_pairs={{0,16},{4,20},{8,24},{12,28},{16,0},{20,4},{24,8},{28,12},{1,17},{... | collective-permute-start | bytes 6291464 | tf_op jit(solution)/shard_map/ppermute | solution.py:18
  213.8 46.6 %collective-permute-start.16 = (bf16[2048,512]{1,0:T(8,128)(2,1)}, bf16[2048,512]{1,0:T(8,128)(2,1)}, u32[]{:S(2)}, u32[]{:S(2)}) collective-permute-start(bf16[2048,512]{1,0:T(8,128)(2,1)} %fusion.66), channel_id=1, source_target_pairs={{0,8},{4,12},{8,0},{12,4},{16,24},{20,28},{24,16},{28,20},{1,9},{5... | collective-permute-start | bytes 6291464 | tf_op jit(solution)/shard_map/ppermute | solution.py:18
  215.3 45.2 %collective-permute-start.17 = (bf16[2048,512]{1,0:T(8,128)(2,1)}, bf16[2048,512]{1,0:T(8,128)(2,1)}, u32[]{:S(2)}, u32[]{:S(2)}) collective-permute-start(bf16[2048,512]{1,0:T(8,128)(2,1)} %fusion.66), channel_id=1, source_target_pairs={{0,4},{4,0},{8,12},{12,8},{16,20},{20,16},{24,28},{28,24},{1,5},{5... | collective-permute-start | bytes 6291464 | tf_op jit(solution)/shard_map/ppermute | solution.py:18
  215.3 13.6 %slice-start = ((s8[8388608]{0:T(1024)(128)(4,1)}), s8[4194304]{0:T(1024)(128)(4,1)S(1)}, s32[]{:S(2)}) async-start(s8[8388608]{0:T(1024)(128)(4,1)} %bitcast.76), calls=%async_computation.2 | async-start | bytes 8388608
  220.9 8.0 %slice-start.1 = ((s8[8388608]{0:T(1024)(128)(4,1)}), s8[4194304]{0:T(1024)(128)(4,1)S(1)}, s32[]{:S(2)}) async-start(s8[8388608]{0:T(1024)(128)(4,1)} %bitcast.76), calls=%async_computation.3 | async-start | bytes 8388608
  228.9 31.5 %copy-start.9 = (bf16[2048,512]{1,0:T(8,128)(2,1)S(1)}, bf16[2048,512]{1,0:T(8,128)(2,1)}, u32[]{:S(2)}) copy-start(bf16[2048,512]{1,0:T(8,128)(2,1)} %copy-done.8) | copy-start | bytes 6291460
  (2 other events, 5.2 us)
Sparse Core Ops, SparseCore 0:
  9.8 83.4 all-gather.4
  94.9 79.5 all-gather.6

commit v4 on v3

--- a/solution.py
+++ b/solution.py
@@ -83,13 +83,13 @@
     rows0 = lax.all_gather(states[0, 0], "fsdp", axis=0, tiled=True)
     rows1 = lax.all_gather(states[1, 0], "fsdp", axis=0, tiled=True)
 
-    got_other, got_moment, sent1 = exchanged(
-        combined(weight, moment, other), part(moment, other)
+    mine_combined = combined(weight, moment, mine)
+    got_first, got_second, sent1 = exchanged(
+        jnp.stack([combined(weight, moment, other), mine_combined]),
+        jnp.stack([part(moment, other), mine_combined]),
     )
-    weight_b, moment_b = after((weight, moment), sent1)
-    combined_mine = combined(weight_b, moment_b, mine)
-    got_mine, _, sent2 = exchanged(combined_mine, combined_mine)
-    weight_c, moment_c = after((weight, moment), sent2)
+    got_other, got_mine, got_moment = got_first[0], got_first[1], got_second[0]
+    weight_c, moment_c, rows0 = after((weight, moment, rows0), sent1)
 
     gradient0, factor0 = gradient_of(rows0, weight)
 
@@ -103,15 +103,14 @@
     got_pair, got1_mine, sent3 = exchanged(
         pair_half, 0.5 * weight1_other.astype(f32) - pull_other
     )
-    got_mine, gradient0_d = after((got_mine, gradient0), sent3)
+    gradient0_d = after(gradient0, sent3)
     weight1_mine, pull_mine = step0(weight_c, moment_c, gradient0_d, got_mine, mine)
     weight1 = jnp.zeros_like(weight)
     weight1 = lax.dynamic_update_slice_in_dim(weight1, weight1_other, other * half, 0)
     weight1 = lax.dynamic_update_slice_in_dim(weight1, weight1_mine, mine * half, 0)
     change0 = (weight1.astype(f32) - weight.astype(f32)).astype(bf16)
 
-    gradient1, factor1 = gradient_of(after(rows1, sent3), weight1)
-    got_pair, gradient1 = lax.optimization_barrier((got_pair, gradient1))
+    got_pair, change0, rows1 = lax.optimization_barrier((got_pair, change0, rows1))
     all_half = pair_half + got_pair.astype(f32)
     base_other = 0.5 * weight1_other.astype(f32) - step_size * pair_keep * factor0 * part(gradient0, other)
     base_mine = (
@@ -121,6 +120,7 @@
     )
     _, got1_other, sent4 = exchanged(base_mine, base_mine)
 
+    gradient1, factor1 = gradient_of(rows1, after(weight1, sent4))
     changes = jnp.zeros((2, 1) + weight.shape, bf16)
     changes = lax.dynamic_update_slice(changes, change0[None, None], (0, 0, 0, 0))
     for which, now, own, got in (

time: 273 us -> 263 us (0.963)
  waiting for transfers between devices: 124 us -> 108 us
  other arithmetic: 66.9 us -> 75.3 us
  starting transfers between devices: 19.4 us -> 15.6 us
    all_gather x1, waiting for transfers between devices: 26.7 us -> 0.01 us  [local(): rows1 = lax.all_gather(states[1, 0], 'fsdp', axis=0, tiled=True)]
    ppermute x12 -> x9, waiting for transfers between devices: 30.5 us -> 41 us  [swapped(): return lax.ppermute(value, 'rep', pairs)]
    sub x0 -> x1, other arithmetic: none -> 7.6 us  [combined(): 0.5 * part(weight, which).astype(f32)]
    convert_element_type x2, other arithmetic: 13.9 us -> 8.01 us  [exchanged(): to_low = jnp.where(top_last, first, second).astype(bf16)]
    broadcast_in_dim x1 -> x0, other arithmetic: 5.59 us -> none  [local(): change0[None, None]]
    convert_element_type x0 -> x1, other arithmetic: none -> 5.38 us  [local(): change0 = (weight1.astype(f32) - weight.astype(f32)).astype(bf16)]
    dynamic_update_slice x0 -> x1, other arithmetic: none -> 5.1 us  [local(): lax.dynamic_update_slice_in_dim(weight1, weight1_other, other * half, 0)]
    convert_element_type x3 -> x2, other arithmetic: 12.7 us -> 9.09 us  [exchanged(): to_top = jnp.where(top_last, second, first).astype(bf16)]
  transfers between devices with their start and end apart: 20 -> 17, of which waited for: 6 -> 7; matrix products, arithmetic and copies ran while one was open for 37% -> 39% of each run, Pallas kernels for 0% -> 0%
where the time goes in v4:
time: 263 us
  waiting for transfers between devices  108 us (41%)
  other arithmetic  75.3 us (29%)
  matrix products  29.1 us (11%)
  between operations  18.4 us (7%)
  local copies, waits for them, and re-layouts  16.9 us (6%)
  starting transfers between devices  15.6 us (6%)
    all_gather x1, waiting for transfers between devices, local(): rows0 = lax.all_gather(states[0, 0], 'fsdp', axis=0, tiled=True)  63.6 us
    ppermute x9, waiting for transfers between devices, swapped(): return lax.ppermute(value, 'rep', pairs)  41 us
    dot_general x2, matrix products, gradient_of(): lax.dot_general(normed, residual, (((0,), (0,)), ((), ())), preferred_ele...  29.1 us
    dynamic_update_slice x2, other arithmetic, local(): lax.dynamic_update_slice(changes, change[None, None], (1, 0, which * half...  11.8 us
    select_n x2, other arithmetic, exchanged(): jnp.where(top_last, from_low, from_top)  9.72 us
    ppermute x9, starting transfers between devices, swapped(): return lax.ppermute(value, 'rep', pairs)  9.63 us
    convert_element_type x2, other arithmetic, exchanged(): to_top = jnp.where(top_last, second, first).astype(bf16)  9.09 us
    dynamic_update_slice x1, other arithmetic, local(): lax.dynamic_update_slice_in_dim(weight1, weight1_mine, mine * half, 0)  8.37 us
  transfers between devices with their start and end apart: 17, of which 7 were waited for; matrix products, arithmetic and copies ran while one was open for 39% of the time, Pallas kernels for 0%

profile of v4, /device:TPU:0, one launch (start us, length us, event | category | flops | bytes accessed | tf_op | source)
XLA Modules:
  0.0 263.0 jit_solution(6816401320042596338)
XLA Ops:
  6.5 3.1 %fusion.71 = (bf16[1,1,128,4096]{3,2,1,0:T(8,128)(2,1)}, bf16[1,1,128,4096]{3,2,1,0:T(8,128)(2,1)}) fusion(bf16[2,1,128,4096]{3,2,1,0:T(8,128)(2,1)} %param.6), kind=kLoop, calls=%fused_computation.83 | loop fusion | bytes 4194304 | tf_op jit(solution)/shard_map/slice | solution.py:84
  12.4 7.6 %multiply_subtract_fusion = (bf16[1,2048,512]{2,1,0:T(8,128)(2,1)S(1)}, bf16[1,2048,512]{2,1,0:T(8,128)(2,1)S(1)}, bf16[1,2048,512]{2,1,0:T(8,128)(2,1)S(1)}) fusion(bf16[1,4096,512]{2,1,0:T(8,128)(2,1)} %param.4, s32[]{:T(128)S(6)} %select_n.104, f32[1,4096,512]{2,1,0:T(8,128)} %param.5, s32[]{:T(128)S(6)} %mul.159), kind=kLoop, calls=%fused_computation.40 | loop fusion | flops 10485760 | bytes 20971528 | tf_op jit(solution)/shard_map/sub | solution.py:79
  20.0 3.7 %select_convert_fusion = (bf16[2,2048,512]{2,1,0:T(8,128)(2,1)}, bf16[2,2048,512]{2,1,0:T(8,128)(2,1)}) fusion(bf16[1,2048,512]{2,1,0:T(8,128)(2,1)S(1)} %get-tuple-element.30, bf16[1,2048,512]{2,1,0:T(8,128)(2,1)S(1)} %get-tuple-element.31, bf16[1,2048,512]{2,1,0:T(8,128)(2,1)S(1)} %get-tuple-element.29, pred[]{:T(512)S(6)} %gt.6), kind=kLoop, calls=%fused_computation.13 | loop fusion | flops 8388608 | bytes 14680065 | tf_op jit(solution)/shard_map/convert_element_type | solution.py:61
  23.7 3.1 %collective-permute-start = (bf16[2,2048,512]{2,1,0:T(8,128)(2,1)}, bf16[2,2048,512]{2,1,0:T(8,128)(2,1)}, u32[]{:S(2)}, u32[]{:S(2)}) collective-permute-start(bf16[2,2048,512]{2,1,0:T(8,128)(2,1)} %get-tuple-element.33), channel_id=1, source_target_pairs={{0,16},{4,20},{8,24},{12,28},{16,0},{20,4},{24,8},{28,12},{1,17},{... | collective-permute-start | bytes 12582920 | tf_op jit(solution)/shard_map/ppermute | solution.py:18
  26.8 1.5 collective-permute-start.1
  29.7 63.6 %all-gather.5.cloned.1.call-done = bf16[1,1,512,4096]{3,2,1,0:T(8,128)(2,1)} async-done(((bf16[1,1,128,4096]{3,2,1,0:T(8,128)(2,1)}), bf16[1,1,512,4096]{3,2,1,0:T(8,128)(2,1)}) %all-gather.5.cloned.1.call-update) | async-done | bytes 4194320 | tf_op jit(solution)/shard_map/all_gather | solution.py:83
  94.6 3.1 %fusion = f32[512]{0:T(512)S(1)} fusion(bf16[512,4096]{1,0:T(8,128)(2,1)} %bitcast.56), kind=kLoop, calls=%fused_computation.6 | loop fusion | flops 6290944 | bytes 4196352 | tf_op jit(solution)/shard_map/reduce_sum | solution.py:23
  97.7 14.6 %multiply_reduce_fusion.1 = (f32[]{:T(128)}, f32[4096,512]{1,0:T(8,128)}) fusion(bf16[512,4096]{1,0:T(8,128)(2,1)} %bitcast.57, f32[512]{0:T(512)S(1)} %add_rsqrt_fusion.1, f32[511,512]{1,0:T(8,128)S(1)} %slice.50, pred[512]{0:T(512)(128)(4,1)S(1)} %iota_compare_fusion, s32[]{:T(128)S(6)} %select_n.111, bf16[1,4096,512]{2,1,0:T(8,128)(2,1)} %param.4), kind=kOutput, calls=%fused_computation.12 | convolution fusion | flops 4315414528 | bytes 22549000 | tf_op jit(solution)/shard_map/dot_general | solution.py:45
  113.7 4.0 %collective-permute-done = bf16[2,2048,512]{2,1,0:T(8,128)(2,1)} collective-permute-done((bf16[2,2048,512]{2,1,0:T(8,128)(2,1)}, bf16[2,2048,512]{2,1,0:T(8,128)(2,1)}, u32[]{:S(2)}, u32[]{:S(2)}) %collective-permute-start) | collective-permute-done | bytes 4194336 | tf_op jit(solution)/shard_map/ppermute | solution.py:18
  117.6 3.9 %collective-permute-start.5 = (f32[8,128]{1,0:T(8,128)S(1)}, f32[8,128]{1,0:T(8,128)S(1)}, u32[]{:S(2)}, u32[]{:S(2)}) collective-permute-start(f32[8,128]{1,0:T(8,128)S(1)} %broadcast_in_dim.43), channel_id=1, source_target_pairs={{0,3},{1,0},{2,1},{3,2},{4,7},{5,4},{6,5},{7,6},{8,11},{9,8},{10,9... | collective-permute-start | bytes 12296 | tf_op jit(solution)/shard_map/ppermute | solution.py:31
  121.5 5.9 %broadcast_select_fusion.1 = (bf16[2,2048,512]{2,1,0:T(8,128)(2,1)}, bf16[2,2048,512]{2,1,0:T(8,128)(2,1)}) fusion(bf16[2,2048,512]{2,1,0:T(8,128)(2,1)} %collective-permute-done, pred[]{:T(512)S(6)} %gt.6, bf16[2,2048,512]{2,1,0:T(8,128)(2,1)} %collective-permute-done.1, bf16[2,2048,512]{2,1,0:T(8,128)(2,1)} %collective-permute-done.2, pred[]{:T(512)S(6)} %eq.2), kind=kLoop, calls=%fused_computation.43 | loop fusion | flops 4194304 | bytes 20971522 | tf_op jit(solution)/shard_map/jit(_where)/select_n | solution.py:67
  129.3 2.3 broadcast_in_dim.44
  131.6 5.1 %constant_dynamic-update-slice_fusion.1 = (bf16[4096,512]{1,0:T(8,128)(2,1)}, bf16[2048,512]{1,0:T(8,128)(2,1)S(1)}) fusion(bf16[4096,512]{1,0:T(8,128)(2,1)} %broadcast_in_dim.44, s32[]{:T(128)S(6)} %select_n.104, f32[]{:T(128)} %bitcast.7, f32[4096,512]{1,0:T(8,128)S(1)} %bitcast.41, bf16[2,2048,512]{2,1,0:T(8,128)(2,1)} %get-tuple-element.27, ...), kind=kLoop, calls=%fused_computation.70 | loop fusion | flops 10485760 | bytes 16777732 | tf_op jit(solution)/shard_map/dynamic_update_slice | solution.py:109
  136.7 4.3 %select_convert_fusion.3 = (bf16[2048,512]{1,0:T(8,128)(2,1)}, f32[2048,512]{1,0:T(8,128)S(1)}) fusion(pred[]{:T(512)S(6)} %gt.6, f32[]{:T(128)} %bitcast.7, f32[4096,512]{1,0:T(8,128)S(1)} %bitcast.41, s32[]{:T(128)S(6)} %select_n.104, bf16[2048,512]{1,0:T(8,128)(2,1)S(1)} %get-tuple-element.24, bf16[2,2048,512]{2,1,0:T(8,128)(2,1)} %get-tuple-element.28, ...), kind=kLoop, calls=%fused_computation.39 | loop fusion | flops 9437184 | bytes 20973572 | tf_op jit(solution)/shard_map/convert_element_type | solution.py:61
  141.0 2.7 %select_convert_fusion.2 = bf16[2048,512]{1,0:T(8,128)(2,1)} fusion(f32[2048,512]{1,0:T(8,128)S(1)} %get-tuple-element.26, pred[]{:T(512)S(6)} %gt.6, f32[]{:T(128)} %bitcast.7, f32[4096,512]{1,0:T(8,128)S(1)} %bitcast.41, s32[]{:T(128)S(6)} %select_n.104, bf16[2048,512]{1,0:T(8,128)(2,1)S(1)} %get-tuple-element.24), kind=kLoop, calls=%fused_computation.38 | loop fusion | flops 6291456 | bytes 12582921 | tf_op jit(solution)/shard_map/convert_element_type | solution.py:60
  143.7 1.5 collective-permute-start.8
  145.2 1.5 collective-permute-start.6
  146.7 8.4 %constant_dynamic-update-slice_fusion = (bf16[4096,512]{1,0:T(8,128)(2,1)}, bf16[2048,512]{1,0:T(8,128)(2,1)}) fusion(bf16[4096,512]{1,0:T(8,128)(2,1)} %get-tuple-element.23, s32[]{:T(128)S(6)} %mul.159, f32[]{:T(128)} %bitcast.7, f32[4096,512]{1,0:T(8,128)} %get-tuple-element.16, bf16[2,2048,512]{2,1,0:T(8,128)(2,1)} %get-tuple-element.27, ...), kind=kLoop, calls=%fused_computation.69 | loop fusion | flops 10485760 | bytes 16777732 | tf_op jit(solution)/shard_map/dynamic_update_slice | solution.py:110
  155.1 5.4 %subtract_convert_fusion = bf16[4096,512]{1,0:T(8,128)(2,1)} fusion(bf16[4096,512]{1,0:T(8,128)(2,1)} %get-tuple-element.20, bf16[1,4096,512]{2,1,0:T(8,128)(2,1)S(1)} %copy-done.3), kind=kLoop, calls=%fused_computation.11 | loop fusion | flops 8388608 | bytes 12582912 | tf_op jit(solution)/shard_map/convert_element_type | solution.py:111
  160.5 29.6 %collective-permute-done.8 = bf16[2048,512]{1,0:T(8,128)(2,1)} collective-permute-done((bf16[2048,512]{1,0:T(8,128)(2,1)}, bf16[2048,512]{1,0:T(8,128)(2,1)}, u32[]{:S(2)}, u32[]{:S(2)}) %collective-permute-start.8) | collective-permute-done | bytes 2097184 | tf_op jit(solution)/shard_map/ppermute | solution.py:18
  191.4 3.8 %broadcast_select_fusion.3 = bf16[2048,512]{1,0:T(8,128)(2,1)} fusion(bf16[2048,512]{1,0:T(8,128)(2,1)} %collective-permute-done.8, pred[]{:T(512)S(6)} %gt.6, bf16[2048,512]{1,0:T(8,128)(2,1)} %collective-permute-done.6, bf16[2048,512]{1,0:T(8,128)(2,1)} %collective-permute-done.7, pred[]{:T(512)S(6)} %eq.2), kind=kLoop, calls=%fused_computation.52 | loop fusion | flops 2097152 | bytes 8388610 | tf_op jit(solution)/shard_map/jit(_where)/select_n | solution.py:67
  195.2 1.3 dynamic-slice_convert_fusion
  196.6 3.2 %fusion.2 = f32[512]{0:T(512)S(1)} fusion(bf16[512,4096]{1,0:T(8,128)(2,1)} %bitcast.53), kind=kLoop, calls=%fused_computation.8 | loop fusion | flops 6290944 | bytes 4196352 | tf_op jit(solution)/shard_map/reduce_sum | solution.py:23
  199.7 6.4 %fusion.68 = bf16[2048,512]{1,0:T(8,128)(2,1)} fusion(f32[2048,512]{1,0:T(8,128)S(1)} %copy-done.1, bf16[2048,512]{1,0:T(8,128)(2,1)} %broadcast_select_fusion.3, f32[4096,512]{1,0:T(8,128)} %get-tuple-element.16, s32[]{:T(128)S(6)} %mul.159, f32[]{:T(128)S(6)} %mul.183, bf16[2048,512]{1,0:T(8,128)(2,1)} %get-tuple-element.22), kind=kLoop, calls=%fused_computation.82 | loop fusion | flops 9437184 | bytes 14680072 | tf_op jit(solution)/shard_map/convert_element_type | solution.py:60
  206.6 1.5 collective-permute-start.13
  209.2 14.5 %multiply_reduce_fusion = (f32[]{:T(128)}, f32[4096,512]{1,0:T(8,128)}) fusion(bf16[4096,512]{1,0:T(8,128)(2,1)} %get-tuple-element.20, bf16[512,4096]{1,0:T(8,128)(2,1)} %bitcast.54, f32[512]{0:T(512)S(1)} %add_rsqrt_fusion, f32[511,512]{1,0:T(8,128)} %slice.52, pred[512]{0:T(512)(128)(4,1)S(1)} %iota_compare_fusion, s32[]{:T(128)S(6)} %select_n.111), kind=kOutput, calls=%fused_computation.10 | convolution fusion | flops 4315414528 | bytes 22549000 | tf_op jit(solution)/shard_map/dot_general | solution.py:45
  224.6 1.3 collective-permute-start.11
  225.8 3.1 %collective-permute-done.10 = f32[8,128]{1,0:T(8,128)S(1)} collective-permute-done((f32[8,128]{1,0:T(8,128)S(1)}, f32[8,128]{1,0:T(8,128)S(1)}, u32[]{:S(2)}, u32[]{:S(2)}) %collective-permute-start.10) | collective-permute-done | bytes 4128 | tf_op jit(solution)/shard_map/ppermute | solution.py:31
  228.9 7.2 %dynamic_update_slice.17 = bf16[2,1,4096,512]{3,2,1,0:T(8,128)(2,1)} pad(bf16[1,1,4096,512]{3,2,1,0:T(8,128)(2,1)} %bitcast.51, bf16[]{:T(256)} %constant.61.clone.1), padding=0_1x0_0x0_0x0_0 | pad | bytes 12582914 | tf_op jit(solution)/shard_map/dynamic_update_slice | solution.py:125
  238.3 7.2 %fusion.18 = bf16[2,1,4096,512]{3,2,1,0:T(8,128)(2,1)} fusion(bf16[2,1,4096,512]{3,2,1,0:T(8,128)(2,1)} %dynamic_update_slice.17, s32[]{:T(128)S(6)} %mul.159, bf16[2048,512]{1,0:T(8,128)(2,1)S(1)} %copy-done.4, f32[4096,512]{1,0:T(8,128)} %get-tuple-element.41, f32[]{:T(128)} %bitcast.11, bf16[2048,512]{1,0:T(8,128)(2,1)} %collective-permute-done.8, ...), kind=kLoop, calls=%fused_computation.45 | loop fusion | flops 19922944 | bytes 25166346 | tf_op jit(solution)/shard_map/dynamic_update_slice | solution.py:132
  245.5 5.8 %collective-permute-done.12 = bf16[2048,512]{1,0:T(8,128)(2,1)} collective-permute-done((bf16[2048,512]{1,0:T(8,128)(2,1)}, bf16[2048,512]{1,0:T(8,128)(2,1)}, u32[]{:S(2)}, u32[]{:S(2)}) %collective-permute-start.12) | collective-permute-done | bytes 2097184 | tf_op jit(solution)/shard_map/ppermute | solution.py:18
  251.7 4.5 %bitcast_dynamic-update-slice_fusion = bf16[2,1,4096,512]{3,2,1,0:T(8,128)(2,1)} fusion(bf16[2,1,4096,512]{3,2,1,0:T(8,128)(2,1)} %fusion.18, s32[]{:T(128)S(6)} %select_n.104, f32[4096,512]{1,0:T(8,128)S(1)} %copy-done.5, bf16[2048,512]{1,0:T(8,128)(2,1)} %collective-permute-done.12, f32[4096,512]{1,0:T(8,128)S(1)} %bitcast.43, ...), kind=kLoop, calls=%fused_computation.50 | loop fusion | flops 15728640 | bytes 18874890 | tf_op jit(solution)/shard_map/dynamic_update_slice | solution.py:132
  (66 shorter events, 10.0 us)
Async XLA Ops:
  6.5 3.2 %copy-start.6 = (s32[2]{0:T(128)S(1)}, s32[2]{0:T(128)}, u32[]{:S(2)}) copy-start(s32[2]{0:T(128)} %param.7) | copy-start | bytes 28
  6.5 86.7 %all-gather.5.cloned.1.call-start = ((), (), s32[]{:S(2)}) async-start(), calls=%async_computation | async-start | bytes 5242880 | tf_op jit(solution)/shard_map/all_gather | solution.py:83
  9.6 185.6 %all-gather.7.cloned.1.call-start = ((), (), s32[]{:S(2)}) async-start(), calls=%async_computation.1 | async-start | bytes 5242880 | tf_op jit(solution)/shard_map/all_gather | solution.py:84
  23.7 93.9 %collective-permute-start = (bf16[2,2048,512]{2,1,0:T(8,128)(2,1)}, bf16[2,2048,512]{2,1,0:T(8,128)(2,1)}, u32[]{:S(2)}, u32[]{:S(2)}) collective-permute-start(bf16[2,2048,512]{2,1,0:T(8,128)(2,1)} %get-tuple-element.33), channel_id=1, source_target_pairs={{0,16},{4,20},{8,24},{12,28},{16,0},{20,4},{24,8},{28,12},{1,17},{... | collective-permute-start | bytes 12582920 | tf_op jit(solution)/shard_map/ppermute | solution.py:18
  26.8 94.7 %collective-permute-start.1 = (bf16[2,2048,512]{2,1,0:T(8,128)(2,1)}, bf16[2,2048,512]{2,1,0:T(8,128)(2,1)}, u32[]{:S(2)}, u32[]{:S(2)}) collective-permute-start(bf16[2,2048,512]{2,1,0:T(8,128)(2,1)} %get-tuple-element.32), channel_id=1, source_target_pairs={{0,8},{4,12},{8,0},{12,4},{16,24},{20,28},{24,16},{28,20},{1,9},{5... | collective-permute-start | bytes 12582920 | tf_op jit(solution)/shard_map/ppermute | solution.py:18
  28.3 93.2 %collective-permute-start.2 = (bf16[2,2048,512]{2,1,0:T(8,128)(2,1)}, bf16[2,2048,512]{2,1,0:T(8,128)(2,1)}, u32[]{:S(2)}, u32[]{:S(2)}) collective-permute-start(bf16[2,2048,512]{2,1,0:T(8,128)(2,1)} %get-tuple-element.32), channel_id=1, source_target_pairs={{0,4},{4,0},{8,12},{12,8},{16,20},{20,16},{24,28},{28,24},{1,5},{5... | collective-permute-start | bytes 12582920 | tf_op jit(solution)/shard_map/ppermute | solution.py:18
  112.3 19.3 %slice-start = ((s8[8388608]{0:T(1024)(128)(4,1)}), s8[4194304]{0:T(1024)(128)(4,1)S(1)}, s32[]{:S(2)}) async-start(s8[8388608]{0:T(1024)(128)(4,1)} %bitcast.40), calls=%async_computation.2 | async-start | bytes 8388608
  112.3 19.3 %slice-start.4 = ((s8[8388608]{0:T(1024)(128)(4,1)}), s8[4194304]{0:T(1024)(128)(4,1)S(1)}, s32[]{:S(2)}) async-start(s8[8388608]{0:T(1024)(128)(4,1)} %bitcast.45), calls=%async_computation.6 | async-start | bytes 8388608
  113.0 18.5 %slice-start.1 = ((s8[8388608]{0:T(1024)(128)(4,1)}), s8[4194304]{0:T(1024)(128)(4,1)S(1)}, s32[]{:S(2)}) async-start(s8[8388608]{0:T(1024)(128)(4,1)} %bitcast.40), calls=%async_computation.3 | async-start | bytes 8388608
  113.1 18.5 %slice-start.5 = ((s8[8388608]{0:T(1024)(128)(4,1)}), s8[4194304]{0:T(1024)(128)(4,1)S(1)}, s32[]{:S(2)}) async-start(s8[8388608]{0:T(1024)(128)(4,1)} %bitcast.45), calls=%async_computation.7 | async-start | bytes 8388608
  113.1 14.3 %collective-permute-start.3 = (f32[8,128]{1,0:T(8,128)S(1)}, f32[8,128]{1,0:T(8,128)S(1)}, u32[]{:S(2)}, u32[]{:S(2)}) collective-permute-start(f32[8,128]{1,0:T(8,128)S(1)} %broadcast_in_dim.43), channel_id=1, source_target_pairs={{0,1},{1,2},{2,3},{3,0},{4,5},{5,6},{6,7},{7,4},{8,9},{9,10},{10,1... | collective-permute-start | bytes 12296 | tf_op jit(solution)/shard_map/ppermute | solution.py:31
  113.1 14.3 %collective-permute-start.4 = (f32[8,128]{1,0:T(8,128)S(1)}, f32[8,128]{1,0:T(8,128)S(1)}, u32[]{:S(2)}, u32[]{:S(2)}) collective-permute-start(f32[8,128]{1,0:T(8,128)S(1)} %broadcast_in_dim.43), channel_id=1, source_target_pairs={{0,2},{1,3},{2,0},{3,1},{4,6},{5,7},{6,4},{7,5},{8,10},{9,11},{10,... | collective-permute-start | bytes 12296 | tf_op jit(solution)/shard_map/ppermute | solution.py:31
  117.6 9.8 %collective-permute-start.5 = (f32[8,128]{1,0:T(8,128)S(1)}, f32[8,128]{1,0:T(8,128)S(1)}, u32[]{:S(2)}, u32[]{:S(2)}) collective-permute-start(f32[8,128]{1,0:T(8,128)S(1)} %broadcast_in_dim.43), channel_id=1, source_target_pairs={{0,3},{1,0},{2,1},{3,2},{4,7},{5,4},{6,5},{7,6},{8,11},{9,8},{10,9... | collective-permute-start | bytes 12296 | tf_op jit(solution)/shard_map/ppermute | solution.py:31
  141.0 2.7 %copy-start = (f32[2048,512]{1,0:T(8,128)}, f32[2048,512]{1,0:T(8,128)S(1)}, u32[]{:S(2)}) copy-start(f32[2048,512]{1,0:T(8,128)S(1)} %get-tuple-element.26) | copy-start | bytes 12582916
  143.7 46.4 %collective-permute-start.8 = (bf16[2048,512]{1,0:T(8,128)(2,1)}, bf16[2048,512]{1,0:T(8,128)(2,1)}, u32[]{:S(2)}, u32[]{:S(2)}) collective-permute-start(bf16[2048,512]{1,0:T(8,128)(2,1)} %select_convert_fusion.2), channel_id=1, source_target_pairs={{0,16},{4,20},{8,24},{12,28},{16,0},{20,4},{24,8},{28,12},{1,17},{... | collective-permute-start | bytes 6291464 | tf_op jit(solution)/shard_map/ppermute | solution.py:18
  145.2 46.1 %collective-permute-start.6 = (bf16[2048,512]{1,0:T(8,128)(2,1)}, bf16[2048,512]{1,0:T(8,128)(2,1)}, u32[]{:S(2)}, u32[]{:S(2)}) collective-permute-start(bf16[2048,512]{1,0:T(8,128)(2,1)} %get-tuple-element.25), channel_id=1, source_target_pairs={{0,8},{4,12},{8,0},{12,4},{16,24},{20,28},{24,16},{28,20},{1,9},{5... | collective-permute-start | bytes 6291464 | tf_op jit(solution)/shard_map/ppermute | solution.py:18
  146.7 44.7 %collective-permute-start.7 = (bf16[2048,512]{1,0:T(8,128)(2,1)}, bf16[2048,512]{1,0:T(8,128)(2,1)}, u32[]{:S(2)}, u32[]{:S(2)}) collective-permute-start(bf16[2048,512]{1,0:T(8,128)(2,1)} %get-tuple-element.25), channel_id=1, source_target_pairs={{0,4},{4,0},{8,12},{12,8},{16,20},{20,16},{24,28},{28,24},{1,5},{5... | collective-permute-start | bytes 6291464 | tf_op jit(solution)/shard_map/ppermute | solution.py:18
  146.7 8.4 %copy-start.3 = (bf16[1,4096,512]{2,1,0:T(8,128)(2,1)S(1)}, bf16[1,4096,512]{2,1,0:T(8,128)(2,1)}, u32[]{:S(2)}) copy-start(bf16[1,4096,512]{2,1,0:T(8,128)(2,1)} %param.4) | copy-start | bytes 12582916
  195.2 4.5 %copy-start.1 = (f32[2048,512]{1,0:T(8,128)S(1)}, f32[2048,512]{1,0:T(8,128)}, u32[]{:S(2)}) copy-start(f32[2048,512]{1,0:T(8,128)} %copy-done) | copy-start | bytes 12582916
  206.1 45.2 %collective-permute-start.12 = (bf16[2048,512]{1,0:T(8,128)(2,1)}, bf16[2048,512]{1,0:T(8,128)(2,1)}, u32[]{:S(2)}, u32[]{:S(2)}) collective-permute-start(bf16[2048,512]{1,0:T(8,128)(2,1)} %fusion.68), channel_id=1, source_target_pairs={{0,16},{4,20},{8,24},{12,28},{16,0},{20,4},{24,8},{28,12},{1,17},{... | collective-permute-start | bytes 6291464 | tf_op jit(solution)/shard_map/ppermute | solution.py:18
  206.6 45.0 %collective-permute-start.13 = (bf16[2048,512]{1,0:T(8,128)(2,1)}, bf16[2048,512]{1,0:T(8,128)(2,1)}, u32[]{:S(2)}, u32[]{:S(2)}) collective-permute-start(bf16[2048,512]{1,0:T(8,128)(2,1)} %fusion.68), channel_id=1, source_target_pairs={{0,8},{4,12},{8,0},{12,4},{16,24},{20,28},{24,16},{28,20},{1,9},{5... | collective-permute-start | bytes 6291464 | tf_op jit(solution)/shard_map/ppermute | solution.py:18
  208.1 43.5 %collective-permute-start.14 = (bf16[2048,512]{1,0:T(8,128)(2,1)}, bf16[2048,512]{1,0:T(8,128)(2,1)}, u32[]{:S(2)}, u32[]{:S(2)}) collective-permute-start(bf16[2048,512]{1,0:T(8,128)(2,1)} %fusion.68), channel_id=1, source_target_pairs={{0,4},{4,0},{8,12},{12,8},{16,20},{20,16},{24,28},{28,24},{1,5},{5... | collective-permute-start | bytes 6291464 | tf_op jit(solution)/shard_map/ppermute | solution.py:18
  224.4 4.6 %collective-permute-start.10 = (f32[8,128]{1,0:T(8,128)S(1)}, f32[8,128]{1,0:T(8,128)S(1)}, u32[]{:S(2)}, u32[]{:S(2)}) collective-permute-start(f32[8,128]{1,0:T(8,128)S(1)} %broadcast_in_dim.46), channel_id=1, source_target_pairs={{0,2},{1,3},{2,0},{3,1},{4,6},{5,7},{6,4},{7,5},{8,10},{9,11},{10,... | collective-permute-start | bytes 12296 | tf_op jit(solution)/shard_map/ppermute | solution.py:31
  224.6 11.5 %collective-permute-start.11 = (f32[8,128]{1,0:T(8,128)S(1)}, f32[8,128]{1,0:T(8,128)S(1)}, u32[]{:S(2)}, u32[]{:S(2)}) collective-permute-start(f32[8,128]{1,0:T(8,128)S(1)} %broadcast_in_dim.46), channel_id=1, source_target_pairs={{0,3},{1,0},{2,1},{3,2},{4,7},{5,4},{6,5},{7,6},{8,11},{9,8},{10,9... | collective-permute-start | bytes 12296 | tf_op jit(solution)/shard_map/ppermute | solution.py:31
  228.9 7.2 %collective-permute-start.9 = (f32[8,128]{1,0:T(8,128)S(1)}, f32[8,128]{1,0:T(8,128)S(1)}, u32[]{:S(2)}, u32[]{:S(2)}) collective-permute-start(f32[8,128]{1,0:T(8,128)S(1)} %broadcast_in_dim.46), channel_id=1, source_target_pairs={{0,1},{1,2},{2,3},{3,0},{4,5},{5,6},{6,7},{7,4},{8,9},{9,10},{10,1... | collective-permute-start | bytes 12296 | tf_op jit(solution)/shard_map/ppermute | solution.py:31
  228.9 9.3 %copy-start.2 = (f32[2048,512]{1,0:T(8,128)S(1)}, f32[2048,512]{1,0:T(8,128)}, u32[]{:S(2)}) copy-start(f32[2048,512]{1,0:T(8,128)} %copy-done) | copy-start | bytes 12582916
  228.9 9.3 %copy-start.4 = (bf16[2048,512]{1,0:T(8,128)(2,1)S(1)}, bf16[2048,512]{1,0:T(8,128)(2,1)}, u32[]{:S(2)}) copy-start(bf16[2048,512]{1,0:T(8,128)(2,1)} %get-tuple-element.22) | copy-start | bytes 6291460
  228.9 22.7 %slice-start.2 = ((s8[8388608]{0:T(1024)(128)(4,1)}), s8[4194304]{0:T(1024)(128)(4,1)S(1)}, s32[]{:S(2)}) async-start(s8[8388608]{0:T(1024)(128)(4,1)} %bitcast.42), calls=%async_computation.4 | async-start | bytes 8388608
  238.3 13.4 %slice-start.3 = ((s8[8388608]{0:T(1024)(128)(4,1)}), s8[4194304]{0:T(1024)(128)(4,1)S(1)}, s32[]{:S(2)}) async-start(s8[8388608]{0:T(1024)(128)(4,1)} %bitcast.42), calls=%async_computation.5 | async-start | bytes 8388608
  238.3 13.4 %copy-start.5 = (f32[4096,512]{1,0:T(8,128)S(1)}, f32[4096,512]{1,0:T(8,128)}, u32[]{:S(2)}) copy-start(f32[4096,512]{1,0:T(8,128)} %get-tuple-element.41) | copy-start | bytes 25165828
Sparse Core Ops, SparseCore 0:
  9.8 83.4 all-gather.4
  94.8 79.6 all-gather.6

commit v5 on v4

--- a/solution.py
+++ b/solution.py
@@ -60,14 +60,18 @@
         to_top = jnp.where(top_last, second, first).astype(bf16)
         to_low = jnp.where(top_last, first, second).astype(bf16)
         from_top = swapped(to_top, top)
-        from_low = swapped(to_low, 0)
-        for bit in range(1, top):
-            from_low = jnp.where(smaller == 1 << bit, swapped(to_low, bit), from_low)
-        return (
-            jnp.where(top_last, from_low, from_top),
-            jnp.where(top_last, from_top, from_low),
-            (to_top, to_low),
-        )
+        from_lows = [swapped(to_low, bit) for bit in range(top)]
+
+        def answers(cut):
+            low = cut(from_lows[0])
+            for bit in range(1, top):
+                low = jnp.where(smaller == 1 << bit, cut(from_lows[bit]), low)
+            high = cut(from_top)
+            return jnp.where(top_last, low, high), jnp.where(top_last, high, low)
+
+        if first.ndim == 2:
+            return *answers(lambda array: array), (to_top, to_low)
+        return answers(lambda array: array[0]), answers(lambda array: array[1]), (to_top, to_low)
 
     def part(value, which):
         return lax.dynamic_slice_in_dim(value, which * half, half, 0)
@@ -84,11 +88,11 @@
     rows1 = lax.all_gather(states[1, 0], "fsdp", axis=0, tiled=True)
 
     mine_combined = combined(weight, moment, mine)
-    got_first, got_second, sent1 = exchanged(
+    got_halves0, got_halves1, sent1 = exchanged(
         jnp.stack([combined(weight, moment, other), mine_combined]),
         jnp.stack([part(moment, other), mine_combined]),
     )
-    got_other, got_mine, got_moment = got_first[0], got_first[1], got_second[0]
+    (got_other, got_moment), (got_mine, _) = got_halves0, got_halves1
     weight_c, moment_c, rows0 = after((weight, moment, rows0), sent1)
 
     gradient0, factor0 = gradient_of(rows0, weight)

time: 263 us -> 261 us (level)
    ppermute x9, waiting for transfers between devices: 41 us -> 32.2 us  [swapped(): return lax.ppermute(value, 'rep', pairs)]
    ppermute x6, waiting for transfers between devices: 3.1 us -> 10.3 us  [fsdp_sum(): lax.ppermute(tile, 'fsdp', [(s, (s + shift) % size) for s in range(size)])]
    select_n x2 -> x1, other arithmetic: 9.72 us -> 3.85 us  [answers(): return (jnp.where(top_last, low, high), jnp.where(top_last, high, low))]
    unnamed x26 -> x30, local copies, waits for them, and re-layouts: 0.05 us -> 4.95 us
  transfers between devices with their start and end apart: 17 -> 17, of which waited for: 7 -> 8; matrix products, arithmetic and copies ran while one was open for 39% -> 37% of each run, Pallas kernels for 0% -> 0%
where the time goes in v5:
time: 261 us; the launch traced here: 260 us
  waiting for transfers between devices  108 us (41%)
  other arithmetic  73.3 us (28%)
  matrix products  28.5 us (11%)
  local copies, waits for them, and re-layouts  18.5 us (7%)
  between operations  17.9 us (7%)
  starting transfers between devices  14.4 us (6%)
    all_gather x1, waiting for transfers between devices, local(): rows0 = lax.all_gather(states[0, 0], 'fsdp', axis=0, tiled=True)  65.4 us
    ppermute x9, waiting for transfers between devices, swapped(): return lax.ppermute(value, 'rep', pairs)  32.2 us
    dot_general x2, matrix products, gradient_of(): lax.dot_general(normed, residual, (((0,), (0,)), ((), ())), preferred_ele...  28.5 us
    dynamic_update_slice x2, other arithmetic, local(): lax.dynamic_update_slice(changes, change[None, None], (1, 0, which * half...  12.9 us
    ppermute x6, waiting for transfers between devices, fsdp_sum(): lax.ppermute(tile, 'fsdp', [(s, (s + shift) % size) for s in range(size)])  10.3 us
    ppermute x9, starting transfers between devices, swapped(): return lax.ppermute(value, 'rep', pairs)  9.49 us
    dynamic_update_slice x1, other arithmetic, local(): lax.dynamic_update_slice_in_dim(weight1, weight1_mine, mine * half, 0)  9.07 us
    convert_element_type x2, other arithmetic, exchanged(): to_top = jnp.where(top_last, second, first).astype(bf16)  9.06 us
  transfers between devices with their start and end apart: 17, of which 8 were waited for; matrix products, arithmetic and copies ran while one was open for 37% of the time, Pallas kernels for 0%

profile of v5, /device:TPU:0, one launch (start us, length us, event | category | flops | bytes accessed | tf_op | source)
XLA Modules:
  0.0 260.4 jit_solution(11631526119359094150)
XLA Ops:
  6.5 3.1 %fusion.71 = (bf16[1,1,128,4096]{3,2,1,0:T(8,128)(2,1)}, bf16[1,1,128,4096]{3,2,1,0:T(8,128)(2,1)}) fusion(bf16[2,1,128,4096]{3,2,1,0:T(8,128)(2,1)} %param.6), kind=kLoop, calls=%fused_computation.81 | loop fusion | bytes 4194304 | tf_op jit(solution)/shard_map/slice | solution.py:88
  12.0 7.6 %multiply_subtract_fusion = (bf16[1,2048,512]{2,1,0:T(8,128)(2,1)S(1)}, bf16[1,2048,512]{2,1,0:T(8,128)(2,1)S(1)}, bf16[1,2048,512]{2,1,0:T(8,128)(2,1)S(1)}) fusion(bf16[1,4096,512]{2,1,0:T(8,128)(2,1)} %param.4, s32[]{:T(128)S(6)} %select_n.117, f32[1,4096,512]{2,1,0:T(8,128)} %param.5, s32[]{:T(128)S(6)} %mul.159), kind=kLoop, calls=%fused_computation.40 | loop fusion | flops 10485760 | bytes 20971528 | tf_op jit(solution)/shard_map/sub | solution.py:83
  19.6 3.8 %select_convert_fusion = (bf16[2,2048,512]{2,1,0:T(8,128)(2,1)}, bf16[2,2048,512]{2,1,0:T(8,128)(2,1)}) fusion(bf16[1,2048,512]{2,1,0:T(8,128)(2,1)S(1)} %get-tuple-element.28, bf16[1,2048,512]{2,1,0:T(8,128)(2,1)S(1)} %get-tuple-element.29, bf16[1,2048,512]{2,1,0:T(8,128)(2,1)S(1)} %get-tuple-element.27, pred[]{:T(512)S(6)} %gt.6), kind=kLoop, calls=%fused_computation.13 | loop fusion | flops 8388608 | bytes 14680065 | tf_op jit(solution)/shard_map/convert_element_type | solution.py:61
  23.4 3.0 %collective-permute-start.1 = (bf16[2,2048,512]{2,1,0:T(8,128)(2,1)}, bf16[2,2048,512]{2,1,0:T(8,128)(2,1)}, u32[]{:S(2)}, u32[]{:S(2)}) collective-permute-start(bf16[2,2048,512]{2,1,0:T(8,128)(2,1)} %get-tuple-element.30), channel_id=1, source_target_pairs={{0,8},{4,12},{8,0},{12,4},{16,24},{20,28},{24,16},{28,20},{1,9},{5... | collective-permute-start | bytes 12582920 | tf_op jit(solution)/shard_map/ppermute | solution.py:18
  26.3 1.5 collective-permute-start
  27.9 65.4 %all-gather.5.cloned.1.call-done = bf16[1,1,512,4096]{3,2,1,0:T(8,128)(2,1)} async-done(((bf16[1,1,128,4096]{3,2,1,0:T(8,128)(2,1)}), bf16[1,1,512,4096]{3,2,1,0:T(8,128)(2,1)}) %all-gather.5.cloned.1.call-update) | async-done | bytes 4194320 | tf_op jit(solution)/shard_map/all_gather | solution.py:87
  94.6 3.1 %fusion = f32[512]{0:T(512)S(1)} fusion(bf16[512,4096]{1,0:T(8,128)(2,1)} %bitcast.52), kind=kLoop, calls=%fused_computation.6 | loop fusion | flops 6290944 | bytes 4196352 | tf_op jit(solution)/shard_map/reduce_sum | solution.py:23
  97.7 14.5 %multiply_reduce_fusion.1 = (f32[]{:T(128)}, f32[4096,512]{1,0:T(8,128)}) fusion(bf16[512,4096]{1,0:T(8,128)(2,1)} %bitcast.53, f32[512]{0:T(512)S(1)} %add_rsqrt_fusion.1, f32[511,512]{1,0:T(8,128)S(1)} %slice.62, pred[512]{0:T(512)(128)(4,1)S(1)} %iota_compare_fusion, s32[]{:T(128)S(6)} %select_n.125, bf16[1,4096,512]{2,1,0:T(8,128)(2,1)} %param.4), kind=kOutput, calls=%fused_computation.12 | convolution fusion | flops 4315414528 | bytes 22549000 | tf_op jit(solution)/shard_map/dot_general | solution.py:45
  113.3 4.9 %collective-permute-done.3 = f32[8,128]{1,0:T(8,128)S(1)} collective-permute-done((f32[8,128]{1,0:T(8,128)S(1)}, f32[8,128]{1,0:T(8,128)S(1)}, u32[]{:S(2)}, u32[]{:S(2)}) %collective-permute-start.3) | collective-permute-done | bytes 4128 | tf_op jit(solution)/shard_map/ppermute | solution.py:31
  119.4 4.1 %collective-permute-done.5 = f32[8,128]{1,0:T(8,128)S(1)} collective-permute-done((f32[8,128]{1,0:T(8,128)S(1)}, f32[8,128]{1,0:T(8,128)S(1)}, u32[]{:S(2)}, u32[]{:S(2)}) %collective-permute-start.5) | collective-permute-done | bytes 4128 | tf_op jit(solution)/shard_map/ppermute | solution.py:31
  125.7 6.6 %constant_dynamic-update-slice_fusion.1 = (bf16[4096,512]{1,0:T(8,128)(2,1)S(1)}, bf16[2048,512]{1,0:T(8,128)(2,1)S(1)}) fusion(bf16[4096,512]{1,0:T(8,128)(2,1)S(1)} %broadcast_in_dim.44, s32[]{:T(128)S(6)} %select_n.117, f32[]{:T(128)} %bitcast.7, f32[4096,512]{1,0:T(8,128)} %get-tuple-element.16, bf16[2,2048,512]{2,1,0:T(8,128)(2,1)} %collective-permute-done, ...), kind=kLoop, calls=%fused_computation.68 | loop fusion | flops 12582912 | bytes 20971530 | tf_op jit(solution)/shard_map/dynamic_update_slice | solution.py:113
  132.3 2.1 copy-done.6
  134.4 1.5 slice-done.1
  136.0 1.2 slice-done.5
  137.2 4.8 %select_convert_fusion.3 = (bf16[2048,512]{1,0:T(8,128)(2,1)}, f32[2048,512]{1,0:T(8,128)S(1)}) fusion(pred[]{:T(512)S(6)} %gt.6, f32[]{:T(128)} %bitcast.7, f32[4096,512]{1,0:T(8,128)S(1)} %bitcast.37, s32[]{:T(128)S(6)} %select_n.117, bf16[2048,512]{1,0:T(8,128)(2,1)S(1)} %get-tuple-element.24, bf16[2,2048,512]{2,1,0:T(8,128)(2,1)} %collective-permute-done.2, ...), kind=kLoop, calls=%fused_computation.39 | loop fusion | flops 10485760 | bytes 23071236 | tf_op jit(solution)/shard_map/convert_element_type | solution.py:61
  142.0 2.7 %select_convert_fusion.2 = bf16[2048,512]{1,0:T(8,128)(2,1)} fusion(f32[2048,512]{1,0:T(8,128)S(1)} %get-tuple-element.26, pred[]{:T(512)S(6)} %gt.6, f32[]{:T(128)} %bitcast.7, f32[4096,512]{1,0:T(8,128)S(1)} %bitcast.37, s32[]{:T(128)S(6)} %select_n.117, bf16[2048,512]{1,0:T(8,128)(2,1)S(1)} %get-tuple-element.24), kind=kLoop, calls=%fused_computation.38 | loop fusion | flops 6291456 | bytes 12582921 | tf_op jit(solution)/shard_map/convert_element_type | solution.py:60
  144.7 1.5 collective-permute-start.8
  146.2 1.5 collective-permute-start.6
  147.7 9.1 %constant_dynamic-update-slice_fusion = (bf16[4096,512]{1,0:T(8,128)(2,1)}, bf16[2048,512]{1,0:T(8,128)(2,1)}) fusion(bf16[4096,512]{1,0:T(8,128)(2,1)} %copy-done.6, s32[]{:T(128)S(6)} %mul.159, f32[]{:T(128)} %bitcast.7, f32[4096,512]{1,0:T(8,128)} %get-tuple-element.16, bf16[2,2048,512]{2,1,0:T(8,128)(2,1)} %collective-permute-done, ...), kind=kLoop, calls=%fused_computation.67 | loop fusion | flops 12582912 | bytes 20972038 | tf_op jit(solution)/shard_map/dynamic_update_slice | solution.py:114
  156.8 5.5 %subtract_convert_fusion = bf16[4096,512]{1,0:T(8,128)(2,1)} fusion(bf16[4096,512]{1,0:T(8,128)(2,1)} %get-tuple-element.20, bf16[1,4096,512]{2,1,0:T(8,128)(2,1)S(1)} %copy-done.4), kind=kLoop, calls=%fused_computation.11 | loop fusion | flops 8388608 | bytes 12582912 | tf_op jit(solution)/shard_map/convert_element_type | solution.py:115
  162.3 27.1 %collective-permute-done.8 = bf16[2048,512]{1,0:T(8,128)(2,1)} collective-permute-done((bf16[2048,512]{1,0:T(8,128)(2,1)}, bf16[2048,512]{1,0:T(8,128)(2,1)}, u32[]{:S(2)}, u32[]{:S(2)}) %collective-permute-start.8) | collective-permute-done | bytes 2097184 | tf_op jit(solution)/shard_map/ppermute | solution.py:18
  190.5 3.8 %broadcast_select_fusion.1 = bf16[2048,512]{1,0:T(8,128)(2,1)} fusion(bf16[2048,512]{1,0:T(8,128)(2,1)} %collective-permute-done.8, pred[]{:T(512)S(6)} %gt.6, bf16[2048,512]{1,0:T(8,128)(2,1)} %collective-permute-done.6, bf16[2048,512]{1,0:T(8,128)(2,1)} %collective-permute-done.7, pred[]{:T(512)S(6)} %eq.2), kind=kLoop, calls=%fused_computation.50 | loop fusion | flops 2097152 | bytes 8388610 | tf_op jit(solution)/shard_map/jit(_where)/select_n | solution.py:70
  194.3 1.3 dynamic-slice_convert_fusion
  195.7 3.2 %fusion.2 = f32[512]{0:T(512)S(1)} fusion(bf16[512,4096]{1,0:T(8,128)(2,1)} %bitcast.49), kind=kLoop, calls=%fused_computation.8 | loop fusion | flops 6290944 | bytes 4196352 | tf_op jit(solution)/shard_map/reduce_sum | solution.py:23
  198.9 6.4 %fusion.68 = bf16[2048,512]{1,0:T(8,128)(2,1)} fusion(f32[2048,512]{1,0:T(8,128)S(1)} %copy-done.1, bf16[2048,512]{1,0:T(8,128)(2,1)} %broadcast_select_fusion.1, f32[4096,512]{1,0:T(8,128)} %get-tuple-element.16, s32[]{:T(128)S(6)} %mul.159, f32[]{:T(128)S(6)} %mul.183, bf16[2048,512]{1,0:T(8,128)(2,1)} %get-tuple-element.22), kind=kLoop, calls=%fused_computation.80 | loop fusion | flops 9437184 | bytes 14680072 | tf_op jit(solution)/shard_map/convert_element_type | solution.py:60
  205.8 1.4 collective-permute-start.13
  207.4 14.0 %multiply_reduce_fusion = (f32[]{:T(128)}, f32[4096,512]{1,0:T(8,128)}) fusion(bf16[4096,512]{1,0:T(8,128)(2,1)} %get-tuple-element.20, bf16[512,4096]{1,0:T(8,128)(2,1)} %bitcast.50, f32[512]{0:T(512)S(1)} %add_rsqrt_fusion, f32[511,512]{1,0:T(8,128)S(1)} %slice.66, pred[512]{0:T(512)(128)(4,1)S(1)} %iota_compare_fusion, s32[]{:T(128)S(6)} %select_n.125), kind=kOutput, calls=%fused_computation.10 | convolution fusion | flops 4315414528 | bytes 22549000 | tf_op jit(solution)/shard_map/dot_general | solution.py:45
  222.1 3.3 %collective-permute-start.11 = (f32[8,128]{1,0:T(8,128)S(1)}, f32[8,128]{1,0:T(8,128)S(1)}, u32[]{:S(2)}, u32[]{:S(2)}) collective-permute-start(f32[8,128]{1,0:T(8,128)S(1)} %broadcast_in_dim.46), channel_id=1, source_target_pairs={{0,3},{1,0},{2,1},{3,2},{4,7},{5,4},{6,5},{7,6},{8,11},{9,8},{10,9... | collective-permute-start | bytes 12296 | tf_op jit(solution)/shard_map/ppermute | solution.py:31
  227.5 7.2 %dynamic_update_slice.17 = bf16[2,1,4096,512]{3,2,1,0:T(8,128)(2,1)} pad(bf16[1,1,4096,512]{3,2,1,0:T(8,128)(2,1)} %bitcast.47, bf16[]{:T(256)} %constant.61.clone.1), padding=0_1x0_0x0_0x0_0 | pad | bytes 12582914 | tf_op jit(solution)/shard_map/dynamic_update_slice | solution.py:129
  236.7 8.3 %fusion.18 = bf16[2,1,4096,512]{3,2,1,0:T(8,128)(2,1)} fusion(bf16[2,1,4096,512]{3,2,1,0:T(8,128)(2,1)} %dynamic_update_slice.17, s32[]{:T(128)S(6)} %mul.159, bf16[2048,512]{1,0:T(8,128)(2,1)} %get-tuple-element.22, f32[4096,512]{1,0:T(8,128)} %get-tuple-element.39, f32[]{:T(128)} %bitcast.11, bf16[2048,512]{1,0:T(8,128)(2,1)} %collective-permute-done.8, ...), kind=kLoop, calls=%fused_computation.43 | loop fusion | flops 19922944 | bytes 25166346 | tf_op jit(solution)/shard_map/dynamic_update_slice | solution.py:136
  245.1 3.5 %collective-permute-done.12 = bf16[2048,512]{1,0:T(8,128)(2,1)} collective-permute-done((bf16[2048,512]{1,0:T(8,128)(2,1)}, bf16[2048,512]{1,0:T(8,128)(2,1)}, u32[]{:S(2)}, u32[]{:S(2)}) %collective-permute-start.12) | collective-permute-done | bytes 2097184 | tf_op jit(solution)/shard_map/ppermute | solution.py:18
  249.0 4.5 %bitcast_dynamic-update-slice_fusion = bf16[2,1,4096,512]{3,2,1,0:T(8,128)(2,1)} fusion(bf16[2,1,4096,512]{3,2,1,0:T(8,128)(2,1)} %fusion.18, s32[]{:T(128)S(6)} %select_n.117, f32[4096,512]{1,0:T(8,128)S(1)} %copy-done.7, bf16[2048,512]{1,0:T(8,128)(2,1)} %collective-permute-done.12, f32[4096,512]{1,0:T(8,128)S(1)} %bitcast.39, ...), kind=kLoop, calls=%fused_computation.48 | loop fusion | flops 15728640 | bytes 18874890 | tf_op jit(solution)/shard_map/dynamic_update_slice | solution.py:136
  (69 shorter events, 11.0 us)
Async XLA Ops:
  6.5 3.2 %copy-start.8 = (s32[2]{0:T(128)S(1)}, s32[2]{0:T(128)}, u32[]{:S(2)}) copy-start(s32[2]{0:T(128)} %param.7) | copy-start | bytes 28
  6.5 86.7 %all-gather.5.cloned.1.call-start = ((), (), s32[]{:S(2)}) async-start(), calls=%async_computation | async-start | bytes 5242880 | tf_op jit(solution)/shard_map/all_gather | solution.py:87
  9.7 184.7 %all-gather.7.cloned.1.call-start = ((), (), s32[]{:S(2)}) async-start(), calls=%async_computation.1 | async-start | bytes 5242880 | tf_op jit(solution)/shard_map/all_gather | solution.py:88
  23.4 101.9 %collective-permute-start.1 = (bf16[2,2048,512]{2,1,0:T(8,128)(2,1)}, bf16[2,2048,512]{2,1,0:T(8,128)(2,1)}, u32[]{:S(2)}, u32[]{:S(2)}) collective-permute-start(bf16[2,2048,512]{2,1,0:T(8,128)(2,1)} %get-tuple-element.30), channel_id=1, source_target_pairs={{0,8},{4,12},{8,0},{12,4},{16,24},{20,28},{24,16},{28,20},{1,9},{5... | collective-permute-start | bytes 12582920 | tf_op jit(solution)/shard_map/ppermute | solution.py:18
  26.3 99.0 %collective-permute-start.2 = (bf16[2,2048,512]{2,1,0:T(8,128)(2,1)}, bf16[2,2048,512]{2,1,0:T(8,128)(2,1)}, u32[]{:S(2)}, u32[]{:S(2)}) collective-permute-start(bf16[2,2048,512]{2,1,0:T(8,128)(2,1)} %get-tuple-element.30), channel_id=1, source_target_pairs={{0,4},{4,0},{8,12},{12,8},{16,20},{20,16},{24,28},{28,24},{1,5},{5... | collective-permute-start | bytes 12582920 | tf_op jit(solution)/shard_map/ppermute | solution.py:18
  26.3 99.0 %collective-permute-start = (bf16[2,2048,512]{2,1,0:T(8,128)(2,1)}, bf16[2,2048,512]{2,1,0:T(8,128)(2,1)}, u32[]{:S(2)}, u32[]{:S(2)}) collective-permute-start(bf16[2,2048,512]{2,1,0:T(8,128)(2,1)} %get-tuple-element.31), channel_id=1, source_target_pairs={{0,16},{4,20},{8,24},{12,28},{16,0},{20,4},{24,8},{28,12},{1,17},{... | collective-permute-start | bytes 12582920 | tf_op jit(solution)/shard_map/ppermute | solution.py:18
  112.8 5.5 %collective-permute-start.3 = (f32[8,128]{1,0:T(8,128)S(1)}, f32[8,128]{1,0:T(8,128)S(1)}, u32[]{:S(2)}, u32[]{:S(2)}) collective-permute-start(f32[8,128]{1,0:T(8,128)S(1)} %broadcast_in_dim.43), channel_id=1, source_target_pairs={{0,1},{1,2},{2,3},{3,0},{4,5},{5,6},{6,7},{7,4},{8,9},{9,10},{10,1... | collective-permute-start | bytes 12296 | tf_op jit(solution)/shard_map/ppermute | solution.py:31
  112.8 6.6 %collective-permute-start.4 = (f32[8,128]{1,0:T(8,128)S(1)}, f32[8,128]{1,0:T(8,128)S(1)}, u32[]{:S(2)}, u32[]{:S(2)}) collective-permute-start(f32[8,128]{1,0:T(8,128)S(1)} %broadcast_in_dim.43), channel_id=1, source_target_pairs={{0,2},{1,3},{2,0},{3,1},{4,6},{5,7},{6,4},{7,5},{8,10},{9,11},{10,... | collective-permute-start | bytes 12296 | tf_op jit(solution)/shard_map/ppermute | solution.py:31
  118.3 5.2 %collective-permute-start.5 = (f32[8,128]{1,0:T(8,128)S(1)}, f32[8,128]{1,0:T(8,128)S(1)}, u32[]{:S(2)}, u32[]{:S(2)}) collective-permute-start(f32[8,128]{1,0:T(8,128)S(1)} %broadcast_in_dim.43), channel_id=1, source_target_pairs={{0,3},{1,0},{2,1},{3,2},{4,7},{5,4},{6,5},{7,6},{8,11},{9,8},{10,9... | collective-permute-start | bytes 12296 | tf_op jit(solution)/shard_map/ppermute | solution.py:31
  119.4 6.2 %copy-start.3 = (bf16[1,4096,512]{2,1,0:T(8,128)(2,1)S(1)}, bf16[1,4096,512]{2,1,0:T(8,128)(2,1)}, u32[]{:S(2)}) copy-start(bf16[1,4096,512]{2,1,0:T(8,128)(2,1)} %param.4) | copy-start | bytes 12582916
  125.3 9.1 %slice-start = ((s8[8388608]{0:T(1024)(128)(4,1)}), s8[4194304]{0:T(1024)(128)(4,1)S(1)}, s32[]{:S(2)}) async-start(s8[8388608]{0:T(1024)(128)(4,1)} %bitcast.36), calls=%async_computation.2 | async-start | bytes 8388608
  125.3 9.1 %slice-start.4 = ((s8[8388608]{0:T(1024)(128)(4,1)}), s8[4194304]{0:T(1024)(128)(4,1)S(1)}, s32[]{:S(2)}) async-start(s8[8388608]{0:T(1024)(128)(4,1)} %bitcast.42), calls=%async_computation.6 | async-start | bytes 8388608
  125.6 10.3 %slice-start.1 = ((s8[8388608]{0:T(1024)(128)(4,1)}), s8[4194304]{0:T(1024)(128)(4,1)S(1)}, s32[]{:S(2)}) async-start(s8[8388608]{0:T(1024)(128)(4,1)} %bitcast.36), calls=%async_computation.3 | async-start | bytes 8388608
  125.6 11.5 %slice-start.5 = ((s8[8388608]{0:T(1024)(128)(4,1)}), s8[4194304]{0:T(1024)(128)(4,1)S(1)}, s32[]{:S(2)}) async-start(s8[8388608]{0:T(1024)(128)(4,1)} %bitcast.42), calls=%async_computation.7 | async-start | bytes 8388608
  132.3 2.1 copy-start.6
  142.0 2.7 %copy-start = (f32[2048,512]{1,0:T(8,128)}, f32[2048,512]{1,0:T(8,128)S(1)}, u32[]{:S(2)}) copy-start(f32[2048,512]{1,0:T(8,128)S(1)} %get-tuple-element.26) | copy-start | bytes 12582916
  144.7 44.6 %collective-permute-start.8 = (bf16[2048,512]{1,0:T(8,128)(2,1)}, bf16[2048,512]{1,0:T(8,128)(2,1)}, u32[]{:S(2)}, u32[]{:S(2)}) collective-permute-start(bf16[2048,512]{1,0:T(8,128)(2,1)} %select_convert_fusion.2), channel_id=1, source_target_pairs={{0,16},{4,20},{8,24},{12,28},{16,0},{20,4},{24,8},{28,12},{1,17},{... | collective-permute-start | bytes 6291464 | tf_op jit(solution)/shard_map/ppermute | solution.py:18
  146.2 44.3 %collective-permute-start.6 = (bf16[2048,512]{1,0:T(8,128)(2,1)}, bf16[2048,512]{1,0:T(8,128)(2,1)}, u32[]{:S(2)}, u32[]{:S(2)}) collective-permute-start(bf16[2048,512]{1,0:T(8,128)(2,1)} %get-tuple-element.25), channel_id=1, source_target_pairs={{0,8},{4,12},{8,0},{12,4},{16,24},{20,28},{24,16},{28,20},{1,9},{5... | collective-permute-start | bytes 6291464 | tf_op jit(solution)/shard_map/ppermute | solution.py:18
  147.7 42.8 %collective-permute-start.7 = (bf16[2048,512]{1,0:T(8,128)(2,1)}, bf16[2048,512]{1,0:T(8,128)(2,1)}, u32[]{:S(2)}, u32[]{:S(2)}) collective-permute-start(bf16[2048,512]{1,0:T(8,128)(2,1)} %get-tuple-element.25), channel_id=1, source_target_pairs={{0,4},{4,0},{8,12},{12,8},{16,20},{20,16},{24,28},{28,24},{1,5},{5... | collective-permute-start | bytes 6291464 | tf_op jit(solution)/shard_map/ppermute | solution.py:18
  147.7 9.1 %copy-start.4 = (bf16[1,4096,512]{2,1,0:T(8,128)(2,1)S(1)}, bf16[1,4096,512]{2,1,0:T(8,128)(2,1)}, u32[]{:S(2)}) copy-start(bf16[1,4096,512]{2,1,0:T(8,128)(2,1)} %param.4) | copy-start | bytes 12582916
  194.3 4.5 %copy-start.1 = (f32[2048,512]{1,0:T(8,128)S(1)}, f32[2048,512]{1,0:T(8,128)}, u32[]{:S(2)}) copy-start(f32[2048,512]{1,0:T(8,128)} %copy-done) | copy-start | bytes 12582916
  205.2 43.4 %collective-permute-start.12 = (bf16[2048,512]{1,0:T(8,128)(2,1)}, bf16[2048,512]{1,0:T(8,128)(2,1)}, u32[]{:S(2)}, u32[]{:S(2)}) collective-permute-start(bf16[2048,512]{1,0:T(8,128)(2,1)} %fusion.68), channel_id=1, source_target_pairs={{0,16},{4,20},{8,24},{12,28},{16,0},{20,4},{24,8},{28,12},{1,17},{... | collective-permute-start | bytes 6291464 | tf_op jit(solution)/shard_map/ppermute | solution.py:18
  205.8 43.2 %collective-permute-start.13 = (bf16[2048,512]{1,0:T(8,128)(2,1)}, bf16[2048,512]{1,0:T(8,128)(2,1)}, u32[]{:S(2)}, u32[]{:S(2)}) collective-permute-start(bf16[2048,512]{1,0:T(8,128)(2,1)} %fusion.68), channel_id=1, source_target_pairs={{0,8},{4,12},{8,0},{12,4},{16,24},{20,28},{24,16},{28,20},{1,9},{5... | collective-permute-start | bytes 6291464 | tf_op jit(solution)/shard_map/ppermute | solution.py:18
  207.3 41.8 %collective-permute-start.14 = (bf16[2048,512]{1,0:T(8,128)(2,1)}, bf16[2048,512]{1,0:T(8,128)(2,1)}, u32[]{:S(2)}, u32[]{:S(2)}) collective-permute-start(bf16[2048,512]{1,0:T(8,128)(2,1)} %fusion.68), channel_id=1, source_target_pairs={{0,4},{4,0},{8,12},{12,8},{16,20},{20,16},{24,28},{28,24},{1,5},{5... | collective-permute-start | bytes 6291464 | tf_op jit(solution)/shard_map/ppermute | solution.py:18
  222.0 4.6 %collective-permute-start.10 = (f32[8,128]{1,0:T(8,128)S(1)}, f32[8,128]{1,0:T(8,128)S(1)}, u32[]{:S(2)}, u32[]{:S(2)}) collective-permute-start(f32[8,128]{1,0:T(8,128)S(1)} %broadcast_in_dim.46), channel_id=1, source_target_pairs={{0,2},{1,3},{2,0},{3,1},{4,6},{5,7},{6,4},{7,5},{8,10},{9,11},{10,... | collective-permute-start | bytes 12296 | tf_op jit(solution)/shard_map/ppermute | solution.py:31
  222.1 12.6 %collective-permute-start.11 = (f32[8,128]{1,0:T(8,128)S(1)}, f32[8,128]{1,0:T(8,128)S(1)}, u32[]{:S(2)}, u32[]{:S(2)}) collective-permute-start(f32[8,128]{1,0:T(8,128)S(1)} %broadcast_in_dim.46), channel_id=1, source_target_pairs={{0,3},{1,0},{2,1},{3,2},{4,7},{5,4},{6,5},{7,6},{8,11},{9,8},{10,9... | collective-permute-start | bytes 12296 | tf_op jit(solution)/shard_map/ppermute | solution.py:31
  226.6 8.1 %collective-permute-start.9 = (f32[8,128]{1,0:T(8,128)S(1)}, f32[8,128]{1,0:T(8,128)S(1)}, u32[]{:S(2)}, u32[]{:S(2)}) collective-permute-start(f32[8,128]{1,0:T(8,128)S(1)} %broadcast_in_dim.46), channel_id=1, source_target_pairs={{0,1},{1,2},{2,3},{3,0},{4,5},{5,6},{6,7},{7,4},{8,9},{9,10},{10,1... | collective-permute-start | bytes 12296 | tf_op jit(solution)/shard_map/ppermute | solution.py:31
  227.5 9.2 %copy-start.2 = (f32[2048,512]{1,0:T(8,128)S(1)}, f32[2048,512]{1,0:T(8,128)}, u32[]{:S(2)}) copy-start(f32[2048,512]{1,0:T(8,128)} %copy-done) | copy-start | bytes 12582916
  227.5 9.2 %copy-start.5 = (bf16[2048,512]{1,0:T(8,128)(2,1)S(1)}, bf16[2048,512]{1,0:T(8,128)(2,1)}, u32[]{:S(2)}) copy-start(bf16[2048,512]{1,0:T(8,128)(2,1)} %broadcast_select_fusion.1) | copy-start | bytes 6291460
  227.5 21.5 %slice-start.2 = ((s8[8388608]{0:T(1024)(128)(4,1)}), s8[4194304]{0:T(1024)(128)(4,1)S(1)}, s32[]{:S(2)}) async-start(s8[8388608]{0:T(1024)(128)(4,1)} %bitcast.38), calls=%async_computation.4 | async-start | bytes 8388608
  236.7 12.3 %slice-start.3 = ((s8[8388608]{0:T(1024)(128)(4,1)}), s8[4194304]{0:T(1024)(128)(4,1)S(1)}, s32[]{:S(2)}) async-start(s8[8388608]{0:T(1024)(128)(4,1)} %bitcast.38), calls=%async_computation.5 | async-start | bytes 8388608
  236.7 12.3 %copy-start.7 = (f32[4096,512]{1,0:T(8,128)S(1)}, f32[4096,512]{1,0:T(8,128)}, u32[]{:S(2)}) copy-start(f32[4096,512]{1,0:T(8,128)} %get-tuple-element.39) | copy-start | bytes 25165828
Sparse Core Ops, SparseCore 0:
  9.8 83.4 all-gather.4
  94.9 79.5 all-gather.6
